TPU v7x, 128 devices: a whole 4x4x4 slice. The times are simulated.
128 devices in a mesh: docs: 32 (over z, y, core), split: 4 (over x).
Axes of the slice: x: 4, y: 4, z: 4, core: 2. Of those that a mesh axis runs over, the one named last changes fastest.
Arguments:
- embeddings: float32 [131072, 768], P(('docs', 'split'))
- cluster_id: int32 [131072], P(('docs', 'split')), may hold values from 0 to 127, as said below
Outputs:
- best_similarity: float32 [131072], P(('docs', 'split'))
Inputs may be any that keep to these rules, and one draw needn't show every extreme that they name: `cluster_id`: documents are in blocks of 1024 rows, one block a device in order. In every block at most 64 documents have ids in any one range k * 4 to (k + 1) * 4 - 1, and in every draw one such range holds exactly 64 documents of every block.
All inputs are finite; a program needn't handle non-finite values.
Results may differ from a plain program's by a relative error of at most 0.0003.
Values may be sent and summed in bfloat16 or wider, within the bound.
No kernel may reach another device: no remote copies, remote signals or barrier semaphores. Data moves between devices by JAX's collectives and lax.ppermute only.
A program may use at most 128 MiB of HBM per device.

v0:
```python
import math

import jax
import jax.numpy as jnp
from jax import lax
from jax.sharding import PartitionSpec as P

CLU_DEV = 4


epsilon = 1e-06


def unit_rows(rows):
    columns = rows.shape[1]
    scaling = lax.rsqrt(jnp.mean(rows * rows, axis=1, keepdims=True) + epsilon) * columns ** (-0.5)
    return (rows * scaling).astype(jnp.bfloat16)


def masked_scores(own_rows, own_ids, own_pos, right_rows, right_ids, right_pos):
    scores = lax.dot_general(
        own_rows, right_rows, (((1,), (1,)), ((), ())), preferred_element_type=jnp.float32
    )
    allowed = (
        (own_ids[:, None] == right_ids[None, :])
        & (own_pos[:, None] != right_pos[None, :])
        & (own_ids[:, None] >= 0)
    )
    return jnp.where(allowed, scores, jnp.float32(-1.0))


def per_device(embeddings, cluster_id):
    docs_here = embeddings.shape[0]
    columns = embeddings.shape[1]
    owners = lax.axis_size("docs")
    capacity = 2 * docs_here // owners
    slots_all = owners * capacity
    target = cluster_id // CLU_DEV
    onehot = (target[:, None] == jnp.arange(owners, dtype=jnp.int32)[None, :]).astype(jnp.bfloat16)
    earlier = (jnp.arange(docs_here)[:, None] > jnp.arange(docs_here)[None, :]).astype(jnp.bfloat16)
    before = jnp.dot(earlier, onehot, preferred_element_type=jnp.float32)
    ranking = jnp.sum(before * onehot.astype(jnp.float32), axis=1).astype(jnp.int32)
    position = target * capacity + ranking
    ids_sent = jnp.full((slots_all,), -1, jnp.int32).at[position].set(cluster_id)
    rows_buffer = jnp.zeros((slots_all, columns), jnp.float32).at[position].set(embeddings)
    got_rows, got_ids = (
        lax.all_to_all(
            rows_buffer.reshape(owners, capacity, columns),
            "docs",
            split_axis=0,
            concat_axis=0,
            tiled=True,
        ),
        lax.all_to_all(
            ids_sent.reshape(owners, capacity), "docs", split_axis=0, concat_axis=0, tiled=True
        ),
    )
    normed = unit_rows(got_rows.reshape(slots_all, columns))
    got_ids = got_ids.reshape(slots_all)
    own_index = lax.axis_index("split")
    local_pos = jnp.arange(slots_all, dtype=jnp.int32)
    own_pos = own_index * slots_all + local_pos
    block_len = math.gcd(slots_all, 512)
    block_count = slots_all // block_len
    own_blocks = (
        normed.reshape(block_count, block_len, columns),
        got_ids.reshape(block_count, block_len),
        own_pos.reshape(block_count, block_len),
    )
    right_rows = lax.all_gather(normed, "split", axis=0, tiled=True)
    right_ids = lax.all_gather(got_ids, "split", axis=0, tiled=True)
    right_pos = jnp.arange(right_rows.shape[0], dtype=jnp.int32)

    def row_block(blockargs):
        return jnp.max(
            masked_scores(
                blockargs[0], blockargs[1], blockargs[2], right_rows, right_ids, right_pos
            ),
            axis=1,
        )

    highest = jnp.maximum(
        jnp.full((slots_all,), -1.0, jnp.float32), lax.map(row_block, own_blocks).reshape(slots_all)
    )
    returned = lax.all_to_all(
        highest.reshape(owners, capacity), "docs", split_axis=0, concat_axis=0, tiled=True
    )
    return returned.reshape(slots_all)[position]


def solution(mesh):
    return jax.shard_map(
        per_device,
        mesh=mesh,
        in_specs=(P(("docs", "split"), None), P(("docs", "split"))),
        out_specs=P(("docs", "split")),
        check_vma=False,
    )
```

profile of v0, /device:TPU:1, one launch (start us, length us, event | category | flops | bytes accessed | tf_op | source)
XLA Modules:
  0.0 311.8 jit_solution(10769239542583701112)
XLA Ops:
  6.5 0.7 add_select_fusion
  7.8 1.3 broadcast_clamp_fusion
  9.1 8.7 %scatter_custom_fusion.1 = f32[2048,768]{1,0:T(8,128)} fusion(s32[1024]{0:T(1024)S(1)} %get-tuple-element.79, f32[1024,768]{1,0:T(8,128)} %param.4, f32[]{:T(128)} %constant.21.clone.1), kind=kCustom, calls=%fused_computation.21 | custom fusion | bytes 6291968 | tf_op jit(solution)/shard_map/scatter | solution.py:45
  17.7 83.0 %all_to_all.20 = f32[32,64,768]{2,1,0:T(8,128)S(1)} all-to-all(f32[32,64,768]{2,1,0:T(8,128)} %bitcast.29), channel_id=1, replica_groups=mesh['docs'=32,'split'=4] {'docs'}, dimensions={0} | all-to-all | bytes 12582912 | tf_op jit(solution)/shard_map/all_to_all | solution.py:47
  100.7 2.6 copy-done
  103.9 4.9 %fusion.7 = bf16[2048,768]{1,0:T(8,128)(2,1)} fusion(f32[32,64,768]{2,1,0:T(8,128)} %copy-done, f32[2048]{0:T(1024)S(1)} %mul.57), kind=kLoop, calls=%fused_computation.15 | loop fusion | flops 3145728 | bytes 9445376 | tf_op jit(solution)/shard_map/convert_element_type | solution.py:17
  108.8 4.5 %scatter_custom_fusion = s32[2048]{0:T(1024)S(1)} fusion(s32[1024]{0:T(1024)S(1)} %get-tuple-element.79, s32[1024]{0:T(1024)} %param.5, s32[]{:T(128)} %constant.34.clone.1), kind=kCustom, calls=%fused_computation.38 | custom fusion | bytes 8704 | tf_op jit(solution)/shard_map/scatter | solution.py:44
  113.3 0.7 all_to_all.13
  113.9 4.7 %all-to-all-start = ((s32[32,1,64]{2,1,0:T(1,128)}), s32[32,1,64]{2,1,0:T(1,128)S(1)}, u32[]{:S(2)}, u32[]{:S(2)}) async-start(s32[32,1,64]{2,1,0:T(1,128)} %all_to_all.13), calls=%async_computation | async-start | bytes 32768 | tf_op jit(solution)/shard_map/all_to_all | solution.py:54
  118.7 6.9 %all-to-all-done = s32[32,1,64]{2,1,0:T(1,128)S(1)} async-done(((s32[32,1,64]{2,1,0:T(1,128)}), s32[32,1,64]{2,1,0:T(1,128)S(1)}, u32[]{:S(2)}, u32[]{:S(2)}) %all-to-all-start) | async-done | bytes 8224 | tf_op jit(solution)/shard_map/all_to_all | solution.py:54
  125.6 0.6 broadcast.89
  126.2 0.7 reduce.9
  127.0 10.5 %all_gather.6 = s32[8192]{0:T(1024)S(1)} all-gather(s32[2048]{0:T(1024)S(1)} %reshape.90), channel_id=1, replica_groups=mesh['docs'=32,'split'=4] {'split'}, dimensions={0}, use_global_device_ids=true | all-gather | bytes 40960 | tf_op jit(solution)/shard_map/all_gather | solution.py:71
  137.6 3.2 %fusion.8 = bf16[4,512,768]{2,1,0:T(8,128)(2,1)S(1)} fusion(f32[4,512]{1,0:T(4,128)S(1)} %mul.54, f32[4,512,768]{2,1,0:T(8,128)} %bitcast.28), kind=kLoop, calls=%fused_computation.17 | loop fusion | flops 3145728 | bytes 9445376 | tf_op jit(solution)/shard_map/convert_element_type | solution.py:17
  140.8 85.3 %all-gather.2.cloned.1.call-done = bf16[8192,768]{1,0:T(8,128)(2,1)} async-done(((bf16[2048,768]{1,0:T(8,128)(2,1)}), bf16[8192,768]{1,0:T(8,128)(2,1)}) %all-gather.2.cloned.1.call-update) | async-done | bytes 12582928 | tf_op jit(solution)/shard_map/all_gather | solution.py:70
  226.1 52.4 %while.11 = (s32[]{:T(128)}, f32[4,512]{1,0:T(4,128)S(1)}, s32[4,512]{1,0:T(4,128)S(1)}, s32[8192]{0:T(1024)S(1)}, s32[4,512]{1,0:T(4,128)S(1)}, /*index=5*/bf16...) while((s32[]{:T(128)}, f32[4,512]{1,0:T(4,128)S(1)}, ...), condition=%wide.region_6.7_spmd.clone, body=%wide.region_4.6_spmd.clone.sunk | while | flops 6467616768 | bytes 13423729 | solution.py:83
  226.1 13.0 %select_reduce_fusion.2 = f32[512]{0:T(512)S(1)} fusion(bf16[8192,768]{1,0:T(8,128)(2,1)} %get-tuple-element.153, s32[512]{0:T(512)S(1)} %bitcast.33, s32[8192]{0:T(1024)S(1)} %get-tuple-element.150, s32[512]{0:T(512)S(1)} %bitcast.31, pred[512]{0:T(512)(128)(4,1)S(1)} %broadcast_compare_fusion.2, bf16[4,512,768]{2,1,0:T(8,128)(2,1)S(1)} %get-tuple-element.152, ...), kind=kOutput, calls=%fused_computation.5.clone.1 | convolution fusion | flops 6467616256 | bytes 13408772 | tf_op jit(solution)/shard_map/while/body/eval_jaxpr/dot_general | solution.py:21
  239.2 13.0 %select_reduce_fusion.2 = f32[512]{0:T(512)S(1)} fusion(bf16[8192,768]{1,0:T(8,128)(2,1)} %get-tuple-element.153, s32[512]{0:T(512)S(1)} %bitcast.33, s32[8192]{0:T(1024)S(1)} %get-tuple-element.150, s32[512]{0:T(512)S(1)} %bitcast.31, pred[512]{0:T(512)(128)(4,1)S(1)} %broadcast_compare_fusion.2, bf16[4,512,768]{2,1,0:T(8,128)(2,1)S(1)} %get-tuple-element.152, ...), kind=kOutput, calls=%fused_computation.5.clone.1 | convolution fusion | flops 6467616256 | bytes 13408772 | tf_op jit(solution)/shard_map/while/body/eval_jaxpr/dot_general | solution.py:21
  252.3 13.0 %select_reduce_fusion.2 = f32[512]{0:T(512)S(1)} fusion(bf16[8192,768]{1,0:T(8,128)(2,1)} %get-tuple-element.153, s32[512]{0:T(512)S(1)} %bitcast.33, s32[8192]{0:T(1024)S(1)} %get-tuple-element.150, s32[512]{0:T(512)S(1)} %bitcast.31, pred[512]{0:T(512)(128)(4,1)S(1)} %broadcast_compare_fusion.2, bf16[4,512,768]{2,1,0:T(8,128)(2,1)S(1)} %get-tuple-element.152, ...), kind=kOutput, calls=%fused_computation.5.clone.1 | convolution fusion | flops 6467616256 | bytes 13408772 | tf_op jit(solution)/shard_map/while/body/eval_jaxpr/dot_general | solution.py:21
  265.4 13.0 %select_reduce_fusion.2 = f32[512]{0:T(512)S(1)} fusion(bf16[8192,768]{1,0:T(8,128)(2,1)} %get-tuple-element.153, s32[512]{0:T(512)S(1)} %bitcast.33, s32[8192]{0:T(1024)S(1)} %get-tuple-element.150, s32[512]{0:T(512)S(1)} %bitcast.31, pred[512]{0:T(512)(128)(4,1)S(1)} %broadcast_compare_fusion.2, bf16[4,512,768]{2,1,0:T(8,128)(2,1)S(1)} %get-tuple-element.152, ...), kind=kOutput, calls=%fused_computation.5.clone.1 | convolution fusion | flops 6467616256 | bytes 13408772 | tf_op jit(solution)/shard_map/while/body/eval_jaxpr/dot_general | solution.py:21
  278.6 14.4 %all_to_all.21 = f32[32,1,64]{2,1,0:T(1,128)S(1)} all-to-all(f32[32,1,64]{2,1,0:T(1,128)S(1)} %max_broadcast_in_dim.15), channel_id=1, replica_groups=mesh['docs'=32,'split'=4] {'docs'}, dimensions={0} | all-to-all | bytes 16384 | tf_op jit(solution)/shard_map/all_to_all | solution.py:85
  293.0 0.6 broadcast.90
  293.6 0.7 reduce.10
  294.4 10.5 %gather_fusion = f32[1024]{0:T(1024)} fusion(f32[2048]{0:T(1024)S(1)} %reshape.94, s32[1024]{0:T(1024)S(1)} %copy-done.1), kind=kCustom, calls=%fused_computation | custom fusion | bytes 12288 | tf_op jit(solution)/shard_map/gather | solution.py:88
  (29 shorter events, 1.8 us)
Async XLA Ops:
  6.5 219.5 %all-gather.2.cloned.1.call-start = ((), (), s32[]{:S(2)}) async-start(), calls=%async_computation.3 | async-start | bytes 15728640 | tf_op jit(solution)/shard_map/all_gather | solution.py:70
  100.7 2.6 copy-start
  113.9 11.6 %all-to-all-start = ((s32[32,1,64]{2,1,0:T(1,128)}), s32[32,1,64]{2,1,0:T(1,128)S(1)}, u32[]{:S(2)}, u32[]{:S(2)}) async-start(s32[32,1,64]{2,1,0:T(1,128)} %all_to_all.13), calls=%async_computation | async-start | bytes 32768 | tf_op jit(solution)/shard_map/all_to_all | solution.py:54
  226.1 68.3 %copy-start.1 = (s32[1024]{0:T(1024)S(1)}, s32[1024]{0:T(1024)}, u32[]{:S(2)}) copy-start(s32[1024]{0:T(1024)} %get-tuple-element.78) | copy-start | bytes 12292
Sparse Core Ops, SparseCore 0:
  108.9 117.1 all-gather.1
where the time goes:
time: 312 us
  blocking collectives  108 us (35%)
  waiting for transfers between devices  92.2 us (30%)
  matrix products  52.6 us (17%)
  local copies, waits for them, and re-layouts  28.8 us (9%)
  between operations  13.5 us (4%)
  other arithmetic  12 us (4%)
  starting transfers between devices  4.7 us (2%)
    all_gather x1, waiting for transfers between devices, per_device(): right_rows = lax.all_gather(normed, 'split', axis=0, tiled=True)  85.3 us
    all_to_all x1, blocking collectives, per_device(): lax.all_to_all(rows_buffer.reshape(owners, capacity, columns), 'docs', sp...  83 us
    dot_general x4, matrix products, masked_scores(): lax.dot_general(own_rows, right_rows, (((1,), (1,)), ((), ())), preferred...  52 us
    all_to_all x1, blocking collectives, per_device(): lax.all_to_all(highest.reshape(owners, capacity), 'docs', split_axis=0, c...  14.4 us
    gather x1, local copies, waits for them, and re-layouts, per_device(): return returned.reshape(slots_all)[position]  10.5 us
    all_gather x1, blocking collectives, per_device(): right_ids = lax.all_gather(got_ids, 'split', axis=0, tiled=True)  10.5 us
    scatter x1, local copies, waits for them, and re-layouts, per_device(): jnp.zeros((slots_all, columns), jnp.float32).at[position].set(embeddings)  8.66 us
    convert_element_type x2, other arithmetic, unit_rows(): return (rows * scaling).astype(jnp.bfloat16)  8.08 us
  transfers between devices with their start and end apart: 2, of which 2 were waited for; matrix products, arithmetic and copies ran while one was open for 3% of the time, Pallas kernels for 0%

commit v1 on v0

v1 whole, which is shorter than its diff:
```python
import jax
import jax.numpy as jnp
from jax import lax
from jax.experimental import pallas as pl
from jax.experimental.pallas import tpu as pltpu
from jax.sharding import PartitionSpec as P

F32 = jnp.float32
BF16 = jnp.bfloat16
CLU_DEV = 4
EPSILON = 1e-06
CAP = 64
T = 16
CHUNKS = CAP // T
GROUPS = ((0,), (1,), (2,), (3,))
X1_CHUNKS = (0, 1)
X2_CHUNKS = (2, 3)
AXES = ("docs", "split")
NT = (((1,), (1,)), ((), ()))
NN = (((1,), (0,)), ((), ()))
VMEM = pl.BlockSpec(memory_space=pltpu.VMEM)
SMEM = pl.BlockSpec(memory_space=pltpu.SMEM)
HBM = pl.BlockSpec(memory_space=pl.ANY)
PARAMS = pltpu.CompilerParams(vmem_limit_bytes=48 * 2**20)


def iota(shape, axis):
    return lax.broadcasted_iota(jnp.int32, shape, axis)


def place(unit, rng, rank, owners, chunk):
    inside = (rank >= chunk * T) & (rank < (chunk + 1) * T)
    row = jnp.where(inside, rng * T + rank - chunk * T, -1)
    pick = jnp.where(iota((owners * T, row.shape[1]), 0) == row, 1.0, 0.0).astype(BF16)
    return lax.dot_general(pick, unit, NN, preferred_element_type=F32).astype(BF16)


def prepare(owners, split, ids_ref, emb_ref, pos_ref, unit_ref, first_ref, sent_ids_ref, emb, sems):
    docs, columns = emb.shape
    parts = 4
    size = docs // parts
    copies = [
        pltpu.make_async_copy(emb_ref.at[pl.ds(p * size, size)], emb.at[pl.ds(p * size, size)], sems.at[p])
        for p in range(parts)
    ]
    for copy in copies:
        copy.start()
    ids = ids_ref[...]
    rng = ids >> 2
    key = (ids * docs + iota(ids.shape, 1)).astype(F32)
    base = (rng * (CLU_DEV * docs)).astype(F32)
    key_col = jnp.transpose(jnp.broadcast_to(key, (128, docs)))
    ranks = []
    for lane in range(0, docs, 128):
        before = (key_col < key[:, lane : lane + 128]) & (key_col >= base[:, lane : lane + 128])
        ranks.append(jnp.sum(jnp.where(before, 1.0, 0.0), axis=0, keepdims=True))
    rank = jnp.concatenate(ranks, axis=1).astype(jnp.int32)
    pos_ref[0:1, :] = rng
    pos_ref[1:2, :] = rank
    owner = jnp.where(iota((owners * split, docs), 0) // split == rng, 1.0, 0.0).astype(BF16)
    code = jnp.where(iota((CAP, docs), 0) == rank, (ids & 3) + 1, 0).astype(F32).astype(BF16)
    sent_ids_ref[...] = lax.dot_general(owner, code, NT, preferred_element_type=F32)
    for p in range(parts):
        copies[p].wait()
        rows = emb[p * size : (p + 1) * size, :]
        scaling = lax.rsqrt(jnp.mean(rows * rows, axis=1, keepdims=True) + EPSILON) * columns ** (-0.5)
        unit_ref[p * size : (p + 1) * size, :] = (rows * scaling).astype(BF16)
    first_ref[...] = place(unit_ref[...], rng, rank, owners, 0)


def place_rest(owners, pos_ref, unit_ref, *outs):
    unit = unit_ref[...]
    for chunk, out in enumerate(outs, start=1):
        out[...] = place(unit, pos_ref[0:1, :], pos_ref[1:2, :], owners, chunk)


def slot_ids(split, owners, roles_ref, got_ref, ids_ref):
    got = got_ref[...]
    width = owners * T
    for chunk in range(CHUNKS):
        spread = jnp.where(iota((CAP, width), 0) == chunk * T + iota((CAP, width), 1) % T, 1.0, 0.0).astype(BF16)
        wide = lax.dot_general(got.astype(BF16), spread, NN, preferred_element_type=F32)
        source = iota((owners * split, width), 0) - iota((owners * split, width), 1) // T * split
        for role in range(4):
            codes = jnp.sum(jnp.where(source == roles_ref[role], wide, 0.0), axis=0, keepdims=True)
            block = role * CHUNKS + chunk
            ids_ref[block : block + 1, :] = codes * roles_ref[4 + role].astype(F32)


def scores(names, pairs, fresh, *refs):
    ids_ref, best_in_ref = refs[0], refs[1]
    blocks = dict(zip(names, refs[2 : 2 + len(names)]))
    best_ref = refs[2 + len(names)]
    best_ref[...] = jnp.full(best_ref.shape, -1.0, F32) if fresh else best_in_ref[...]
    width = best_ref.shape[1]

    def into(block, values):
        best_ref[block : block + 1, :] = jnp.maximum(best_ref[block : block + 1, :], values)

    for left in dict.fromkeys(p[0] for p in pairs):
        ids_left = ids_ref[left : left + 1, :]
        ids_rows = jnp.transpose(jnp.broadcast_to(jnp.where(ids_left > 0, ids_left, -1.0), (128, width)))[:, :1]
        total = None
        for right in [p[1] for p in pairs if p[0] == left]:
            score = lax.dot_general(blocks[left][...], blocks[right][...], NT, preferred_element_type=F32)
            allowed = ids_rows == ids_ref[right : right + 1, :]
            if left == right:
                allowed = allowed & (iota((width, width), 0) != iota((width, width), 1))
            score = jnp.where(allowed, score, -1.0)
            into(right, jnp.max(score, axis=0, keepdims=True))
            if left != right:
                for lane in range(0, width, 128):
                    part = score[:, lane : lane + 128]
                    total = part if total is None else jnp.maximum(total, part)
        if total is not None:
            into(left, jnp.max(jnp.transpose(total), axis=0, keepdims=True))


def pack(split, owners, roles_ref, best_ref, out_ref):
    width = best_ref.shape[1]
    rows = owners * split
    source = iota((rows, width), 0) - iota((rows, width), 1) // T * split
    result = jnp.zeros((rows, CAP), F32)
    for chunk in range(CHUNKS):
        wide = jnp.zeros((rows, width), F32)
        for role in range(4):
            block = role * CHUNKS + chunk
            wide = jnp.where(source == roles_ref[role], best_ref[block : block + 1, :], wide)
        narrow = jnp.where(iota((width, CAP), 1) == chunk * T + iota((width, CAP), 0) % T, 1.0, 0.0)
        result = result + lax.dot_general(
            wide, narrow, NN, precision=lax.Precision.HIGHEST, preferred_element_type=F32
        )
    out_ref[...] = result


def finish(owners, split, pos_ref, got_ref, out_ref):
    best = got_ref[pl.ds(0, owners, stride=split), :]
    for part in range(1, split):
        best = jnp.maximum(best, got_ref[pl.ds(part, owners, stride=split), :])
    rng, rank = pos_ref[0:1, :], pos_ref[1:2, :]
    docs = rng.shape[1]
    pick = jnp.where(iota((owners, docs), 0) == rng, 1.0, 0.0)
    columns = lax.dot_general(
        best, pick, (((0,), (0,)), ((), ())), precision=lax.Precision.HIGHEST, preferred_element_type=F32
    )
    out_ref[...] = jnp.sum(jnp.where(iota((CAP, docs), 0) == rank, columns, 0.0), axis=0, keepdims=True)


def ring_moves(owners, split):
    def moves(pairs):
        out = []
        for d in range(owners):
            for a, b in pairs:
                if d % 2:
                    a, b = (2 - a) % split, (2 - b) % split
                out.append((d * split + a % split, d * split + b % split))
        return out

    return moves([(a, a - 1) for a in range(split)]), moves([(1, 0), (2, 1)]), moves([(2, 3), (3, 0)])


def per_device(embeddings, cluster_id):
    docs, columns = embeddings.shape
    owners, split = lax.axis_size("docs"), lax.axis_size("split")
    width = owners * T
    block = jax.ShapeDtypeStruct((width, columns), BF16)
    odd, place_x = lax.axis_index("docs") % 2, lax.axis_index("split")
    step = 1 - 2 * odd
    mirrored = jnp.where(odd == 1, (2 - place_x) % split, place_x)
    roles = jnp.stack(
        [
            place_x,
            (place_x + step) % split,
            (place_x + 2) % split,
            (place_x - step) % split,
            1,
            1,
            (mirrored <= 1).astype(jnp.int32),
            ((mirrored == 3) | (mirrored == 0)).astype(jnp.int32),
        ]
    ).astype(jnp.int32)

    pos, unit, first, sent_ids = pl.pallas_call(
        lambda *refs: prepare(owners, split, *refs),
        in_specs=[VMEM, HBM],
        out_specs=[VMEM] * 4,
        out_shape=[
            jax.ShapeDtypeStruct((2, docs), jnp.int32),
            jax.ShapeDtypeStruct((docs, columns), BF16),
            block,
            jax.ShapeDtypeStruct((owners * split, CAP), F32),
        ],
        scratch_shapes=[pltpu.VMEM((docs, columns), F32), pltpu.SemaphoreType.DMA((4,))],
        compiler_params=PARAMS,
        name="prepare",
    )(cluster_id.reshape(1, docs), embeddings)
    rest = pl.pallas_call(
        lambda *refs: place_rest(owners, *refs),
        in_specs=[VMEM, VMEM],
        out_specs=[VMEM] * (CHUNKS - 1),
        out_shape=[block] * (CHUNKS - 1),
        compiler_params=PARAMS,
        name="place_rest",
    )(pos, unit)
    placed = [first, *rest]

    def to_owner(x):
        return lax.all_to_all(x.reshape(owners, T, columns), "docs", 0, 0, tiled=True).reshape(width, columns)

    own = [to_owner(x) for x in placed]
    got_ids = lax.all_to_all(sent_ids, AXES, 0, 0, tiled=True)
    ids = pl.pallas_call(
        lambda *refs: slot_ids(split, owners, *refs),
        in_specs=[SMEM, VMEM],
        out_specs=VMEM,
        out_shape=jax.ShapeDtypeStruct((4 * CHUNKS, width), F32),
        compiler_params=PARAMS,
        name="slot_ids",
    )(roles, got_ids)

    moves_n, moves_1, moves_2 = ring_moves(owners, split)
    near = [lax.ppermute(x, AXES, moves_n) for x in own]
    held = {c: x for c, x in enumerate(own)}
    held |= {CHUNKS + c: x for c, x in enumerate(near)}
    held |= {2 * CHUNKS + c: lax.ppermute(near[c], AXES, moves_1) for c in X1_CHUNKS}
    held |= {3 * CHUNKS + c: lax.ppermute(own[c], AXES, moves_2) for c in X2_CHUNKS}

    def score_call(best, pairs, name):
        names = sorted({b for p in pairs for b in p})
        return pl.pallas_call(
            lambda *refs: scores(names, pairs, best is None, *refs),
            in_specs=[VMEM] * (2 + len(names)),
            out_specs=VMEM,
            out_shape=jax.ShapeDtypeStruct((4 * CHUNKS, width), F32),
            compiler_params=PARAMS,
            name=name,
        )(ids, ids if best is None else best, *[held[b] for b in names])

    every = range(CHUNKS)
    best = score_call(None, [(a, b) for a in every for b in every if a <= b], "own_own")
    best = score_call(best, [(a, CHUNKS + b) for a in every for b in (0, 1)], "own_near01")
    best = score_call(
        best, [(a, b) for a in every for b in (2 * CHUNKS, 2 * CHUNKS + 1, CHUNKS + 2)], "own_far01_near2"
    )
    best = score_call(
        best,
        [(a, CHUNKS + 3) for a in every] + [(CHUNKS + a, 3 * CHUNKS + b) for a in every for b in X2_CHUNKS],
        "last",
    )
    sent_best = pl.pallas_call(
        lambda *refs: pack(split, owners, *refs),
        in_specs=[SMEM, VMEM],
        out_specs=VMEM,
        out_shape=jax.ShapeDtypeStruct((owners * split, CAP), F32),
        compiler_params=PARAMS,
        name="pack",
    )(roles, best)
    got_best = lax.all_to_all(sent_best, AXES, 0, 0, tiled=True)
    out = pl.pallas_call(
        lambda *refs: finish(owners, split, *refs),
        in_specs=[VMEM, VMEM],
        out_specs=VMEM,
        out_shape=jax.ShapeDtypeStruct((1, docs), F32),
        compiler_params=PARAMS,
        name="finish",
    )(pos, got_best)
    return out.reshape(docs)


def solution(mesh):
    return jax.shard_map(
        per_device,
        mesh=mesh,
        in_specs=(P(AXES, None), P(AXES)),
        out_specs=P(AXES),
        check_vma=False,
    )
```

time: 312 us -> 158 us (0.51)
  waiting for transfers between devices: 92.2 us -> 30.5 us
  matrix products: 52.6 us -> 0 us
  blocking collectives: 108 us -> 56.5 us
  Pallas kernels: 0 us -> 33.7 us
  starting transfers between devices: 4.7 us -> 34.4 us
  local copies, waits for them, and re-layouts: 28.8 us -> 2.66 us
  between operations: 13.5 us -> 0.2 us
  other arithmetic: 12 us -> 0 us
    all_gather x1 -> x0, waiting for transfers between devices: 85.3 us -> none  [per_device(): right_rows = lax.all_gather(normed, 'split', axis=0, tiled=True)]
    dot_general x5 -> x0, matrix products: 52.6 us -> none  [the longest x4 52 us: masked_scores(): lax.dot_general(own_rows, right_rows, (((1,), (1,)), ((), ())), preferred...]
    all_to_all x2 -> x3, blocking collectives: 97.4 us -> 56.5 us  [the longest x2 41.5 us: to_owner(): lax.all_to_all(x.reshape(owners, T, columns), 'docs', 0, 0, tiled=True)]
    pallas_call x0 -> x9, Pallas kernels: none -> 33.7 us  [the longest x4 23.9 us: score_call(): pl.pallas_call(lambda *refs: scores(names, pairs, best is None, *refs), i...]
    all_to_all x1 -> x3, waiting for transfers between devices: 6.91 us -> 30.5 us  [the longest x2 18.4 us: to_owner(): lax.all_to_all(x.reshape(owners, T, columns), 'docs', 0, 0, tiled=True)]
    ppermute x0 -> x8, starting transfers between devices: none -> 16.9 us  [the longest x2 8.8 us: per_device(): lax.ppermute(own[c], AXES, moves_2)]
    scatter x2 -> x0, local copies, waits for them, and re-layouts: 13.1 us -> none  [the longest x1 8.66 us: per_device(): jnp.zeros((slots_all, columns), jnp.float32).at[position].set(embeddings)]
    all_to_all x1 -> x3, starting transfers between devices: 4.7 us -> 17.5 us  [the longest x2 9.81 us: to_owner(): lax.all_to_all(x.reshape(owners, T, columns), 'docs', 0, 0, tiled=True)]
  transfers between devices with their start and end apart: 2 -> 11, of which waited for: 2 -> 3; matrix products, arithmetic and copies ran while one was open for 3% -> 0% of each run, Pallas kernels for 0% -> 11%
where the time goes in v1:
time: 158 us
  blocking collectives  56.5 us (36%)
  starting transfers between devices  34.4 us (22%)
  Pallas kernels  33.7 us (21%)
  waiting for transfers between devices  30.5 us (19%)
  local copies, waits for them, and re-layouts  2.66 us (2%)
    all_to_all x2, blocking collectives, to_owner(): lax.all_to_all(x.reshape(owners, T, columns), 'docs', 0, 0, tiled=True)  41.5 us
    pallas_call x4, Pallas kernels, score_call(): pl.pallas_call(lambda *refs: scores(names, pairs, best is None, *refs), i...  23.9 us
    all_to_all x2, waiting for transfers between devices, to_owner(): lax.all_to_all(x.reshape(owners, T, columns), 'docs', 0, 0, tiled=True)  18.4 us
    all_to_all x1, blocking collectives, per_device(): got_best = lax.all_to_all(sent_best, AXES, 0, 0, tiled=True)  15 us
    all_to_all x1, waiting for transfers between devices, per_device(): got_ids = lax.all_to_all(sent_ids, AXES, 0, 0, tiled=True)  12 us
    all_to_all x2, starting transfers between devices, to_owner(): lax.all_to_all(x.reshape(owners, T, columns), 'docs', 0, 0, tiled=True)  9.81 us
    ppermute x2, starting transfers between devices, per_device(): lax.ppermute(own[c], AXES, moves_2)  8.8 us
    all_to_all x1, starting transfers between devices, per_device(): got_ids = lax.all_to_all(sent_ids, AXES, 0, 0, tiled=True)  7.65 us
  transfers between devices with their start and end apart: 11, of which 3 were waited for; matrix products, arithmetic and copies ran while one was open for 0% of the time, Pallas kernels for 11%

profile of v1, /device:TPU:1, one launch (start us, length us, event | category | flops | bytes accessed | tf_op | source)
XLA Modules:
  0.0 157.9 jit_solution(4373483030292404080)
XLA Ops:
  0.0 1.9 %copy-done = f32[1024,768]{1,0:T(8,128)S(1)} copy-done((f32[1024,768]{1,0:T(8,128)S(1)}, f32[1024,768]{1,0:T(8,128)}, u32[]{:S(2)}) %copy-start) | copy-done | bytes 3145752
  2.6 2.8 %prepare.1 = (s32[2,1024]{1,0:T(2,128)S(1)}, bf16[1024,768]{1,0:T(8,128)(2,1)S(1)}, bf16[512,768]{1,0:T(8,128)(2,1)S(1)}, f32[128,64]{1,0:T(8,128)}) custom-call(s32[1,1024]{1,0:T(1,128)S(1)} %bitcast.52, f32[1024,768]{1,0:T(8,128)S(1)} %copy-done), custom_call_target="tpu_custom_call" | custom-call | tf_op jit(solution)/shard_map/prepare/pallas_call | solution.py:183
  5.4 3.0 %place_rest.1 = (bf16[512,768]{1,0:T(8,128)(2,1)S(1)}, bf16[512,768]{1,0:T(8,128)(2,1)}, bf16[512,768]{1,0:T(8,128)(2,1)S(1)}) custom-call(s32[2,1024]{1,0:T(2,128)S(1)} %get-tuple-element.12.refs_0_, bf16[1024,768]{1,0:T(8,128)(2,1)S(1)} %get-tuple-element.15.refs_1_), custom_call_target="tpu_custom_call" | custom-call | tf_op jit(solution)/shard_map/place_rest/pallas_call | solution.py:197
  8.3 23.6 %all_to_all.42 = bf16[32,16,768]{2,1,0:T(8,128)(2,1)S(1)} all-to-all(bf16[32,16,768]{2,1,0:T(8,128)(2,1)S(1)} %bitcast.48), channel_id=1, replica_groups=mesh['docs'=32,'split'=4] {'docs'}, dimensions={0} | all-to-all | bytes 1572864 | tf_op jit(solution)/shard_map/all_to_all | solution.py:208
  32.0 17.9 %all_to_all.43 = bf16[32,16,768]{2,1,0:T(8,128)(2,1)S(1)} all-to-all(bf16[32,16,768]{2,1,0:T(8,128)(2,1)S(1)} %bitcast.47), channel_id=1, replica_groups=mesh['docs'=32,'split'=4] {'docs'}, dimensions={0} | all-to-all | bytes 1572864 | tf_op jit(solution)/shard_map/all_to_all | solution.py:208
  49.8 4.1 %all-to-all-start.3 = ((bf16[32,16,768]{2,1,0:T(8,128)(2,1)}), bf16[32,16,768]{2,1,0:T(8,128)(2,1)S(1)}, u32[]{:S(2)}, u32[]{:S(2)}) async-start(bf16[32,16,768]{2,1,0:T(8,128)(2,1)} %bitcast.14), calls=%async_computation.3 | async-start | bytes 1572864 | tf_op jit(solution)/shard_map/all_to_all | solution.py:208
  54.0 1.3 collective-permute-start.1
  55.2 1.2 collective-permute-start
  56.5 11.8 %all-to-all-done.3 = bf16[32,16,768]{2,1,0:T(8,128)(2,1)S(1)} async-done(((bf16[32,16,768]{2,1,0:T(8,128)(2,1)}), bf16[32,16,768]{2,1,0:T(8,128)(2,1)S(1)}, u32[]{:S(2)}, u32[]{:S(2)}) %all-to-all-start.3) | async-done | bytes 786464 | tf_op jit(solution)/shard_map/all_to_all | solution.py:208
  68.3 1.2 collective-permute-start.2
  69.5 5.7 %all-to-all-start.4 = ((bf16[32,16,768]{2,1,0:T(8,128)(2,1)}), bf16[32,16,768]{2,1,0:T(8,128)(2,1)S(1)}, u32[]{:S(2)}, u32[]{:S(2)}) async-start(bf16[32,16,768]{2,1,0:T(8,128)(2,1)} %bitcast.46), calls=%async_computation.4 | async-start | bytes 1572864 | tf_op jit(solution)/shard_map/all_to_all | solution.py:208
  75.2 3.3 %collective-permute-start.6 = (bf16[512,768]{1,0:T(8,128)(2,1)S(1)}, bf16[512,768]{1,0:T(8,128)(2,1)}, u32[]{:S(2)}, u32[]{:S(2)}) collective-permute-start(bf16[512,768]{1,0:T(8,128)(2,1)S(1)} %bitcast.35), channel_id=1, source_target_pairs={{2,3},{3,0},{4,7},{7,6},{10,11},{11,8},{12,15},{15,14},{18,19},{19... | collective-permute-start | bytes 2359304 | tf_op jit(solution)/shard_map/ppermute | solution.py:226
  78.5 2.2 %collective-permute-start.4 = (bf16[512,768]{1,0:T(8,128)(2,1)}, bf16[512,768]{1,0:T(8,128)(2,1)}, u32[]{:S(2)}, u32[]{:S(2)}) collective-permute-start(bf16[512,768]{1,0:T(8,128)(2,1)} %collective-permute-done.1.refs_7_), channel_id=1, source_target_pairs={{1,0},{2,1},{5,6},{4,5},{9,8},{10,9},{13,14},{12,13},{17,16},{18,1... | collective-permute-start | bytes 2359304 | tf_op jit(solution)/shard_map/ppermute | solution.py:225
  80.7 2.2 %collective-permute-start.3 = (bf16[512,768]{1,0:T(8,128)(2,1)}, bf16[512,768]{1,0:T(8,128)(2,1)}, u32[]{:S(2)}, u32[]{:S(2)}) collective-permute-start(bf16[512,768]{1,0:T(8,128)(2,1)} %collective-permute-done.refs_6_), channel_id=1, source_target_pairs={{1,0},{2,1},{5,6},{4,5},{9,8},{10,9},{13,14},{12,13},{17,16},{18,1... | collective-permute-start | bytes 2359304 | tf_op jit(solution)/shard_map/ppermute | solution.py:225
  83.0 6.6 %all-to-all-done.4 = bf16[32,16,768]{2,1,0:T(8,128)(2,1)S(1)} async-done(((bf16[32,16,768]{2,1,0:T(8,128)(2,1)}), bf16[32,16,768]{2,1,0:T(8,128)(2,1)S(1)}, u32[]{:S(2)}, u32[]{:S(2)}) %all-to-all-start.4) | async-done | bytes 786464 | tf_op jit(solution)/shard_map/all_to_all | solution.py:208
  89.6 5.5 %collective-permute-start.7 = (bf16[512,768]{1,0:T(8,128)(2,1)S(1)}, bf16[512,768]{1,0:T(8,128)(2,1)}, u32[]{:S(2)}, u32[]{:S(2)}) collective-permute-start(bf16[512,768]{1,0:T(8,128)(2,1)S(1)} %bitcast.41), channel_id=1, source_target_pairs={{2,3},{3,0},{4,7},{7,6},{10,11},{11,8},{12,15},{15,14},{18,19},{19... | collective-permute-start | bytes 2359304 | tf_op jit(solution)/shard_map/ppermute | solution.py:226
  95.0 7.7 %all-to-all-start = ((f32[128,1,64]{2,1,0:T(1,128)}), f32[128,1,64]{2,1,0:T(1,128)S(1)}, u32[]{:S(2)}, u32[]{:S(2)}) async-start(f32[128,1,64]{2,1,0:T(1,128)} %bitcast.8), calls=%async_computation | async-start | bytes 131072 | tf_op jit(solution)/shard_map/all_to_all | solution.py:211
  102.8 12.0 %all-to-all-done = f32[128,1,64]{2,1,0:T(1,128)S(1)} async-done(((f32[128,1,64]{2,1,0:T(1,128)}), f32[128,1,64]{2,1,0:T(1,128)S(1)}, u32[]{:S(2)}, u32[]{:S(2)}) %all-to-all-start) | async-done | bytes 32800 | tf_op jit(solution)/shard_map/all_to_all | solution.py:211
  116.1 4.4 %own_own.1.refs_1_ = f32[16,512]{1,0:T(8,128)S(1)} custom-call(f32[16,512]{1,0:T(8,128)S(1)} %slot_ids.1.refs_0_.refs_1_, f32[16,512]{1,0:T(8,128)S(1)} %slot_ids.1.refs_0_.refs_1_, bf16[512,768]{1,0:T(8,128)(2,1)S(1)} %bitcast.30, bf16[512,768]{1,0:T(8,128)(2,1)S(1)} %bitcast.25, bf16[512,768]{1,0:T(8,128)(2,1)S(1)} %bitcast.36, bf16[512,768]{1,0:T(8,128)(2,1)S(1)} %bitcast.42), custom_call_target="tpu_custom_call" | custom-call | tf_op jit(solution)/shard_map/own_own/pallas_call | solution.py:230
  120.4 4.9 %own_near01.1.refs_1_ = f32[16,512]{1,0:T(8,128)S(1)} custom-call(f32[16,512]{1,0:T(8,128)S(1)} %slot_ids.1.refs_0_.refs_1_, f32[16,512]{1,0:T(8,128)S(1)} %own_own.1.refs_1_, bf16[512,768]{1,0:T(8,128)(2,1)S(1)} %bitcast.31, bf16[512,768]{1,0:T(8,128)(2,1)S(1)} %bitcast.26, bf16[512,768]{1,0:T(8,128)(2,1)S(1)} %bitcast.37, bf16[512,768]{1,0:T(8,128)(2,1)S(1)} %bitcast.43, ...), custom_call_target="tpu_custom_call" | custom-call | tf_op jit(solution)/shard_map/own_near01/pallas_call | solution.py:230
  125.4 6.8 %own_far01_near2.1.refs_1_ = f32[16,512]{1,0:T(8,128)S(1)} custom-call(f32[16,512]{1,0:T(8,128)S(1)} %slot_ids.1.refs_0_.refs_1_, f32[16,512]{1,0:T(8,128)S(1)} %own_near01.1.refs_1_, bf16[512,768]{1,0:T(8,128)(2,1)S(1)} %bitcast.32, bf16[512,768]{1,0:T(8,128)(2,1)S(1)} %bitcast.27, bf16[512,768]{1,0:T(8,128)(2,1)S(1)} %bitcast.38, ...), custom_call_target="tpu_custom_call" | custom-call | tf_op jit(solution)/shard_map/own_far01_near2/pallas_call | solution.py:230
  132.3 7.8 %last.1.refs_1_ = f32[16,512]{1,0:T(8,128)S(1)} custom-call(f32[16,512]{1,0:T(8,128)S(1)} %slot_ids.1.refs_0_.refs_1_, f32[16,512]{1,0:T(8,128)S(1)} %own_far01_near2.1.refs_1_, bf16[512,768]{1,0:T(8,128)(2,1)S(1)} %bitcast.33, bf16[512,768]{1,0:T(8,128)(2,1)S(1)} %bitcast.28, bf16[512,768]{1,0:T(8,128)(2,1)S(1)} %bitcast.39, bf16[512,768]{1,0:T(8,128)(2,1)S(1)} %bitcast.45, ...), custom_call_target="tpu_custom_call" | custom-call | tf_op jit(solution)/shard_map/last/pallas_call | solution.py:230
  140.1 1.8 %pack.1 = f32[128,64]{1,0:T(8,128)S(1)} custom-call(s32[8]{0:T(128)S(1)} %stack.35.refs_0_, f32[16,512]{1,0:T(8,128)S(1)} %last.1.refs_1_), custom_call_target="tpu_custom_call" | custom-call | tf_op jit(solution)/shard_map/pack/pallas_call | solution.py:250
  141.9 15.0 %all_to_all.44 = f32[128,1,64]{2,1,0:T(1,128)S(1)} all-to-all(f32[128,1,64]{2,1,0:T(1,128)S(1)} %bitcast.50), channel_id=1, replica_groups=mesh['docs'=32,'split'=4] {'docs','split'}, dimensions={0} | all-to-all | bytes 65536 | tf_op jit(solution)/shard_map/all_to_all | solution.py:258
  (18 shorter events, 3.0 us)
Async XLA Ops:
  0.0 1.9 %copy-start = (f32[1024,768]{1,0:T(8,128)S(1)}, f32[1024,768]{1,0:T(8,128)}, u32[]{:S(2)}) copy-start(f32[1024,768]{1,0:T(8,128)} %refs_1_.1) | copy-start | bytes 9437188
  1.9 0.7 copy-start.2
  8.3 23.6 %copy-start.1 = (bf16[512,768]{1,0:T(8,128)(2,1)}, bf16[512,768]{1,0:T(8,128)(2,1)S(1)}, u32[]{:S(2)}) copy-start(bf16[512,768]{1,0:T(8,128)(2,1)S(1)} %get-tuple-element.18) | copy-start | bytes 2359300
  49.8 18.5 %all-to-all-start.3 = ((bf16[32,16,768]{2,1,0:T(8,128)(2,1)}), bf16[32,16,768]{2,1,0:T(8,128)(2,1)S(1)}, u32[]{:S(2)}, u32[]{:S(2)}) async-start(bf16[32,16,768]{2,1,0:T(8,128)(2,1)} %bitcast.14), calls=%async_computation.3 | async-start | bytes 1572864 | tf_op jit(solution)/shard_map/all_to_all | solution.py:208
  54.0 24.6 %collective-permute-start.1 = (bf16[512,768]{1,0:T(8,128)(2,1)S(1)}, bf16[512,768]{1,0:T(8,128)(2,1)}, u32[]{:S(2)}, u32[]{:S(2)}) collective-permute-start(bf16[512,768]{1,0:T(8,128)(2,1)S(1)} %bitcast.24), channel_id=1, source_target_pairs={{0,3},{1,0},{2,1},{3,2},{6,7},{5,6},{4,5},{7,4},{8,11},{9,8},{10,9... | collective-permute-start | bytes 2359304 | tf_op jit(solution)/shard_map/ppermute | solution.py:222
  55.2 25.5 %collective-permute-start = (bf16[512,768]{1,0:T(8,128)(2,1)S(1)}, bf16[512,768]{1,0:T(8,128)(2,1)}, u32[]{:S(2)}, u32[]{:S(2)}) collective-permute-start(bf16[512,768]{1,0:T(8,128)(2,1)S(1)} %bitcast.29), channel_id=1, source_target_pairs={{0,3},{1,0},{2,1},{3,2},{6,7},{5,6},{4,5},{7,4},{8,11},{9,8},{10,9... | collective-permute-start | bytes 2359304 | tf_op jit(solution)/shard_map/ppermute | solution.py:222
  68.3 21.2 %collective-permute-start.2 = (bf16[512,768]{1,0:T(8,128)(2,1)S(1)}, bf16[512,768]{1,0:T(8,128)(2,1)}, u32[]{:S(2)}, u32[]{:S(2)}) collective-permute-start(bf16[512,768]{1,0:T(8,128)(2,1)S(1)} %bitcast.34), channel_id=1, source_target_pairs={{0,3},{1,0},{2,1},{3,2},{6,7},{5,6},{4,5},{7,4},{8,11},{9,8},{10,9... | collective-permute-start | bytes 2359304 | tf_op jit(solution)/shard_map/ppermute | solution.py:222
  69.5 20.0 %all-to-all-start.4 = ((bf16[32,16,768]{2,1,0:T(8,128)(2,1)}), bf16[32,16,768]{2,1,0:T(8,128)(2,1)S(1)}, u32[]{:S(2)}, u32[]{:S(2)}) async-start(bf16[32,16,768]{2,1,0:T(8,128)(2,1)} %bitcast.46), calls=%async_computation.4 | async-start | bytes 1572864 | tf_op jit(solution)/shard_map/all_to_all | solution.py:208
  75.2 57.1 %collective-permute-start.6 = (bf16[512,768]{1,0:T(8,128)(2,1)S(1)}, bf16[512,768]{1,0:T(8,128)(2,1)}, u32[]{:S(2)}, u32[]{:S(2)}) collective-permute-start(bf16[512,768]{1,0:T(8,128)(2,1)S(1)} %bitcast.35), channel_id=1, source_target_pairs={{2,3},{3,0},{4,7},{7,6},{10,11},{11,8},{12,15},{15,14},{18,19},{19... | collective-permute-start | bytes 2359304 | tf_op jit(solution)/shard_map/ppermute | solution.py:226
  78.5 46.8 %collective-permute-start.4 = (bf16[512,768]{1,0:T(8,128)(2,1)}, bf16[512,768]{1,0:T(8,128)(2,1)}, u32[]{:S(2)}, u32[]{:S(2)}) collective-permute-start(bf16[512,768]{1,0:T(8,128)(2,1)} %collective-permute-done.1.refs_7_), channel_id=1, source_target_pairs={{1,0},{2,1},{5,6},{4,5},{9,8},{10,9},{13,14},{12,13},{17,16},{18,1... | collective-permute-start | bytes 2359304 | tf_op jit(solution)/shard_map/ppermute | solution.py:225
  80.7 44.7 %collective-permute-start.3 = (bf16[512,768]{1,0:T(8,128)(2,1)}, bf16[512,768]{1,0:T(8,128)(2,1)}, u32[]{:S(2)}, u32[]{:S(2)}) collective-permute-start(bf16[512,768]{1,0:T(8,128)(2,1)} %collective-permute-done.refs_6_), channel_id=1, source_target_pairs={{1,0},{2,1},{5,6},{4,5},{9,8},{10,9},{13,14},{12,13},{17,16},{18,1... | collective-permute-start | bytes 2359304 | tf_op jit(solution)/shard_map/ppermute | solution.py:225
  89.5 42.7 %collective-permute-start.5 = (bf16[512,768]{1,0:T(8,128)(2,1)S(1)}, bf16[512,768]{1,0:T(8,128)(2,1)}, u32[]{:S(2)}, u32[]{:S(2)}) collective-permute-start(bf16[512,768]{1,0:T(8,128)(2,1)S(1)} %bitcast.40), channel_id=1, source_target_pairs={{0,3},{1,0},{2,1},{3,2},{6,7},{5,6},{4,5},{7,4},{8,11},{9,8},{10,9... | collective-permute-start | bytes 2359304 | tf_op jit(solution)/shard_map/ppermute | solution.py:222
  89.6 42.7 %collective-permute-start.7 = (bf16[512,768]{1,0:T(8,128)(2,1)S(1)}, bf16[512,768]{1,0:T(8,128)(2,1)}, u32[]{:S(2)}, u32[]{:S(2)}) collective-permute-start(bf16[512,768]{1,0:T(8,128)(2,1)S(1)} %bitcast.41), channel_id=1, source_target_pairs={{2,3},{3,0},{4,7},{7,6},{10,11},{11,8},{12,15},{15,14},{18,19},{19... | collective-permute-start | bytes 2359304 | tf_op jit(solution)/shard_map/ppermute | solution.py:226
  95.0 19.9 %all-to-all-start = ((f32[128,1,64]{2,1,0:T(1,128)}), f32[128,1,64]{2,1,0:T(1,128)S(1)}, u32[]{:S(2)}, u32[]{:S(2)}) async-start(f32[128,1,64]{2,1,0:T(1,128)} %bitcast.8), calls=%async_computation | async-start | bytes 131072 | tf_op jit(solution)/shard_map/all_to_all | solution.py:211

commit v2 on v0

v2 whole, which is shorter than its diff:
```python
import jax
import jax.numpy as jnp
from jax import lax
from jax.experimental import pallas as pl
from jax.experimental.pallas import tpu as pltpu
from jax.sharding import PartitionSpec as P

F32 = jnp.float32
BF16 = jnp.bfloat16
CLU_DEV = 4
EPSILON = 1e-06
SIDE = 4
PEERS = SIDE * SIDE
CAP = 64
LANES = 128
CODE_ROWS = 16
CHUNKS = ((0, 0, 64), (1, 0, 32), (1, 32, 32))
STEP = 32
ROWS = 16
OWN, NEAR, FAR = 0, 1, 2
AXES = ("docs", "split")
NT = (((1,), (1,)), ((), ()))
NN = (((1,), (0,)), ((), ()))
VMEM = pl.BlockSpec(memory_space=pltpu.VMEM)
SMEM = pl.BlockSpec(memory_space=pltpu.SMEM)
HBM = pl.BlockSpec(memory_space=pl.ANY)
PARAMS = pltpu.CompilerParams(vmem_limit_bytes=48 * 2**20)


def iota(shape, axis):
    return lax.broadcasted_iota(jnp.int32, shape, axis)


def flat(x, y, z, core):
    return ((z % SIDE * SIDE + y % SIDE) * 2 + core) * SIDE + x % SIDE


def plane_groups():
    side = range(SIDE)
    first = [[flat(x, y, z, 0) for z in side for y in side] for x in side]
    return first + [[flat(x, y, z, 1) for z in side for x in side] for y in side]


def line_moves(steps):
    side = range(SIDE)
    out = [(flat(a, u, z, 0), flat(b, u, z, 0)) for a, b in steps for u in side for z in side]
    return out + [(flat(u, a, z, 1), flat(u, b, z, 1)) for a, b in steps for u in side for z in side]


def core_moves():
    side = range(SIDE)
    return [(flat(x, y, z, c), flat(x, y, z, 1 - c)) for x in side for y in side for z in side for c in (0, 1)]


def chunk_shape(width, columns):
    return (PEERS, width * columns // LANES + CODE_ROWS, LANES)


def place(unit, kind_rng, rank, ids, chunk, out):
    kind, low, width = chunk
    docs, columns = unit.shape
    inside = (kind_rng >= kind * PEERS) & (kind_rng < (kind + 1) * PEERS) & (rank >= low) & (rank < low + width)
    row = jnp.where(inside, (kind_rng - kind * PEERS) * width + rank - low, -1)
    pick = jnp.where(iota((PEERS * width, docs), 0) == row, 1.0, 0.0).astype(BF16)
    rows = lax.dot_general(pick, unit, NN, preferred_element_type=F32).astype(BF16)
    for tile in range(columns // LANES):
        part = rows[:, tile * LANES : (tile + 1) * LANES]
        out[:, tile * width : (tile + 1) * width, :] = part.reshape(PEERS, width, LANES)
    peer = iota((PEERS * CODE_ROWS, docs), 0) // CODE_ROWS
    owner = jnp.where(inside & (kind_rng - kind * PEERS == peer), 1.0, 0.0).astype(BF16)
    code = jnp.where(iota((LANES, docs), 0) == rank - low, (ids & (CLU_DEV - 1)) + 1, 0).astype(F32).astype(BF16)
    codes = lax.dot_general(owner, code, NT, preferred_element_type=F32).astype(BF16)
    out[:, width * columns // LANES :, :] = codes.reshape(PEERS, CODE_ROWS, LANES)


def prepare(here_ref, ids_ref, emb_ref, pos_ref, unit_ref, first_ref, emb, sems):
    docs, columns = emb.shape
    parts = 4
    size = docs // parts
    copies = [
        pltpu.make_async_copy(emb_ref.at[pl.ds(p * size, size)], emb.at[pl.ds(p * size, size)], sems.at[p])
        for p in range(parts)
    ]
    for copy in copies:
        copy.start()
    ids = ids_ref[...]
    rng = ids >> 2
    key = (ids * docs + iota(ids.shape, 1)).astype(F32)
    base = (rng * (CLU_DEV * docs)).astype(F32)
    key_col = jnp.transpose(jnp.broadcast_to(key, (LANES, docs)))
    ranks = []
    for lane in range(0, docs, LANES):
        before = (key_col < key[:, lane : lane + LANES]) & (key_col >= base[:, lane : lane + LANES])
        ranks.append(jnp.sum(jnp.where(before, 1.0, 0.0), axis=0, keepdims=True))
    rank = jnp.concatenate(ranks, axis=1).astype(jnp.int32)
    kind_rng = rng ^ (here_ref[0] * PEERS)
    pos_ref[0:1, :] = rng
    pos_ref[1:2, :] = rank
    pos_ref[2:3, :] = kind_rng
    pos_ref[3:4, :] = ids
    for p in range(parts):
        copies[p].wait()
        rows = emb[p * size : (p + 1) * size, :]
        scaling = lax.rsqrt(jnp.mean(rows * rows, axis=1, keepdims=True) + EPSILON) * columns ** (-0.5)
        unit_ref[p * size : (p + 1) * size, :] = (rows * scaling).astype(BF16)
    place(unit_ref[...], kind_rng, rank, ids, CHUNKS[0], first_ref)


def place_rest(pos_ref, unit_ref, *outs):
    unit = unit_ref[...]
    rank, kind_rng, ids = pos_ref[1:2, :], pos_ref[2:3, :], pos_ref[3:4, :]
    for chunk, out in zip(CHUNKS[1:], outs):
        place(unit, kind_rng, rank, ids, chunk, out)


def lane_slot(width):
    lane = iota((1, PEERS * width), 1)
    return lane // STEP % PEERS, lane // (STEP * PEERS) * STEP + lane % STEP


def chunk_codes(ref, width):
    codes = ref[:, ref.shape[1] - CODE_ROWS :, :].astype(F32)[:, 0, :].astype(BF16)
    peer, slot = lane_slot(width)
    spread = jnp.where(iota((LANES, PEERS * width), 0) == slot, 1.0, 0.0).astype(BF16)
    wide = lax.dot_general(codes, spread, NN, preferred_element_type=F32)
    return jnp.sum(jnp.where(iota(wide.shape, 0) == peer, wide, 0.0), axis=0, keepdims=True)


def block_rows(ref, width, step):
    tiles = (ref.shape[1] - CODE_ROWS) // width
    parts = [ref[:, t * width + step * STEP : t * width + (step + 1) * STEP, :] for t in range(tiles)]
    return jnp.concatenate([p.reshape(PEERS * STEP, LANES) for p in parts], axis=1)


def scores(names, pairs, fresh, here_ref, best_in_ref, *refs):
    chunks = dict(zip(names, refs[: len(names)]))
    best_ref = refs[len(names)]
    best_ref[...] = jnp.full(best_ref.shape, -1.0, F32) if fresh else best_in_ref[...]
    size = PEERS * STEP
    width = {n: CHUNKS[n[1]][2] for n in names}
    codes = {n: chunk_codes(chunks[n], width[n]) for n in names}

    def into(name, step, values):
        row = name[0] * len(CHUNKS) + name[1]
        at = (slice(row, row + 1), slice(step * size, (step + 1) * size))
        best_ref[at] = jnp.maximum(best_ref[at], values)

    def run(some):
        for left in dict.fromkeys(p[0] for p in some):
            for i in range(width[left] // STEP):
                left_rows = block_rows(chunks[left], width[left], i)
                left_codes = codes[left][:, i * size : (i + 1) * size]
                left_codes = jnp.where(left_codes > 0, left_codes, -1.0)
                left_codes = jnp.transpose(jnp.broadcast_to(left_codes, (LANES, size)))[:, :1]
                total = None
                for right in [p[1] for p in some if p[0] == left]:
                    for j in range(width[right] // STEP):
                        if left == right and j < i:
                            continue
                        right_rows = block_rows(chunks[right], width[right], j)
                        score = lax.dot_general(left_rows, right_rows, NT, preferred_element_type=F32)
                        allowed = left_codes == codes[right][:, j * size : (j + 1) * size]
                        same = left == right and i == j
                        if same:
                            allowed = allowed & (iota((size, size), 0) != iota((size, size), 1))
                        score = jnp.where(allowed, score, -1.0)
                        into(right, j, jnp.max(score, axis=0, keepdims=True))
                        if not same:
                            for lane in range(0, size, LANES):
                                part = score[:, lane : lane + LANES]
                                total = part if total is None else jnp.maximum(total, part)
                if total is not None:
                    into(left, i, jnp.max(jnp.transpose(total), axis=0, keepdims=True))

    run([p for p in pairs if p[1][0] != FAR])
    far = [p for p in pairs if p[1][0] == FAR]
    if far:
        pl.when(here_ref[2] > 0)(lambda: run(far))


def pack(here_ref, best_ref, out_ref):
    core, spot = here_ref[0], here_ref[1]
    devices = out_ref.shape[0]
    result = jnp.zeros(out_ref.shape, F32)
    for number, (kind, low, width) in enumerate(CHUNKS):
        size = PEERS * width
        peer, slot = lane_slot(width)
        from_core = core if kind == 0 else 1 - core
        wide = jnp.zeros((devices, size), F32)
        for role, shift in ((OWN, 0), (NEAR, 1), (FAR, 3), (None, 2)):
            line = (spot + shift) % SIDE
            first = peer * (2 * SIDE) + from_core * SIDE + line
            second = peer // SIDE * (2 * PEERS) + line * (2 * SIDE) + from_core * SIDE + peer % SIDE
            source = jnp.where(core == 0, first, second)
            row = 0 if role is None else role * len(CHUNKS) + number
            values = jnp.full((1, size), -1.0, F32) if role is None else best_ref[row : row + 1, :size]
            wide = jnp.where(iota(wide.shape, 0) == source, values, wide)
        narrow = jnp.where(iota((CAP, size), 0) == slot + low, 1.0, 0.0)
        result = result + lax.dot_general(wide, narrow, NT, precision=lax.Precision.HIGHEST, preferred_element_type=F32)
    out_ref[...] = result


def finish(pos_ref, got_ref, out_ref):
    rng, rank = pos_ref[0:1, :], pos_ref[1:2, :]
    got = got_ref[...]
    devices, docs = got.shape[0], rng.shape[1]
    peer = rng % PEERS
    best = jnp.full((CAP, docs), -1.0, F32)
    for line in range(SIDE):
        first = peer * (2 * SIDE) + line
        second = peer // SIDE * (2 * PEERS) + line * (2 * SIDE) + SIDE + peer % SIDE
        source = jnp.where(rng < PEERS, first, second)
        pick = jnp.where(iota((devices, docs), 0) == source, 1.0, 0.0)
        found = lax.dot_general(
            got, pick, (((0,), (0,)), ((), ())), precision=lax.Precision.HIGHEST, preferred_element_type=F32
        )
        best = jnp.maximum(best, found)
    out_ref[...] = jnp.sum(jnp.where(iota((CAP, docs), 0) == rank, best, 0.0), axis=0, keepdims=True)


def after(x, *others):
    return lax.optimization_barrier((x, *others))[0]


def per_device(embeddings, cluster_id):
    docs, columns = embeddings.shape
    devices = lax.axis_size("docs") * lax.axis_size("split")
    at = lax.axis_index("docs")
    core = at % 2
    spot = jnp.where(core == 0, lax.axis_index("split"), at // 2 % SIDE)
    has_far = ((spot == 3) | (spot == 0)).astype(jnp.int32)
    here = jnp.stack([core, spot, has_far]).astype(jnp.int32)
    shapes = [jax.ShapeDtypeStruct(chunk_shape(c[2], columns), BF16) for c in CHUNKS]

    pos, unit, first = pl.pallas_call(
        prepare,
        in_specs=[SMEM, VMEM, HBM],
        out_specs=[VMEM] * 3,
        out_shape=[
            jax.ShapeDtypeStruct((4, docs), jnp.int32),
            jax.ShapeDtypeStruct((docs, columns), BF16),
            shapes[0],
        ],
        scratch_shapes=[pltpu.VMEM((docs, columns), F32), pltpu.SemaphoreType.DMA((4,))],
        compiler_params=PARAMS,
        name="prepare",
    )(here, cluster_id.reshape(1, docs), embeddings)
    rest = pl.pallas_call(
        place_rest,
        in_specs=[VMEM, VMEM],
        out_specs=[VMEM] * (len(CHUNKS) - 1),
        out_shape=shapes[1:],
        compiler_params=PARAMS,
        name="place_rest",
    )(pos, unit)

    groups = plane_groups()
    moves_near = line_moves([(a, a - 1) for a in range(SIDE)])
    moves_far = line_moves([(2, 3), (3, 0)])
    placed = [first] + [lax.ppermute(x, AXES, core_moves()) for x in rest]
    held = {}
    for number, x in enumerate(placed):
        if number:
            x = after(x, held[OWN, number - 1])
        own = lax.all_to_all(x, AXES, 0, 0, axis_index_groups=groups, tiled=True)
        held[OWN, number] = own
        held[NEAR, number] = lax.ppermute(own, AXES, moves_near)
        held[FAR, number] = lax.ppermute(own, AXES, moves_far)

    def score_call(best, pairs, name):
        names = sorted({n for p in pairs for n in p})
        shape = jax.ShapeDtypeStruct((ROWS, PEERS * CAP), F32)
        return pl.pallas_call(
            lambda *refs: scores(names, pairs, best is None, *refs),
            in_specs=[SMEM, VMEM] + [VMEM] * len(names),
            out_specs=VMEM,
            out_shape=shape,
            compiler_params=PARAMS,
            name=name,
        )(here, pos if best is None else best, *[held[n] for n in names])

    best = None
    for number in range(len(CHUNKS)):
        older = range(number)
        pairs = [((OWN, a), (OWN, number)) for a in older] + [((OWN, number), (OWN, number))]
        pairs += [((OWN, number), (NEAR, a)) for a in older]
        best = score_call(best, pairs, f"own_{number}")
        pairs = [((OWN, a), (NEAR, number)) for a in range(number + 1)]
        pairs += [((NEAR, a), (FAR, number)) for a in range(number + 1)]
        pairs += [((NEAR, number), (FAR, a)) for a in older]
        best = score_call(best, pairs, f"near_{number}")
    sent = pl.pallas_call(
        pack,
        in_specs=[SMEM, VMEM],
        out_specs=VMEM,
        out_shape=jax.ShapeDtypeStruct((devices, CAP), F32),
        compiler_params=PARAMS,
        name="pack",
    )(here, best)
    got = lax.all_to_all(sent, AXES, 0, 0, tiled=True)
    out = pl.pallas_call(
        finish,
        in_specs=[VMEM, VMEM],
        out_specs=VMEM,
        out_shape=jax.ShapeDtypeStruct((1, docs), F32),
        compiler_params=PARAMS,
        name="finish",
    )(pos, got)
    return out.reshape(docs)


def solution(mesh):
    return jax.shard_map(
        per_device,
        mesh=mesh,
        in_specs=(P(AXES, None), P(AXES)),
        out_specs=P(AXES),
        check_vma=False,
    )
```

time: 312 us -> 142 us (0.46)
  blocking collectives: 108 us -> 19.9 us
  matrix products: 52.6 us -> 0 us
  waiting for transfers between devices: 92.2 us -> 41.2 us
  Pallas kernels: 0 us -> 43.2 us
  starting transfers between devices: 4.7 us -> 35.1 us
  local copies, waits for them, and re-layouts: 28.8 us -> 1.68 us
  between operations: 13.5 us -> 0.18 us
  other arithmetic: 12 us -> 0.08 us
    all_gather x1 -> x0, waiting for transfers between devices: 85.3 us -> none  [per_device(): right_rows = lax.all_gather(normed, 'split', axis=0, tiled=True)]
    all_to_all x2 -> x1, blocking collectives: 97.4 us -> 19.9 us  [per_device(): got = lax.all_to_all(sent, AXES, 0, 0, tiled=True)]
    dot_general x5 -> x0, matrix products: 52.6 us -> none  [the longest x4 52 us: masked_scores(): lax.dot_general(own_rows, right_rows, (((1,), (1,)), ((), ())), preferred...]
    pallas_call x0 -> x10, Pallas kernels: none -> 43.2 us  [the longest x6 30.7 us: score_call(): pl.pallas_call(lambda *refs: scores(names, pairs, best is None, *refs), i...]
    all_to_all x1 -> x3, waiting for transfers between devices: 6.91 us -> 34.4 us  [per_device(): own = lax.all_to_all(x, AXES, 0, 0, axis_index_groups=groups, tiled=True)]
    ppermute x0 -> x8, starting transfers between devices: none -> 16.2 us  [the longest x3 11.2 us: per_device(): held[NEAR, number] = lax.ppermute(own, AXES, moves_near)]
    all_to_all x1 -> x3, starting transfers between devices: 4.7 us -> 18.9 us  [per_device(): own = lax.all_to_all(x, AXES, 0, 0, axis_index_groups=groups, tiled=True)]
    scatter x2 -> x0, local copies, waits for them, and re-layouts: 13.1 us -> none  [the longest x1 8.66 us: per_device(): jnp.zeros((slots_all, columns), jnp.float32).at[position].set(embeddings)]
  transfers between devices with their start and end apart: 2 -> 11, of which waited for: 2 -> 4; matrix products, arithmetic and copies ran while one was open for 3% -> 0% of each run, Pallas kernels for 0% -> 18%
where the time goes in v2:
time: 142 us; the launch traced here: 141 us
  Pallas kernels  43.2 us (30%)
  waiting for transfers between devices  41.2 us (29%)
  starting transfers between devices  35.1 us (25%)
  blocking collectives  19.9 us (14%)
  local copies, waits for them, and re-layouts  1.68 us (1%)
    all_to_all x3, waiting for transfers between devices, per_device(): own = lax.all_to_all(x, AXES, 0, 0, axis_index_groups=groups, tiled=True)  34.4 us
    pallas_call x6, Pallas kernels, score_call(): pl.pallas_call(lambda *refs: scores(names, pairs, best is None, *refs), i...  30.7 us
    all_to_all x1, blocking collectives, per_device(): got = lax.all_to_all(sent, AXES, 0, 0, tiled=True)  19.9 us
    all_to_all x3, starting transfers between devices, per_device(): own = lax.all_to_all(x, AXES, 0, 0, axis_index_groups=groups, tiled=True)  18.9 us
    ppermute x3, starting transfers between devices, per_device(): held[NEAR, number] = lax.ppermute(own, AXES, moves_near)  11.2 us
    ppermute x3, waiting for transfers between devices, per_device(): held[NEAR, number] = lax.ppermute(own, AXES, moves_near)  6.73 us
    pallas_call x1, Pallas kernels, per_device(): pl.pallas_call(prepare, in_specs=[SMEM, VMEM, HBM], out_specs=[VMEM] * 3,...  5.56 us
    ppermute x3, starting transfers between devices, per_device(): held[FAR, number] = lax.ppermute(own, AXES, moves_far)  3.84 us
  transfers between devices with their start and end apart: 11, of which 4 were waited for; matrix products, arithmetic and copies ran while one was open for 0% of the time, Pallas kernels for 18%

profile of v2, /device:TPU:1, one launch (start us, length us, event | category | flops | bytes accessed | tf_op | source)
XLA Modules:
  0.0 141.3 jit_solution(12569374744175642968)
XLA Ops:
  0.8 5.6 %prepare.1 = (s32[4,1024]{1,0:T(4,128)S(1)}, bf16[1024,768]{1,0:T(8,128)(2,1)S(1)}, bf16[16,400,128]{2,1,0:T(8,128)(2,1)}) custom-call(s32[3]{0:T(128)S(1)} %pad_add_fusion.here_ref.refs_0_, s32[1,1024]{1,0:T(1,128)S(1)} %bitcast.11, f32[1024,768]{1,0:T(8,128)} %emb_ref.1), custom_call_target="tpu_custom_call" | custom-call | tf_op jit(solution)/shard_map/prepare/pallas_call | solution.py:235
  6.3 8.4 %all-to-all-start = ((bf16[16,400,128]{2,1,0:T(8,128)(2,1)}), bf16[16,400,128]{2,1,0:T(8,128)(2,1)S(1)}, u32[]{:S(2)}, u32[]{:S(2)}) async-start(bf16[16,400,128]{2,1,0:T(8,128)(2,1)} %get-tuple-element.13), calls=%async_computation | async-start | bytes 3276800 | tf_op jit(solution)/shard_map/all_to_all | solution.py:265
  14.8 3.0 %place_rest.1 = (bf16[16,208,128]{2,1,0:T(8,128)(2,1)}, bf16[16,208,128]{2,1,0:T(8,128)(2,1)}) custom-call(s32[4,1024]{1,0:T(4,128)S(1)} %get-tuple-element.12.refs_1_.pos_ref, bf16[1024,768]{1,0:T(8,128)(2,1)S(1)} %get-tuple-element.14.unit_ref), custom_call_target="tpu_custom_call" | custom-call | tf_op jit(solution)/shard_map/place_rest/pallas_call | solution.py:248
  18.9 15.7 %all-to-all-done.refs_2_ = bf16[16,400,128]{2,1,0:T(8,128)(2,1)S(1)} async-done(((bf16[16,400,128]{2,1,0:T(8,128)(2,1)}), bf16[16,400,128]{2,1,0:T(8,128)(2,1)S(1)}, u32[]{:S(2)}, u32[]{:S(2)}) %all-to-all-start) | async-done | bytes 1638432 | tf_op jit(solution)/shard_map/all_to_all | solution.py:265
  34.6 1.3 collective-permute-start.1
  35.9 6.2 %all-to-all-start.1 = ((bf16[16,208,128]{2,1,0:T(8,128)(2,1)}), bf16[16,208,128]{2,1,0:T(8,128)(2,1)S(1)}, u32[]{:S(2)}, u32[]{:S(2)}) async-start(bf16[16,208,128]{2,1,0:T(8,128)(2,1)} %collective-permute-done.2), calls=%async_computation.1 | async-start | bytes 1703936 | tf_op jit(solution)/shard_map/all_to_all | solution.py:265
  42.1 15.3 %all-to-all-done.1.refs_3_ = bf16[16,208,128]{2,1,0:T(8,128)(2,1)S(1)} async-done(((bf16[16,208,128]{2,1,0:T(8,128)(2,1)}), bf16[16,208,128]{2,1,0:T(8,128)(2,1)S(1)}, u32[]{:S(2)}, u32[]{:S(2)}) %all-to-all-start.1) | async-done | bytes 852000 | tf_op jit(solution)/shard_map/all_to_all | solution.py:265
  58.4 4.3 %all-to-all-start.2 = ((bf16[16,208,128]{2,1,0:T(8,128)(2,1)}), bf16[16,208,128]{2,1,0:T(8,128)(2,1)}, u32[]{:S(2)}, u32[]{:S(2)}) async-start(bf16[16,208,128]{2,1,0:T(8,128)(2,1)} %collective-permute-done.5), calls=%async_computation.2 | async-start | bytes 1703936 | tf_op jit(solution)/shard_map/all_to_all | solution.py:265
  62.7 3.4 %collective-permute-start = (bf16[16,400,128]{2,1,0:T(8,128)(2,1)S(1)}, bf16[16,400,128]{2,1,0:T(8,128)(2,1)S(1)}, u32[]{:S(2)}, u32[]{:S(2)}) collective-permute-start(bf16[16,400,128]{2,1,0:T(8,128)(2,1)S(1)} %all-to-all-done.refs_2_), channel_id=1, source_target_pairs={{0,3},{32,35},{64,67},{96,99},{8,11},{40,43},{72,75},{104,107},{16... | collective-permute-start | bytes 4915208 | tf_op jit(solution)/shard_map/ppermute | solution.py:267
  66.1 1.3 collective-permute-start.4
  67.4 3.4 %collective-permute-start.3 = (bf16[16,208,128]{2,1,0:T(8,128)(2,1)}, bf16[16,208,128]{2,1,0:T(8,128)(2,1)}, u32[]{:S(2)}, u32[]{:S(2)}) collective-permute-start(bf16[16,208,128]{2,1,0:T(8,128)(2,1)} %copy-done.2), channel_id=1, source_target_pairs={{0,3},{32,35},{64,67},{96,99},{8,11},{40,43},{72,75},{104,107},{16... | collective-permute-start | bytes 2555912 | tf_op jit(solution)/shard_map/ppermute | solution.py:267
  70.8 3.4 %all-to-all-done.2.refs_4_ = bf16[16,208,128]{2,1,0:T(8,128)(2,1)} async-done(((bf16[16,208,128]{2,1,0:T(8,128)(2,1)}), bf16[16,208,128]{2,1,0:T(8,128)(2,1)}, u32[]{:S(2)}, u32[]{:S(2)}) %all-to-all-start.2) | async-done | bytes 852000 | tf_op jit(solution)/shard_map/all_to_all | solution.py:265
  74.1 1.3 collective-permute-start.7
  75.4 4.5 %collective-permute-start.6 = (bf16[16,208,128]{2,1,0:T(8,128)(2,1)}, bf16[16,208,128]{2,1,0:T(8,128)(2,1)S(1)}, u32[]{:S(2)}, u32[]{:S(2)}) collective-permute-start(bf16[16,208,128]{2,1,0:T(8,128)(2,1)} %all-to-all-done.2.refs_4_), channel_id=1, source_target_pairs={{0,3},{32,35},{64,67},{96,99},{8,11},{40,43},{72,75},{104,107},{16... | collective-permute-start | bytes 2555912 | tf_op jit(solution)/shard_map/ppermute | solution.py:267
  79.9 2.1 %own_0.1.refs_1_ = f32[16,1024]{1,0:T(8,128)S(1)} custom-call(s32[3]{0:T(128)S(1)} %pad_add_fusion.here_ref.refs_0_, s32[4,1024]{1,0:T(4,128)S(1)} %get-tuple-element.12.refs_1_.pos_ref, bf16[16,400,128]{2,1,0:T(8,128)(2,1)S(1)} %all-to-all-done.refs_2_), custom_call_target="tpu_custom_call" | custom-call | tf_op jit(solution)/shard_map/own_0/pallas_call | solution.py:273
  82.0 6.7 %collective-permute-done.refs_3_.refs_4_.refs_5_ = bf16[16,400,128]{2,1,0:T(8,128)(2,1)S(1)} collective-permute-done((bf16[16,400,128]{2,1,0:T(8,128)(2,1)S(1)}, bf16[16,400,128]{2,1,0:T(8,128)(2,1)S(1)}, u32[]{:S(2)}, u32[]{:S(2)}) %collective-permute-start) | collective-permute-done | bytes 1638432 | tf_op jit(solution)/shard_map/ppermute | solution.py:267
  88.7 6.2 %near_0.1.refs_1_ = f32[16,1024]{1,0:T(8,128)S(1)} custom-call(s32[3]{0:T(128)S(1)} %pad_add_fusion.here_ref.refs_0_, f32[16,1024]{1,0:T(8,128)S(1)} %own_0.1.refs_1_, bf16[16,400,128]{2,1,0:T(8,128)(2,1)S(1)} %all-to-all-done.refs_2_, bf16[16,400,128]{2,1,0:T(8,128)(2,1)S(1)} %collective-permute-done.refs_3_.refs_4_.refs_5_, ...), custom_call_target="tpu_custom_call" | custom-call | tf_op jit(solution)/shard_map/near_0/pallas_call | solution.py:273
  95.0 3.0 %own_1.1.refs_1_ = f32[16,1024]{1,0:T(8,128)S(1)} custom-call(s32[3]{0:T(128)S(1)} %pad_add_fusion.here_ref.refs_0_, f32[16,1024]{1,0:T(8,128)S(1)} %near_0.1.refs_1_, bf16[16,400,128]{2,1,0:T(8,128)(2,1)S(1)} %all-to-all-done.refs_2_, bf16[16,208,128]{2,1,0:T(8,128)(2,1)S(1)} %copy-done.3, bf16[16,400,128]{2,1,0:T(8,128)(2,1)S(1)} %collective-permute-done.refs_3_.refs_4_.refs_5_), custom_call_target="tpu_custom_call" | custom-call | tf_op jit(solution)/shard_map/own_1/pallas_call | solution.py:273
  98.0 6.0 %near_1.1.refs_1_ = f32[16,1024]{1,0:T(8,128)S(1)} custom-call(s32[3]{0:T(128)S(1)} %pad_add_fusion.here_ref.refs_0_, f32[16,1024]{1,0:T(8,128)S(1)} %own_1.1.refs_1_, bf16[16,400,128]{2,1,0:T(8,128)(2,1)S(1)} %all-to-all-done.refs_2_, bf16[16,208,128]{2,1,0:T(8,128)(2,1)S(1)} %copy-done.3, ...), custom_call_target="tpu_custom_call" | custom-call | tf_op jit(solution)/shard_map/near_1/pallas_call | solution.py:273
  104.0 4.7 %own_2.1.refs_1_ = f32[16,1024]{1,0:T(8,128)S(1)} custom-call(s32[3]{0:T(128)S(1)} %pad_add_fusion.here_ref.refs_0_, f32[16,1024]{1,0:T(8,128)S(1)} %near_1.1.refs_1_, bf16[16,400,128]{2,1,0:T(8,128)(2,1)S(1)} %all-to-all-done.refs_2_, bf16[16,208,128]{2,1,0:T(8,128)(2,1)S(1)} %copy-done.3, bf16[16,208,128]{2,1,0:T(8,128)(2,1)} %all-to-all-done.2.refs_4_, ...), custom_call_target="tpu_custom_call" | custom-call | tf_op jit(solution)/shard_map/own_2/pallas_call | solution.py:273
  108.8 8.7 %near_2.1.best_ref = f32[16,1024]{1,0:T(8,128)S(1)} custom-call(s32[3]{0:T(128)S(1)} %pad_add_fusion.here_ref.refs_0_, f32[16,1024]{1,0:T(8,128)S(1)} %own_2.1.refs_1_, bf16[16,400,128]{2,1,0:T(8,128)(2,1)} %copy-done, bf16[16,208,128]{2,1,0:T(8,128)(2,1)S(1)} %copy-done.3, bf16[16,208,128]{2,1,0:T(8,128)(2,1)} %all-to-all-done.2.refs_4_, ...), custom_call_target="tpu_custom_call" | custom-call | tf_op jit(solution)/shard_map/near_2/pallas_call | solution.py:273
  117.5 1.9 %pack.1 = f32[128,64]{1,0:T(8,128)S(1)} custom-call(s32[3]{0:T(128)S(1)} %pad_add_fusion.here_ref.refs_0_, f32[16,1024]{1,0:T(8,128)S(1)} %near_2.1.best_ref), custom_call_target="tpu_custom_call" | custom-call | tf_op jit(solution)/shard_map/pack/pallas_call | solution.py:292
  119.4 19.9 %all_to_all.26 = f32[128,1,64]{2,1,0:T(1,128)S(1)} all-to-all(f32[128,1,64]{2,1,0:T(1,128)S(1)} %bitcast.9), channel_id=1, replica_groups=mesh['docs'=32,'split'=4] {'docs','split'}, dimensions={0} | all-to-all | bytes 65536 | tf_op jit(solution)/shard_map/all_to_all | solution.py:300
  139.3 2.0 %finish.1 = f32[1,1024]{1,0:T(1,128)} custom-call(s32[4,1024]{1,0:T(4,128)S(1)} %get-tuple-element.12.refs_1_.pos_ref, f32[128,64]{1,0:T(8,128)S(1)} %bitcast.10), custom_call_target="tpu_custom_call" | custom-call | tf_op jit(solution)/shard_map/finish/pallas_call | solution.py:301
  (20 shorter events, 2.9 us)
Async XLA Ops:
  0.1 0.7 copy-start.4
  6.3 28.3 %all-to-all-start = ((bf16[16,400,128]{2,1,0:T(8,128)(2,1)}), bf16[16,400,128]{2,1,0:T(8,128)(2,1)S(1)}, u32[]{:S(2)}, u32[]{:S(2)}) async-start(bf16[16,400,128]{2,1,0:T(8,128)(2,1)} %get-tuple-element.13), calls=%async_computation | async-start | bytes 3276800 | tf_op jit(solution)/shard_map/all_to_all | solution.py:265
  17.8 18.1 %collective-permute-start.2 = (bf16[16,208,128]{2,1,0:T(8,128)(2,1)}, bf16[16,208,128]{2,1,0:T(8,128)(2,1)}, u32[]{:S(2)}, u32[]{:S(2)}) collective-permute-start(bf16[16,208,128]{2,1,0:T(8,128)(2,1)} %get-tuple-element.15), channel_id=1, source_target_pairs={{0,4},{4,0},{32,36},{36,32},{64,68},{68,64},{96,100},{100,96},{8,1... | collective-permute-start | bytes 2555912 | tf_op jit(solution)/shard_map/ppermute | solution.py:260
  18.9 23.2 %collective-permute-start.5 = (bf16[16,208,128]{2,1,0:T(8,128)(2,1)}, bf16[16,208,128]{2,1,0:T(8,128)(2,1)}, u32[]{:S(2)}, u32[]{:S(2)}) collective-permute-start(bf16[16,208,128]{2,1,0:T(8,128)(2,1)} %get-tuple-element.17), channel_id=1, source_target_pairs={{0,4},{4,0},{32,36},{36,32},{64,68},{68,64},{96,100},{100,96},{8,1... | collective-permute-start | bytes 2555912 | tf_op jit(solution)/shard_map/ppermute | solution.py:260
  34.6 69.4 %copy-start = (bf16[16,400,128]{2,1,0:T(8,128)(2,1)}, bf16[16,400,128]{2,1,0:T(8,128)(2,1)S(1)}, u32[]{:S(2)}) copy-start(bf16[16,400,128]{2,1,0:T(8,128)(2,1)S(1)} %all-to-all-done.refs_2_) | copy-start | bytes 4915204
  34.6 40.8 %collective-permute-start.1 = (bf16[16,400,128]{2,1,0:T(8,128)(2,1)S(1)}, bf16[16,400,128]{2,1,0:T(8,128)(2,1)}, u32[]{:S(2)}, u32[]{:S(2)}) collective-permute-start(bf16[16,400,128]{2,1,0:T(8,128)(2,1)S(1)} %all-to-all-done.refs_2_), channel_id=1, source_target_pairs={{2,3},{34,35},{66,67},{98,99},{10,11},{42,43},{74,75},{106,107},{1... | collective-permute-start | bytes 4915208 | tf_op jit(solution)/shard_map/ppermute | solution.py:268
  35.9 21.5 %all-to-all-start.1 = ((bf16[16,208,128]{2,1,0:T(8,128)(2,1)}), bf16[16,208,128]{2,1,0:T(8,128)(2,1)S(1)}, u32[]{:S(2)}, u32[]{:S(2)}) async-start(bf16[16,208,128]{2,1,0:T(8,128)(2,1)} %collective-permute-done.2), calls=%async_computation.1 | async-start | bytes 1703936 | tf_op jit(solution)/shard_map/all_to_all | solution.py:265
  57.5 1.0 copy-start.2
  58.4 15.7 %all-to-all-start.2 = ((bf16[16,208,128]{2,1,0:T(8,128)(2,1)}), bf16[16,208,128]{2,1,0:T(8,128)(2,1)}, u32[]{:S(2)}, u32[]{:S(2)}) async-start(bf16[16,208,128]{2,1,0:T(8,128)(2,1)} %collective-permute-done.5), calls=%async_computation.2 | async-start | bytes 1703936 | tf_op jit(solution)/shard_map/all_to_all | solution.py:265
  62.7 26.0 %collective-permute-start = (bf16[16,400,128]{2,1,0:T(8,128)(2,1)S(1)}, bf16[16,400,128]{2,1,0:T(8,128)(2,1)S(1)}, u32[]{:S(2)}, u32[]{:S(2)}) collective-permute-start(bf16[16,400,128]{2,1,0:T(8,128)(2,1)S(1)} %all-to-all-done.refs_2_), channel_id=1, source_target_pairs={{0,3},{32,35},{64,67},{96,99},{8,11},{40,43},{72,75},{104,107},{16... | collective-permute-start | bytes 4915208 | tf_op jit(solution)/shard_map/ppermute | solution.py:267
  66.1 31.9 %collective-permute-start.4 = (bf16[16,208,128]{2,1,0:T(8,128)(2,1)}, bf16[16,208,128]{2,1,0:T(8,128)(2,1)}, u32[]{:S(2)}, u32[]{:S(2)}) collective-permute-start(bf16[16,208,128]{2,1,0:T(8,128)(2,1)} %copy-done.2), channel_id=1, source_target_pairs={{2,3},{34,35},{66,67},{98,99},{10,11},{42,43},{74,75},{106,107},{1... | collective-permute-start | bytes 2555912 | tf_op jit(solution)/shard_map/ppermute | solution.py:268
  67.4 30.6 %collective-permute-start.3 = (bf16[16,208,128]{2,1,0:T(8,128)(2,1)}, bf16[16,208,128]{2,1,0:T(8,128)(2,1)}, u32[]{:S(2)}, u32[]{:S(2)}) collective-permute-start(bf16[16,208,128]{2,1,0:T(8,128)(2,1)} %copy-done.2), channel_id=1, source_target_pairs={{0,3},{32,35},{64,67},{96,99},{8,11},{40,43},{72,75},{104,107},{16... | collective-permute-start | bytes 2555912 | tf_op jit(solution)/shard_map/ppermute | solution.py:267
  74.1 34.6 %collective-permute-start.7 = (bf16[16,208,128]{2,1,0:T(8,128)(2,1)}, bf16[16,208,128]{2,1,0:T(8,128)(2,1)S(1)}, u32[]{:S(2)}, u32[]{:S(2)}) collective-permute-start(bf16[16,208,128]{2,1,0:T(8,128)(2,1)} %all-to-all-done.2.refs_4_), channel_id=1, source_target_pairs={{2,3},{34,35},{66,67},{98,99},{10,11},{42,43},{74,75},{106,107},{1... | collective-permute-start | bytes 2555912 | tf_op jit(solution)/shard_map/ppermute | solution.py:268
  75.4 33.4 %collective-permute-start.6 = (bf16[16,208,128]{2,1,0:T(8,128)(2,1)}, bf16[16,208,128]{2,1,0:T(8,128)(2,1)S(1)}, u32[]{:S(2)}, u32[]{:S(2)}) collective-permute-start(bf16[16,208,128]{2,1,0:T(8,128)(2,1)} %all-to-all-done.2.refs_4_), channel_id=1, source_target_pairs={{0,3},{32,35},{64,67},{96,99},{8,11},{40,43},{72,75},{104,107},{16... | collective-permute-start | bytes 2555912 | tf_op jit(solution)/shard_map/ppermute | solution.py:267
  82.0 13.0 %copy-start.3 = (bf16[16,208,128]{2,1,0:T(8,128)(2,1)S(1)}, bf16[16,208,128]{2,1,0:T(8,128)(2,1)}, u32[]{:S(2)}) copy-start(bf16[16,208,128]{2,1,0:T(8,128)(2,1)} %copy-done.2) | copy-start | bytes 2555908
  88.7 15.3 %copy-start.1 = (bf16[16,400,128]{2,1,0:T(8,128)(2,1)}, bf16[16,400,128]{2,1,0:T(8,128)(2,1)S(1)}, u32[]{:S(2)}) copy-start(bf16[16,400,128]{2,1,0:T(8,128)(2,1)S(1)} %collective-permute-done.refs_3_.refs_4_.refs_5_) | copy-start | bytes 4915204

commit v3 on v0

v3 whole, which is shorter than its diff:
```python
import functools

import jax
import jax.numpy as jnp
from jax import lax
from jax.experimental import pallas as pl
from jax.experimental.pallas import tpu as pltpu
from jax.sharding import PartitionSpec as P

F32 = jnp.float32
BF16 = jnp.bfloat16
CLU_DEV = 4
EPSILON = 1e-06
SIDE = 4
PEERS = SIDE * SIDE
CAP = 64
LANES = 128
CODE_ROWS = 16
HALF = PEERS // 2
BLOCK = HALF * CAP
ROWS = 8
CHUNKS = ((0, 0, 64), (1, 0, 48), (1, 48, 16))
BLOCKS = (((0, 32), (32, 32)), ((0, 32), (32, 16)), ((0, 16),))
OWN, NEAR, FAR = 0, 1, 2
LIGHT, HEAVY, ALWAYS = 0, 1, 2
AXES = ("docs", "split")
NT = (((1,), (1,)), ((), ()))
NN = (((1,), (0,)), ((), ()))
VMEM = pl.BlockSpec(memory_space=pltpu.VMEM)
SMEM = pl.BlockSpec(memory_space=pltpu.SMEM)
HBM = pl.BlockSpec(memory_space=pltpu.HBM)
PARAMS = pltpu.CompilerParams(vmem_limit_bytes=32 * 2**20)
SCORE_PARAMS = pltpu.CompilerParams(vmem_limit_bytes=28 * 2**20)


def iota(shape, axis):
    return lax.broadcasted_iota(jnp.int32, shape, axis)


def flat(x, y, z, core):
    return ((z % SIDE * SIDE + y % SIDE) * 2 + core) * SIDE + x % SIDE


def plane_groups():
    side = range(SIDE)
    first = [[flat(x, y, z, 0) for z in side for y in side] for x in side]
    return first + [[flat(x, y, z, 1) for z in side for x in side] for y in side]


def line_moves(steps):
    side = range(SIDE)
    out = [(flat(a, u, z, 0), flat(b, u, z, 0)) for a, b in steps for u in side for z in side]
    return out + [(flat(u, a, z, 1), flat(u, b, z, 1)) for a, b in steps for u in side for z in side]


def core_moves():
    side = range(SIDE)
    return [(flat(x, y, z, c), flat(x, y, z, 1 - c)) for x in side for y in side for z in side for c in (0, 1)]


def place(unit, kind_rng, rank, ids, kind, out):
    docs, columns = unit.shape
    owner = kind_rng - kind * PEERS
    inside = (owner >= 0) & (owner < PEERS) & (rank < CAP)
    row = jnp.where(inside, owner * CAP + rank, -1)
    pick = jnp.where(iota((PEERS * CAP, docs), 0) == row, 1.0, 0.0).astype(BF16)
    rows = lax.dot_general(pick, unit, NN, preferred_element_type=F32).astype(BF16)
    for tile in range(columns // LANES):
        part = rows[:, tile * LANES : (tile + 1) * LANES]
        out[:, tile * CAP : (tile + 1) * CAP, :] = part.reshape(PEERS, CAP, LANES)
    code_peer = iota((PEERS * CODE_ROWS, docs), 0) // CODE_ROWS
    owned = jnp.where(owner == code_peer, 1.0, 0.0).astype(BF16)
    code = jnp.where(iota((LANES, docs), 0) == rank, (ids & (CLU_DEV - 1)) + 1, 0).astype(F32).astype(BF16)
    codes = lax.dot_general(owned, code, NT, preferred_element_type=F32).astype(BF16)
    out[:, CAP * columns // LANES :, :] = codes.reshape(PEERS, CODE_ROWS, LANES)


def prepare(here_ref, ids_ref, emb_ref, pos_ref, first_ref, other_ref, emb, unit, sems):
    docs, columns = emb.shape
    parts = 4
    size = docs // parts
    copies = [
        pltpu.make_async_copy(emb_ref.at[pl.ds(p * size, size)], emb.at[pl.ds(p * size, size)], sems.at[p])
        for p in range(parts)
    ]
    for copy in copies:
        copy.start()
    ids = ids_ref[...]
    rng = ids >> 2
    key = (ids * docs + iota(ids.shape, 1)).astype(F32)
    base = (rng * (CLU_DEV * docs)).astype(F32)
    key_col = jnp.transpose(jnp.broadcast_to(key, (LANES, docs)))
    ranks = []
    for lane in range(0, docs, LANES):
        before = (key_col < key[:, lane : lane + LANES]) & (key_col >= base[:, lane : lane + LANES])
        ranks.append(jnp.sum(jnp.where(before, 1.0, 0.0), axis=0, keepdims=True))
    rank = jnp.concatenate(ranks, axis=1).astype(jnp.int32)
    pos_ref[0:1, :] = rng
    pos_ref[1:2, :] = rank
    for p in range(parts):
        copies[p].wait()
        rows = emb[p * size : (p + 1) * size, :]
        scaling = lax.rsqrt(jnp.mean(rows * rows, axis=1, keepdims=True) + EPSILON) * columns ** (-0.5)
        unit[p * size : (p + 1) * size, :] = (rows * scaling).astype(BF16)
    kind_rng = rng ^ (here_ref[0] * PEERS)
    for kind, out in enumerate((first_ref, other_ref)):
        place(unit[...], kind_rng, rank, ids, kind, out)


def slot_codes(ref):
    codes = ref[:, ref.shape[1] - CODE_ROWS :, :].astype(F32)[:, 0, :].astype(BF16)
    lane = iota((1, ref.shape[0] * CAP), 1)
    spread = jnp.where(iota((LANES, lane.shape[1]), 0) == lane % CAP, 1.0, 0.0).astype(BF16)
    wide = lax.dot_general(codes, spread, NN, preferred_element_type=F32)
    return jnp.sum(jnp.where(iota(wide.shape, 0) == lane // CAP, wide, 0.0), axis=0, keepdims=True)


def block_rows(ref, half):
    tiles = (ref.shape[1] - CODE_ROWS) // CAP
    peers = slice(half * HALF, (half + 1) * HALF)
    parts = [ref[peers, t * CAP : (t + 1) * CAP, :].reshape(BLOCK, LANES) for t in range(tiles)]
    return jnp.concatenate(parts, axis=1)


def scores(names, new, pairs, fresh, here_ref, best_in_ref, codes_in_ref, *refs):
    arrays = dict(zip(names, refs[: len(names)]))
    best_ref, codes_ref = refs[len(names) : len(names) + 2]
    if fresh:
        best_ref[...] = jnp.full(best_ref.shape, -1.0, F32)
        codes_ref[...] = jnp.zeros(codes_ref.shape, F32)
    else:
        best_ref[...] = best_in_ref[...]
        codes_ref[...] = codes_in_ref[...]

    def at(block):
        row = block[0] * 2 + block[1]
        return slice(row, row + 1), slice(block[2] * BLOCK, (block[2] + 1) * BLOCK)

    def rows_of(block):
        if block in arrays:
            return block_rows(arrays[block], 0)
        return block_rows(arrays[block[0], block[1], 0], block[2])

    for name in new:
        codes = slot_codes(arrays[name])
        start = name[2] * BLOCK
        codes_ref[at(name)[0], start : start + codes.shape[1]] = codes

    def into(block, values):
        best_ref[at(block)] = jnp.maximum(best_ref[at(block)], values)

    def run(some):
        for left in dict.fromkeys(p[0] for p in some):
            left_rows = rows_of(left)
            left_codes = codes_ref[at(left)]
            left_codes = jnp.where(left_codes > 0, left_codes, -1.0)
            left_codes = jnp.transpose(jnp.broadcast_to(left_codes, (LANES, BLOCK)))[:, :1]
            total = None
            for right in [p[1] for p in some if p[0] == left]:
                score = lax.dot_general(left_rows, rows_of(right), NT, preferred_element_type=F32)
                allowed = left_codes == codes_ref[at(right)]
                if left == right:
                    allowed = allowed & (iota(score.shape, 0) != iota(score.shape, 1))
                score = jnp.where(allowed, score, -1.0)
                into(right, jnp.max(score, axis=0, keepdims=True))
                if left != right:
                    for lane in range(0, BLOCK, LANES):
                        part = score[:, lane : lane + LANES]
                        total = part if total is None else jnp.maximum(total, part)
            if total is not None:
                into(left, jnp.max(jnp.transpose(total), axis=0, keepdims=True))

    run([p[:2] for p in pairs if p[2] == ALWAYS])
    for when in (HEAVY, LIGHT):
        some = [p[:2] for p in pairs if p[2] == when]
        if some:
            pl.when(here_ref[2] == when)(functools.partial(run, some))
    if len(refs) > len(names) + 2:
        pack(here_ref, best_ref, refs[-1])


def pack(here_ref, best_ref, out_ref):
    core, spot = here_ref[0], here_ref[1]
    out_ref[...] = jnp.full(out_ref.shape, -1.0, F32)
    for kind in range(2):
        from_core = core if kind == 0 else 1 - core
        for role, shift in ((OWN, 0), (NEAR, 1), (FAR, 3)):
            line = (spot + shift) % SIDE
            row = role * 2 + kind
            for peer in range(PEERS):
                first = peer * (2 * SIDE) + from_core * SIDE + line
                second = peer // SIDE * (2 * PEERS) + line * (2 * SIDE) + from_core * SIDE + peer % SIDE
                device = jnp.where(core == 0, first, second)
                out_ref[pl.ds(device, 1), :] = best_ref[row : row + 1, peer * CAP : (peer + 1) * CAP]


def finish(pos_ref, got_ref, out_ref):
    rng, rank = pos_ref[0:1, :], pos_ref[1:2, :]
    docs = rng.shape[1]
    first = got_ref[pl.ds(0, PEERS, stride=2 * SIDE), :]
    for line in range(1, SIDE):
        first = jnp.maximum(first, got_ref[pl.ds(line, PEERS, stride=2 * SIDE), :])
    second = []
    for z in range(SIDE):
        rows = [got_ref[pl.ds(z * 2 * PEERS + line * 2 * SIDE + SIDE, SIDE), :] for line in range(SIDE)]
        second.append(functools.reduce(jnp.maximum, rows))
    best = jnp.concatenate([first] + second, axis=0)
    pick = jnp.where(iota((best.shape[0], docs), 0) == rng, 1.0, 0.0)
    found = lax.dot_general(
        best, pick, (((0,), (0,)), ((), ())), precision=lax.Precision.HIGHEST, preferred_element_type=F32
    )
    out_ref[...] = jnp.sum(jnp.where(iota((CAP, docs), 0) == rank, found, 0.0), axis=0, keepdims=True)


def after(x, *others):
    return lax.optimization_barrier((x, *others))[0]


def per_device(embeddings, cluster_id):
    docs, columns = embeddings.shape
    devices = lax.axis_size("docs") * lax.axis_size("split")
    at = lax.axis_index("docs")
    core = at % 2
    spot = jnp.where(core == 0, lax.axis_index("split"), at // 2 % SIDE)
    heavy = ((spot == 3) | (spot == 0)).astype(jnp.int32)
    here = jnp.stack([core, spot, heavy]).astype(jnp.int32)
    slots = jax.ShapeDtypeStruct((PEERS, CAP * columns // LANES + CODE_ROWS, LANES), BF16)

    pos, first, other = pl.pallas_call(
        prepare,
        in_specs=[SMEM, VMEM, HBM],
        out_specs=[VMEM] * 3,
        out_shape=[jax.ShapeDtypeStruct((2, docs), jnp.int32), slots, slots],
        scratch_shapes=[
            pltpu.VMEM((docs, columns), F32),
            pltpu.VMEM((docs, columns), BF16),
            pltpu.SemaphoreType.DMA((4,)),
        ],
        compiler_params=pltpu.CompilerParams(vmem_limit_bytes=56 * 2**20),
        name="prepare",
    )(here, cluster_id.reshape(1, docs), embeddings)

    groups = plane_groups()
    moves_near = line_moves([(a, a - 1) for a in range(SIDE)])
    moves_far = line_moves([(a, a + 1) for a in range(SIDE)])

    def to_owner(x):
        return lax.all_to_all(x, AXES, 0, 0, axis_index_groups=groups, tiled=True)

    held = {}

    def score_call(state, new, pairs, name, extra=()):
        names = sorted({n if n in held else (n[0], n[1], 0) for p in pairs for n in p[:2]})
        table = jax.ShapeDtypeStruct((ROWS, PEERS * CAP), F32)
        return pl.pallas_call(
            lambda *refs: scores(names, new, pairs, state[0] is pos, *refs),
            in_specs=[SMEM, VMEM, VMEM] + [VMEM] * len(names),
            out_specs=[VMEM] * (2 + len(extra)),
            out_shape=[table, table, *extra],
            compiler_params=SCORE_PARAMS,
            name=name,
        )(here, *state[:2], *[held[n] for n in names])

    def blocks(role, kind):
        return [(role, kind, half) for half in range(2)]

    def every(lefts, rights, when=ALWAYS):
        return [(a, b, when) for a in lefts for b in rights if a[:2] != b[:2] or a <= b]

    own_0, own_1, near_0, far_0 = blocks(OWN, 0), blocks(OWN, 1), blocks(NEAR, 0), blocks(FAR, 0)
    (near_a, near_b), (far_a, far_b) = blocks(NEAR, 1), blocks(FAR, 1)
    own = to_owner(first)
    held[own_0[0]] = own
    held[near_0[0]] = lax.ppermute(own, AXES, moves_near)
    held[far_0[0]] = lax.ppermute(own, AXES, moves_far)
    state = score_call(
        (pos, pos),
        (own_0[0], near_0[0], far_0[0]),
        every(own_0, own_0 + near_0) + every(near_0, far_0, LIGHT),
        "scores_first",
    )
    own = to_owner(lax.ppermute(other, AXES, core_moves()))
    held[own_1[0]] = own

    for near, far, peers in ((near_a, far_a, slice(0, HALF)), (near_b, far_b, slice(HALF, PEERS))):
        held[near] = lax.ppermute(own[peers], AXES, moves_near)
        held[far] = lax.ppermute(own[peers], AXES, moves_far)
    state = score_call(
        state,
        (own_1[0],),
        every(own_0, own_1) + every(own_1, own_1 + near_0),
        "scores_own",
    )
    state = score_call(
        state,
        (near_a, far_a),
        every(own_0 + own_1, [near_a]) + every([near_a], far_0) + every([near_a], [far_a], HEAVY),
        "scores_near_a",
    )
    state = score_call(
        state,
        (near_b, far_b),
        every(own_0 + own_1, [near_b])
        + every([near_b], far_0)
        + every([near_b], [far_a, far_b], HEAVY)
        + every([near_a], [far_b], HEAVY),
        "scores_near_b",
        (jax.ShapeDtypeStruct((devices, CAP), F32),),
    )
    got = lax.all_to_all(state[2], AXES, 0, 0, tiled=True)
    out = pl.pallas_call(
        finish,
        in_specs=[VMEM, VMEM],
        out_specs=VMEM,
        out_shape=jax.ShapeDtypeStruct((1, docs), F32),
        compiler_params=PARAMS,
        name="finish",
    )(pos, got)
    return out.reshape(docs)


def solution(mesh):
    return jax.shard_map(
        per_device,
        mesh=mesh,
        in_specs=(P(AXES, None), P(AXES)),
        out_specs=P(AXES),
        check_vma=False,
    )
```

time: 312 us -> 118 us (0.38)
  waiting for transfers between devices: 92.2 us -> 22.5 us
  blocking collectives: 108 us -> 44.8 us
  matrix products: 52.6 us -> 0 us
  Pallas kernels: 0 us -> 31.7 us
  local copies, waits for them, and re-layouts: 28.8 us -> 0.11 us
  between operations: 13.5 us -> 0.09 us
  starting transfers between devices: 4.7 us -> 17.8 us
  other arithmetic: 12 us -> 0.64 us
    all_gather x1 -> x0, waiting for transfers between devices: 85.3 us -> none  [per_device(): right_rows = lax.all_gather(normed, 'split', axis=0, tiled=True)]
    all_to_all x2, blocking collectives: 97.4 us -> 44.8 us  [the longest x1 28.8 us: to_owner(): return lax.all_to_all(x, AXES, 0, 0, axis_index_groups=groups, tiled=True)]
    dot_general x5 -> x0, matrix products: 52.6 us -> none  [the longest x4 52 us: masked_scores(): lax.dot_general(own_rows, right_rows, (((1,), (1,)), ((), ())), preferred...]
    pallas_call x0 -> x6, Pallas kernels: none -> 31.7 us  [the longest x4 23.2 us: score_call(): pl.pallas_call(lambda *refs: scores(names, new, pairs, state[0] is pos, *...]
    scatter x2 -> x0, local copies, waits for them, and re-layouts: 13.1 us -> none  [the longest x1 8.66 us: per_device(): jnp.zeros((slots_all, columns), jnp.float32).at[position].set(embeddings)]
    ppermute x0 -> x7, starting transfers between devices: none -> 12.3 us  [the longest x2 5.11 us: per_device(): held[near] = lax.ppermute(own[peers], AXES, moves_near)]
    gather x1 -> x0, local copies, waits for them, and re-layouts: 10.5 us -> none  [per_device(): return returned.reshape(slots_all)[position]]
    all_gather x1 -> x0, blocking collectives: 10.5 us -> none  [per_device(): right_ids = lax.all_gather(got_ids, 'split', axis=0, tiled=True)]
  transfers between devices with their start and end apart: 2 -> 8, of which waited for: 2 -> 2; matrix products, arithmetic and copies ran while one was open for 3% -> 0% of each run, Pallas kernels for 0% -> 14%
where the time goes in v3:
time: 118 us
  blocking collectives  44.8 us (38%)
  Pallas kernels  31.7 us (27%)
  waiting for transfers between devices  22.5 us (19%)
  starting transfers between devices  17.8 us (15%)
    all_to_all x1, blocking collectives, to_owner(): return lax.all_to_all(x, AXES, 0, 0, axis_index_groups=groups, tiled=True)  28.8 us
    pallas_call x4, Pallas kernels, score_call(): pl.pallas_call(lambda *refs: scores(names, new, pairs, state[0] is pos, *...  23.2 us
    all_to_all x1, waiting for transfers between devices, to_owner(): return lax.all_to_all(x, AXES, 0, 0, axis_index_groups=groups, tiled=True)  16.9 us
    all_to_all x1, blocking collectives, per_device(): got = lax.all_to_all(state[2], AXES, 0, 0, tiled=True)  15.9 us
    pallas_call x1, Pallas kernels, per_device(): pl.pallas_call(prepare, in_specs=[SMEM, VMEM, HBM], out_specs=[VMEM] * 3,...  7.48 us
    ppermute x1, waiting for transfers between devices, per_device(): held[far_0[0]] = lax.ppermute(own, AXES, moves_far)  5.59 us
    all_to_all x1, starting transfers between devices, to_owner(): return lax.all_to_all(x, AXES, 0, 0, axis_index_groups=groups, tiled=True)  5.53 us
    ppermute x2, starting transfers between devices, per_device(): held[near] = lax.ppermute(own[peers], AXES, moves_near)  5.11 us
  transfers between devices with their start and end apart: 8, of which 2 were waited for; matrix products, arithmetic and copies ran while one was open for 0% of the time, Pallas kernels for 14%

profile of v3, /device:TPU:1, one launch (start us, length us, event | category | flops | bytes accessed | tf_op | source)
XLA Modules:
  0.0 117.6 jit_solution(7873189455842026330)
XLA Ops:
  0.0 0.6 pad_add_fusion.here_ref.refs_0_
  0.6 7.5 %prepare.1 = (s32[2,1024]{1,0:T(2,128)}, bf16[16,400,128]{2,1,0:T(8,128)(2,1)}, bf16[16,400,128]{2,1,0:T(8,128)(2,1)}) custom-call(s32[3]{0:T(128)} %pad_add_fusion.here_ref.refs_0_, s32[1,1024]{1,0:T(1,128)} %bitcast.11, f32[1024,768]{1,0:T(8,128)} %emb_ref.1), custom_call_target="tpu_custom_call" | custom-call | tf_op jit(solution)/shard_map/prepare/pallas_call | solution.py:229
  8.1 1.5 %collective-permute-start.2 = (bf16[16,400,128]{2,1,0:T(8,128)(2,1)}, bf16[16,400,128]{2,1,0:T(8,128)(2,1)}, u32[]{:S(2)}, u32[]{:S(2)}) collective-permute-start(bf16[16,400,128]{2,1,0:T(8,128)(2,1)} %get-tuple-element.19), channel_id=1, source_target_pairs={{0,4},{4,0},{32,36},{36,32},{64,68},{68,64},{96,100},{100,96},{8,1... | collective-permute-start | bytes 4915208 | tf_op jit(solution)/shard_map/ppermute | solution.py:282
  9.6 28.8 %all_to_all.21.refs_3_ = bf16[16,400,128]{2,1,0:T(8,128)(2,1)S(1)} all-to-all(bf16[16,400,128]{2,1,0:T(8,128)(2,1)} %get-tuple-element.16), channel_id=1, replica_groups={{0,8,16,24,32,40,48,56,64,72,80,88,96,104,112,120},{1,9,17,25,33,41,49,..., dimensions={0} | all-to-all | bytes 3276800 | tf_op jit(solution)/shard_map/all_to_all | solution.py:248
  38.5 5.5 %all-to-all-start.1 = ((bf16[16,400,128]{2,1,0:T(8,128)(2,1)}), bf16[16,400,128]{2,1,0:T(8,128)(2,1)S(1)}, u32[]{:S(2)}, u32[]{:S(2)}) async-start(bf16[16,400,128]{2,1,0:T(8,128)(2,1)} %collective-permute-done.2), calls=%async_computation.1 | async-start | bytes 3276800 | tf_op jit(solution)/shard_map/all_to_all | solution.py:248
  44.0 1.8 %collective-permute-start.1 = (bf16[16,400,128]{2,1,0:T(8,128)(2,1)S(1)}, bf16[16,400,128]{2,1,0:T(8,128)(2,1)}, u32[]{:S(2)}, u32[]{:S(2)}) collective-permute-start(bf16[16,400,128]{2,1,0:T(8,128)(2,1)S(1)} %all_to_all.21.refs_3_), channel_id=1, source_target_pairs={{0,1},{32,33},{64,65},{96,97},{8,9},{40,41},{72,73},{104,105},{16,... | collective-permute-start | bytes 4915208 | tf_op jit(solution)/shard_map/ppermute | solution.py:275
  45.8 1.7 %collective-permute-start = (bf16[16,400,128]{2,1,0:T(8,128)(2,1)S(1)}, bf16[16,400,128]{2,1,0:T(8,128)(2,1)}, u32[]{:S(2)}, u32[]{:S(2)}) collective-permute-start(bf16[16,400,128]{2,1,0:T(8,128)(2,1)S(1)} %all_to_all.21.refs_3_), channel_id=1, source_target_pairs={{0,3},{32,35},{64,67},{96,99},{8,11},{40,43},{72,75},{104,107},{16... | collective-permute-start | bytes 4915208 | tf_op jit(solution)/shard_map/ppermute | solution.py:274
  47.5 16.9 %all-to-all-done.1.refs_4_ = bf16[16,400,128]{2,1,0:T(8,128)(2,1)S(1)} async-done(((bf16[16,400,128]{2,1,0:T(8,128)(2,1)}), bf16[16,400,128]{2,1,0:T(8,128)(2,1)S(1)}, u32[]{:S(2)}, u32[]{:S(2)}) %all-to-all-start.1) | async-done | bytes 1638432 | tf_op jit(solution)/shard_map/all_to_all | solution.py:248
  64.4 0.1 fusion
  64.5 2.1 %collective-permute-start.4 = (bf16[8,400,128]{2,1,0:T(8,128)(2,1)S(1)}, bf16[8,400,128]{2,1,0:T(8,128)(2,1)S(1)}, u32[]{:S(2)}, u32[]{:S(2)}) collective-permute-start(bf16[8,400,128]{2,1,0:T(8,128)(2,1)S(1)} %get-tuple-element.26), channel_id=1, source_target_pairs={{0,1},{32,33},{64,65},{96,97},{8,9},{40,41},{72,73},{104,105},{16,... | collective-permute-start | bytes 2457608 | tf_op jit(solution)/shard_map/ppermute | solution.py:287
  66.6 2.6 %collective-permute-start.3 = (bf16[8,400,128]{2,1,0:T(8,128)(2,1)S(1)}, bf16[8,400,128]{2,1,0:T(8,128)(2,1)S(1)}, u32[]{:S(2)}, u32[]{:S(2)}) collective-permute-start(bf16[8,400,128]{2,1,0:T(8,128)(2,1)S(1)} %get-tuple-element.26), channel_id=1, source_target_pairs={{0,3},{32,35},{64,67},{96,99},{8,11},{40,43},{72,75},{104,107},{16... | collective-permute-start | bytes 2457608 | tf_op jit(solution)/shard_map/ppermute | solution.py:286
  69.2 0.0 collective-permute-start.6
  69.2 5.6 %collective-permute-done.1.refs_5_.refs_6_.refs_7_ = bf16[16,400,128]{2,1,0:T(8,128)(2,1)} collective-permute-done((bf16[16,400,128]{2,1,0:T(8,128)(2,1)S(1)}, bf16[16,400,128]{2,1,0:T(8,128)(2,1)}, u32[]{:S(2)}, u32[]{:S(2)}) %collective-permute-start.1) | collective-permute-done | bytes 1638432 | tf_op jit(solution)/shard_map/ppermute | solution.py:275
  74.8 2.5 %collective-permute-start.5 = (bf16[8,400,128]{2,1,0:T(8,128)(2,1)S(1)}, bf16[8,400,128]{2,1,0:T(8,128)(2,1)S(1)}, u32[]{:S(2)}, u32[]{:S(2)}) collective-permute-start(bf16[8,400,128]{2,1,0:T(8,128)(2,1)S(1)} %get-tuple-element.25), channel_id=1, source_target_pairs={{0,3},{32,35},{64,67},{96,99},{8,11},{40,43},{72,75},{104,107},{16... | collective-permute-start | bytes 2457608 | tf_op jit(solution)/shard_map/ppermute | solution.py:286
  77.3 0.0 collective-permute-done.refs_4_.refs_5_
  77.3 5.4 %scores_first.1 = (f32[8,1024]{1,0:T(8,128)S(1)}, f32[8,1024]{1,0:T(8,128)S(1)}) custom-call(s32[3]{0:T(128)S(1)} %copy-done.1, s32[2,1024]{1,0:T(2,128)S(1)} %copy-done, s32[2,1024]{1,0:T(2,128)S(1)} %copy-done, bf16[16,400,128]{2,1,0:T(8,128)(2,1)S(1)} %all_to_all.21.refs_3_, bf16[16,400,128]{2,1,0:T(8,128)(2,1)} %collective-permute-done.refs_4_.refs_5_, ...), custom_call_target="tpu_custom_call" | custom-call | tf_op jit(solution)/shard_map/scores_first/pallas_call | solution.py:255
  82.7 6.3 %scores_own.1 = (f32[8,1024]{1,0:T(8,128)S(1)}, f32[8,1024]{1,0:T(8,128)S(1)}) custom-call(s32[3]{0:T(128)S(1)} %copy-done.1, f32[8,1024]{1,0:T(8,128)S(1)} %get-tuple-element.17.refs_1_, f32[8,1024]{1,0:T(8,128)S(1)} %get-tuple-element.18.refs_2_, bf16[16,400,128]{2,1,0:T(8,128)(2,1)S(1)} %all_to_all.21.refs_3_, ...), custom_call_target="tpu_custom_call" | custom-call | tf_op jit(solution)/shard_map/scores_own/pallas_call | solution.py:255
  89.1 0.0 collective-permute-done.4.refs_7_.refs_8_
  89.1 4.9 %scores_near_a.1 = (f32[8,1024]{1,0:T(8,128)S(1)}, f32[8,1024]{1,0:T(8,128)S(1)}) custom-call(s32[3]{0:T(128)S(1)} %copy-done.1, f32[8,1024]{1,0:T(8,128)S(1)} %get-tuple-element.20.refs_1_, f32[8,1024]{1,0:T(8,128)S(1)} %get-tuple-element.21.refs_2_, bf16[16,400,128]{2,1,0:T(8,128)(2,1)S(1)} %all_to_all.21.refs_3_, ...), custom_call_target="tpu_custom_call" | custom-call | tf_op jit(solution)/shard_map/scores_near_a/pallas_call | solution.py:255
  94.0 0.0 collective-permute-done.6.refs_9_
  94.0 0.0 collective-permute-done.5.refs_6_
  94.0 6.6 %scores_near_b.1 = (f32[8,1024]{1,0:T(8,128)}, f32[8,1024]{1,0:T(8,128)}, f32[128,64]{1,0:T(8,128)S(1)}) custom-call(s32[3]{0:T(128)S(1)} %copy-done.1, f32[8,1024]{1,0:T(8,128)S(1)} %get-tuple-element.22.refs_1_, f32[8,1024]{1,0:T(8,128)S(1)} %get-tuple-element.23.refs_2_, bf16[16,400,128]{2,1,0:T(8,128)(2,1)S(1)} %all_to_all.21.refs_3_, ...), custom_call_target="tpu_custom_call" | custom-call | tf_op jit(solution)/shard_map/scores_near_b/pallas_call | solution.py:255
  100.6 15.9 %all_to_all.22 = f32[128,1,64]{2,1,0:T(1,128)S(1)} all-to-all(f32[128,1,64]{2,1,0:T(1,128)S(1)} %bitcast.10), channel_id=1, replica_groups=mesh['docs'=32,'split'=4] {'docs','split'}, dimensions={0} | all-to-all | bytes 65536 | tf_op jit(solution)/shard_map/all_to_all | solution.py:310
  116.6 1.0 finish.1
  (6 shorter events, 0.0 us)
Async XLA Ops:
  8.1 30.3 %collective-permute-start.2 = (bf16[16,400,128]{2,1,0:T(8,128)(2,1)}, bf16[16,400,128]{2,1,0:T(8,128)(2,1)}, u32[]{:S(2)}, u32[]{:S(2)}) collective-permute-start(bf16[16,400,128]{2,1,0:T(8,128)(2,1)} %get-tuple-element.19), channel_id=1, source_target_pairs={{0,4},{4,0},{32,36},{36,32},{64,68},{68,64},{96,100},{100,96},{8,1... | collective-permute-start | bytes 4915208 | tf_op jit(solution)/shard_map/ppermute | solution.py:282
  38.5 25.9 %all-to-all-start.1 = ((bf16[16,400,128]{2,1,0:T(8,128)(2,1)}), bf16[16,400,128]{2,1,0:T(8,128)(2,1)S(1)}, u32[]{:S(2)}, u32[]{:S(2)}) async-start(bf16[16,400,128]{2,1,0:T(8,128)(2,1)} %collective-permute-done.2), calls=%async_computation.1 | async-start | bytes 3276800 | tf_op jit(solution)/shard_map/all_to_all | solution.py:248
  44.0 33.3 %copy-start = (s32[2,1024]{1,0:T(2,128)S(1)}, s32[2,1024]{1,0:T(2,128)}, u32[]{:S(2)}) copy-start(s32[2,1024]{1,0:T(2,128)} %get-tuple-element.15.refs_1_.refs_2_.pos_ref) | copy-start | bytes 24580
  44.0 33.3 %copy-start.1 = (s32[3]{0:T(128)S(1)}, s32[3]{0:T(128)}, u32[]{:S(2)}) copy-start(s32[3]{0:T(128)} %pad_add_fusion.here_ref.refs_0_) | copy-start | bytes 40
  44.0 30.8 %collective-permute-start.1 = (bf16[16,400,128]{2,1,0:T(8,128)(2,1)S(1)}, bf16[16,400,128]{2,1,0:T(8,128)(2,1)}, u32[]{:S(2)}, u32[]{:S(2)}) collective-permute-start(bf16[16,400,128]{2,1,0:T(8,128)(2,1)S(1)} %all_to_all.21.refs_3_), channel_id=1, source_target_pairs={{0,1},{32,33},{64,65},{96,97},{8,9},{40,41},{72,73},{104,105},{16,... | collective-permute-start | bytes 4915208 | tf_op jit(solution)/shard_map/ppermute | solution.py:275
  45.8 31.5 %collective-permute-start = (bf16[16,400,128]{2,1,0:T(8,128)(2,1)S(1)}, bf16[16,400,128]{2,1,0:T(8,128)(2,1)}, u32[]{:S(2)}, u32[]{:S(2)}) collective-permute-start(bf16[16,400,128]{2,1,0:T(8,128)(2,1)S(1)} %all_to_all.21.refs_3_), channel_id=1, source_target_pairs={{0,3},{32,35},{64,67},{96,99},{8,11},{40,43},{72,75},{104,107},{16... | collective-permute-start | bytes 4915208 | tf_op jit(solution)/shard_map/ppermute | solution.py:274
  64.5 24.6 %collective-permute-start.4 = (bf16[8,400,128]{2,1,0:T(8,128)(2,1)S(1)}, bf16[8,400,128]{2,1,0:T(8,128)(2,1)S(1)}, u32[]{:S(2)}, u32[]{:S(2)}) collective-permute-start(bf16[8,400,128]{2,1,0:T(8,128)(2,1)S(1)} %get-tuple-element.26), channel_id=1, source_target_pairs={{0,1},{32,33},{64,65},{96,97},{8,9},{40,41},{72,73},{104,105},{16,... | collective-permute-start | bytes 2457608 | tf_op jit(solution)/shard_map/ppermute | solution.py:287
  66.6 22.4 %collective-permute-start.3 = (bf16[8,400,128]{2,1,0:T(8,128)(2,1)S(1)}, bf16[8,400,128]{2,1,0:T(8,128)(2,1)S(1)}, u32[]{:S(2)}, u32[]{:S(2)}) collective-permute-start(bf16[8,400,128]{2,1,0:T(8,128)(2,1)S(1)} %get-tuple-element.26), channel_id=1, source_target_pairs={{0,3},{32,35},{64,67},{96,99},{8,11},{40,43},{72,75},{104,107},{16... | collective-permute-start | bytes 2457608 | tf_op jit(solution)/shard_map/ppermute | solution.py:286
  69.2 24.8 %collective-permute-start.6 = (bf16[8,400,128]{2,1,0:T(8,128)(2,1)S(1)}, bf16[8,400,128]{2,1,0:T(8,128)(2,1)S(1)}, u32[]{:S(2)}, u32[]{:S(2)}) collective-permute-start(bf16[8,400,128]{2,1,0:T(8,128)(2,1)S(1)} %get-tuple-element.25), channel_id=1, source_target_pairs={{0,1},{32,33},{64,65},{96,97},{8,9},{40,41},{72,73},{104,105},{16,... | collective-permute-start | bytes 2457608 | tf_op jit(solution)/shard_map/ppermute | solution.py:287
  74.8 19.2 %collective-permute-start.5 = (bf16[8,400,128]{2,1,0:T(8,128)(2,1)S(1)}, bf16[8,400,128]{2,1,0:T(8,128)(2,1)S(1)}, u32[]{:S(2)}, u32[]{:S(2)}) collective-permute-start(bf16[8,400,128]{2,1,0:T(8,128)(2,1)S(1)} %get-tuple-element.25), channel_id=1, source_target_pairs={{0,3},{32,35},{64,67},{96,99},{8,11},{40,43},{72,75},{104,107},{16... | collective-permute-start | bytes 2457608 | tf_op jit(solution)/shard_map/ppermute | solution.py:286

commit v4 on v3

--- a/solution.py
+++ b/solution.py
@@ -17,7 +17,6 @@
 LANES = 128
 CODE_ROWS = 16
 HALF = PEERS // 2
-BLOCK = HALF * CAP
 ROWS = 8
 CHUNKS = ((0, 0, 64), (1, 0, 48), (1, 48, 16))
 BLOCKS = (((0, 32), (32, 32)), ((0, 32), (32, 16)), ((0, 16),))
@@ -27,9 +26,8 @@
 NT = (((1,), (1,)), ((), ()))
 NN = (((1,), (0,)), ((), ()))
 VMEM = pl.BlockSpec(memory_space=pltpu.VMEM)
-SMEM = pl.BlockSpec(memory_space=pltpu.SMEM)
 HBM = pl.BlockSpec(memory_space=pltpu.HBM)
-PARAMS = pltpu.CompilerParams(vmem_limit_bytes=32 * 2**20)
+PARAMS = pltpu.CompilerParams(vmem_limit_bytes=24 * 2**20)
 SCORE_PARAMS = pltpu.CompilerParams(vmem_limit_bytes=28 * 2**20)
 
 
@@ -56,6 +54,14 @@
 def core_moves():
     side = range(SIDE)
     return [(flat(x, y, z, c), flat(x, y, z, 1 - c)) for x in side for y in side for z in side for c in (0, 1)]
+
+
+def own_core():
+    return lax.axis_index("docs") & 1
+
+
+def own_spot():
+    return jnp.where(own_core() == 0, lax.axis_index("split"), (lax.axis_index("docs") >> 1) & (SIDE - 1))
 
 
 def place(unit, kind_rng, rank, ids, kind, out):
@@ -75,7 +81,7 @@
     out[:, CAP * columns // LANES :, :] = codes.reshape(PEERS, CODE_ROWS, LANES)
 
 
-def prepare(here_ref, ids_ref, emb_ref, pos_ref, first_ref, other_ref, emb, unit, sems):
+def prepare(ids_ref, emb_ref, pos_ref, first_ref, other_ref, emb, unit, sems):
     docs, columns = emb.shape
     parts = 4
     size = docs // parts
@@ -102,7 +108,7 @@
         rows = emb[p * size : (p + 1) * size, :]
         scaling = lax.rsqrt(jnp.mean(rows * rows, axis=1, keepdims=True) + EPSILON) * columns ** (-0.5)
         unit[p * size : (p + 1) * size, :] = (rows * scaling).astype(BF16)
-    kind_rng = rng ^ (here_ref[0] * PEERS)
+    kind_rng = rng ^ (own_core() * PEERS)
     for kind, out in enumerate((first_ref, other_ref)):
         place(unit[...], kind_rng, rank, ids, kind, out)
 
@@ -115,16 +121,26 @@
     return jnp.sum(jnp.where(iota(wide.shape, 0) == lane // CAP, wide, 0.0), axis=0, keepdims=True)
 
 
-def block_rows(ref, half):
+def block_rows(ref, start, peers):
     tiles = (ref.shape[1] - CODE_ROWS) // CAP
-    peers = slice(half * HALF, (half + 1) * HALF)
-    parts = [ref[peers, t * CAP : (t + 1) * CAP, :].reshape(BLOCK, LANES) for t in range(tiles)]
+    parts = [ref[start : start + peers, t * CAP : (t + 1) * CAP, :].reshape(peers * CAP, LANES) for t in range(tiles)]
     return jnp.concatenate(parts, axis=1)
 
 
-def scores(names, new, pairs, fresh, here_ref, best_in_ref, codes_in_ref, *refs):
+def holder(names, block):
+    return next(n for n in names if n[:2] == block[:2] and n[2] <= block[2] < n[2] + n[3])
+
+
+def scores(names, new, loaded, pairs, fresh, last, best_in_ref, codes_in_ref, *refs):
     arrays = dict(zip(names, refs[: len(names)]))
-    best_ref, codes_ref = refs[len(names) : len(names) + 2]
+    refs = list(refs[len(names) :])
+    best_ref, codes_ref = refs[:2]
+    copies = {}
+    for number, name in enumerate(loaded):
+        target = refs[2] if name == loaded[-1] else refs[3 + number]
+        copies[name] = pltpu.make_async_copy(arrays[name], target, refs[-1].at[number])
+        copies[name].start()
+        arrays[name] = target
     if fresh:
         best_ref[...] = jnp.full(best_ref.shape, -1.0, F32)
         codes_ref[...] = jnp.zeros(codes_ref.shape, F32)
@@ -133,18 +149,17 @@
         codes_ref[...] = codes_in_ref[...]
 
     def at(block):
-        row = block[0] * 2 + block[1]
-        return slice(row, row + 1), slice(block[2] * BLOCK, (block[2] + 1) * BLOCK)
+        role, kind, start, peers = block
+        return slice(role * 2 + kind, role * 2 + kind + 1), slice(start * CAP, (start + peers) * CAP)
 
     def rows_of(block):
-        if block in arrays:
-            return block_rows(arrays[block], 0)
-        return block_rows(arrays[block[0], block[1], 0], block[2])
-
-    for name in new:
-        codes = slot_codes(arrays[name])
-        start = name[2] * BLOCK
-        codes_ref[at(name)[0], start : start + codes.shape[1]] = codes
+        name = holder(names, block)
+        return block_rows(arrays[name], block[2] - name[2], block[3])
+
+    def arrive(name):
+        if name in copies:
+            copies.pop(name).wait()
+        codes_ref[at(name)] = slot_codes(arrays[name])
 
     def into(block, values):
         best_ref[at(block)] = jnp.maximum(best_ref[at(block)], values)
@@ -154,7 +169,7 @@
             left_rows = rows_of(left)
             left_codes = codes_ref[at(left)]
             left_codes = jnp.where(left_codes > 0, left_codes, -1.0)
-            left_codes = jnp.transpose(jnp.broadcast_to(left_codes, (LANES, BLOCK)))[:, :1]
+            left_codes = jnp.transpose(jnp.broadcast_to(left_codes, (LANES, left_codes.shape[1])))[:, :1]
             total = None
             for right in [p[1] for p in some if p[0] == left]:
                 score = lax.dot_general(left_rows, rows_of(right), NT, preferred_element_type=F32)
@@ -164,23 +179,28 @@
                 score = jnp.where(allowed, score, -1.0)
                 into(right, jnp.max(score, axis=0, keepdims=True))
                 if left != right:
-                    for lane in range(0, BLOCK, LANES):
+                    for lane in range(0, score.shape[1], LANES):
                         part = score[:, lane : lane + LANES]
                         total = part if total is None else jnp.maximum(total, part)
             if total is not None:
                 into(left, jnp.max(jnp.transpose(total), axis=0, keepdims=True))
 
-    run([p[:2] for p in pairs if p[2] == ALWAYS])
-    for when in (HEAVY, LIGHT):
-        some = [p[:2] for p in pairs if p[2] == when]
-        if some:
-            pl.when(here_ref[2] == when)(functools.partial(run, some))
-    if len(refs) > len(names) + 2:
-        pack(here_ref, best_ref, refs[-1])
-
-
-def pack(here_ref, best_ref, out_ref):
-    core, spot = here_ref[0], here_ref[1]
+    waiting = list(new)
+    for some in pairs:
+        for name in [n for n in waiting if any(holder(names, block) == n for p in some for block in p[:2])]:
+            waiting.remove(name)
+            arrive(name)
+        run([p[:2] for p in some if p[2] == ALWAYS])
+        for when in (HEAVY, LIGHT):
+            part = [p[:2] for p in some if p[2] == when]
+            if part:
+                pl.when(((own_spot() + 1) & 2) == 2 * (1 - when))(functools.partial(run, part))
+    if last:
+        pack(best_ref, refs[2])
+
+
+def pack(best_ref, out_ref):
+    core, spot = own_core(), own_spot()
     out_ref[...] = jnp.full(out_ref.shape, -1.0, F32)
     for kind in range(2):
         from_core = core if kind == 0 else 1 - core
@@ -219,16 +239,11 @@
 def per_device(embeddings, cluster_id):
     docs, columns = embeddings.shape
     devices = lax.axis_size("docs") * lax.axis_size("split")
-    at = lax.axis_index("docs")
-    core = at % 2
-    spot = jnp.where(core == 0, lax.axis_index("split"), at // 2 % SIDE)
-    heavy = ((spot == 3) | (spot == 0)).astype(jnp.int32)
-    here = jnp.stack([core, spot, heavy]).astype(jnp.int32)
     slots = jax.ShapeDtypeStruct((PEERS, CAP * columns // LANES + CODE_ROWS, LANES), BF16)
 
     pos, first, other = pl.pallas_call(
         prepare,
-        in_specs=[SMEM, VMEM, HBM],
+        in_specs=[VMEM, HBM],
         out_specs=[VMEM] * 3,
         out_shape=[jax.ShapeDtypeStruct((2, docs), jnp.int32), slots, slots],
         scratch_shapes=[
@@ -236,9 +251,9 @@
             pltpu.VMEM((docs, columns), BF16),
             pltpu.SemaphoreType.DMA((4,)),
         ],
-        compiler_params=pltpu.CompilerParams(vmem_limit_bytes=56 * 2**20),
+        compiler_params=PARAMS,
         name="prepare",
-    )(here, cluster_id.reshape(1, docs), embeddings)
+    )(cluster_id.reshape(1, docs), pltpu.with_memory_space_constraint(embeddings, pltpu.HBM))
 
     groups = plane_groups()
     moves_near = line_moves([(a, a - 1) for a in range(SIDE)])
@@ -249,64 +264,68 @@
 
     held = {}
 
-    def score_call(state, new, pairs, name, extra=()):
-        names = sorted({n if n in held else (n[0], n[1], 0) for p in pairs for n in p[:2]})
+    def score_call(state, new, pairs, name, loaded=(), last=False):
+        names = sorted({holder(held, n) for some in pairs for p in some for n in p[:2]})
         table = jax.ShapeDtypeStruct((ROWS, PEERS * CAP), F32)
-        return pl.pallas_call(
-            lambda *refs: scores(names, new, pairs, state[0] is pos, *refs),
-            in_specs=[SMEM, VMEM, VMEM] + [VMEM] * len(names),
+        extra = [jax.ShapeDtypeStruct(held[n].shape, BF16) for n in loaded[-1:]]
+        if last:
+            extra.append(jax.ShapeDtypeStruct((devices, CAP), F32))
+        scratch = [pltpu.VMEM(held[n].shape, BF16) for n in loaded[:-1]]
+        if loaded:
+            scratch.append(pltpu.SemaphoreType.DMA((len(loaded),)))
+        out = pl.pallas_call(
+            lambda *refs: scores(names, new, loaded, pairs, state[0] is pos, last, *refs),
+            in_specs=[VMEM, VMEM] + [HBM if n in loaded else VMEM for n in names],
             out_specs=[VMEM] * (2 + len(extra)),
             out_shape=[table, table, *extra],
+            scratch_shapes=scratch,
             compiler_params=SCORE_PARAMS,
             name=name,
-        )(here, *state[:2], *[held[n] for n in names])
-
-    def blocks(role, kind):
-        return [(role, kind, half) for half in range(2)]
+        )(*state[:2], *[held[n] for n in names])
+        held.update(zip(loaded[-1:], out[2:]))
+        return out
+
+    def blocks(role, kind, start=0, end=PEERS):
+        return [(role, kind, p, min(HALF, end - p)) for p in range(start, end, HALF)]
 
     def every(lefts, rights, when=ALWAYS):
         return [(a, b, when) for a in lefts for b in rights if a[:2] != b[:2] or a <= b]
 
     own_0, own_1, near_0, far_0 = blocks(OWN, 0), blocks(OWN, 1), blocks(NEAR, 0), blocks(FAR, 0)
-    (near_a, near_b), (far_a, far_b) = blocks(NEAR, 1), blocks(FAR, 1)
+    whole_0 = [(role, 0, 0, PEERS) for role in (OWN, NEAR, FAR)]
     own = to_owner(first)
-    held[own_0[0]] = own
-    held[near_0[0]] = lax.ppermute(own, AXES, moves_near)
-    held[far_0[0]] = lax.ppermute(own, AXES, moves_far)
-    state = score_call(
-        (pos, pos),
-        (own_0[0], near_0[0], far_0[0]),
-        every(own_0, own_0 + near_0) + every(near_0, far_0, LIGHT),
-        "scores_first",
-    )
+    held[whole_0[0]] = own
+    held[whole_0[1]] = lax.ppermute(own, AXES, moves_near)
+    held[whole_0[2]] = lax.ppermute(own, AXES, moves_far)
+    state = score_call((pos, pos), whole_0[:1], [every(own_0, own_0)], "scores_own_first")
     own = to_owner(lax.ppermute(other, AXES, core_moves()))
-    held[own_1[0]] = own
-
-    for near, far, peers in ((near_a, far_a, slice(0, HALF)), (near_b, far_b, slice(HALF, PEERS))):
-        held[near] = lax.ppermute(own[peers], AXES, moves_near)
-        held[far] = lax.ppermute(own[peers], AXES, moves_far)
+    whole_1 = (OWN, 1, 0, PEERS)
+    held[whole_1] = own
+    own = after(own, state[0])
+    parts = ((0, 8), (8, 12), (12, 16))
+    for start, end in parts:
+        held[NEAR, 1, start, end - start] = lax.ppermute(own[start:end], AXES, moves_near)
+        if not start:
+            held[FAR, 1, 0, PEERS] = lax.ppermute(own, AXES, moves_far)
+    state = score_call(state, (whole_1,), [every(own_0, own_1) + every(own_1, own_1)], "scores_own")
     state = score_call(
         state,
-        (own_1[0],),
-        every(own_0, own_1) + every(own_1, own_1 + near_0),
-        "scores_own",
+        whole_0[1:],
+        [every(own_0 + own_1, near_0), every(near_0[:1], far_0, HEAVY) + every(near_0, far_0[1:], LIGHT)],
+        "scores_near_first",
+        whole_0[1:],
     )
-    state = score_call(
-        state,
-        (near_a, far_a),
-        every(own_0 + own_1, [near_a]) + every([near_a], far_0) + every([near_a], [far_a], HEAVY),
-        "scores_near_a",
-    )
-    state = score_call(
-        state,
-        (near_b, far_b),
-        every(own_0 + own_1, [near_b])
-        + every([near_b], far_0)
-        + every([near_b], [far_a, far_b], HEAVY)
-        + every([near_a], [far_b], HEAVY),
-        "scores_near_b",
-        (jax.ShapeDtypeStruct((devices, CAP), F32),),
-    )
+    for start, end in parts:
+        near = blocks(NEAR, 1, start, end)
+        new = ((NEAR, 1, start, end - start),)
+        pairs = [every(own_0 + own_1, near) + every(near, far_0)]
+        if end == PEERS:
+            new += ((FAR, 1, 0, PEERS),)
+            older = [block for part in parts for block in blocks(NEAR, 1, *part)]
+            far_1 = blocks(FAR, 1)
+            first_half = [block for block in older if block[2] < HALF]
+            pairs.append(every(first_half, far_1, HEAVY) + every(older, far_1[1:], LIGHT))
+        state = score_call(state, new, pairs, f"scores_near_{start}", (), end == PEERS)
     got = lax.all_to_all(state[2], AXES, 0, 0, tiled=True)
     out = pl.pallas_call(
         finish,

time: 118 us -> 113 us (0.958)
  Pallas kernels: 31.7 us -> 25.5 us
  blocking collectives: 44.8 us -> 46.6 us
  waiting for transfers between devices: 22.5 us -> 20.9 us
  starting transfers between devices: 17.8 us -> 19.2 us
    pallas_call x5 -> x7, Pallas kernels: 30.7 us -> 24.5 us  [the longest x6 18.9 us: score_call(): pl.pallas_call(lambda *refs: scores(names, new, loaded, pairs, state[0] i...]
    all_to_all x1, blocking collectives: 15.9 us -> 18 us  [per_device(): got = lax.all_to_all(state[2], AXES, 0, 0, tiled=True)]
    all_to_all x1, waiting for transfers between devices: 16.9 us -> 15.4 us  [to_owner(): return lax.all_to_all(x, AXES, 0, 0, axis_index_groups=groups, tiled=True)]
    ppermute x6, starting transfers between devices: 10.8 us -> 12.1 us  [the longest x3 6.53 us: per_device(): lax.ppermute(own[start:end], AXES, moves_near)]
  transfers between devices with their start and end apart: 8 -> 8, of which waited for: 2 -> 3; matrix products, arithmetic and copies ran while one was open for 0% -> 0% of each run, Pallas kernels for 14% -> 14%
where the time goes in v4:
time: 113 us
  blocking collectives  46.6 us (41%)
  Pallas kernels  25.5 us (23%)
  waiting for transfers between devices  20.9 us (18%)
  starting transfers between devices  19.2 us (17%)
    all_to_all x1, blocking collectives, to_owner(): return lax.all_to_all(x, AXES, 0, 0, axis_index_groups=groups, tiled=True)  28.6 us
    pallas_call x6, Pallas kernels, score_call(): pl.pallas_call(lambda *refs: scores(names, new, loaded, pairs, state[0] i...  18.9 us
    all_to_all x1, blocking collectives, per_device(): got = lax.all_to_all(state[2], AXES, 0, 0, tiled=True)  18 us
    all_to_all x1, waiting for transfers between devices, to_owner(): return lax.all_to_all(x, AXES, 0, 0, axis_index_groups=groups, tiled=True)  15.4 us
    ppermute x3, starting transfers between devices, per_device(): lax.ppermute(own[start:end], AXES, moves_near)  6.53 us
    pallas_call x1, Pallas kernels, per_device(): pl.pallas_call(prepare, in_specs=[VMEM, HBM], out_specs=[VMEM] * 3, out_s...  5.57 us
    all_to_all x1, starting transfers between devices, to_owner(): return lax.all_to_all(x, AXES, 0, 0, axis_index_groups=groups, tiled=True)  5.53 us
    ppermute x1, waiting for transfers between devices, per_device(): held[whole_0[2]] = lax.ppermute(own, AXES, moves_far)  4.12 us
  transfers between devices with their start and end apart: 8, of which 3 were waited for; matrix products, arithmetic and copies ran while one was open for 0% of the time, Pallas kernels for 14%

profile of v4, /device:TPU:1, one launch (start us, length us, event | category | flops | bytes accessed | tf_op | source)
XLA Modules:
  0.0 113.1 jit_solution(7315474317270750457)
XLA Ops:
  0.0 0.7 copy-done
  0.7 5.6 %prepare.1 = (s32[2,1024]{1,0:T(2,128)S(1)}, bf16[16,400,128]{2,1,0:T(8,128)(2,1)S(1)}, bf16[16,400,128]{2,1,0:T(8,128)(2,1)S(1)}) custom-call(s32[1,1024]{1,0:T(1,128)S(1)} %bitcast.8, f32[1024,768]{1,0:T(8,128)} %emb_ref.1), custom_call_target="tpu_custom_call" | custom-call | tf_op jit(solution)/shard_map/prepare/pallas_call | solution.py:244
  6.3 1.5 %collective-permute-start = (bf16[16,400,128]{2,1,0:T(8,128)(2,1)S(1)}, bf16[16,400,128]{2,1,0:T(8,128)(2,1)}, u32[]{:S(2)}, u32[]{:S(2)}) collective-permute-start(bf16[16,400,128]{2,1,0:T(8,128)(2,1)S(1)} %get-tuple-element.25), channel_id=1, source_target_pairs={{0,4},{4,0},{32,36},{36,32},{64,68},{68,64},{96,100},{100,96},{8,1... | collective-permute-start | bytes 4915208 | tf_op jit(solution)/shard_map/ppermute | solution.py:301
  7.8 28.6 %all_to_all.21.refs_2_ = bf16[16,400,128]{2,1,0:T(8,128)(2,1)S(1)} all-to-all(bf16[16,400,128]{2,1,0:T(8,128)(2,1)S(1)} %get-tuple-element.22), channel_id=1, replica_groups={{0,8,16,24,32,40,48,56,64,72,80,88,96,104,112,120},{1,9,17,25,33,41,49,..., dimensions={0} | all-to-all | bytes 3276800 | tf_op jit(solution)/shard_map/all_to_all | solution.py:263
  36.4 5.5 %all-to-all-start.1 = ((bf16[16,400,128]{2,1,0:T(8,128)(2,1)}), bf16[16,400,128]{2,1,0:T(8,128)(2,1)S(1)}, u32[]{:S(2)}, u32[]{:S(2)}) async-start(bf16[16,400,128]{2,1,0:T(8,128)(2,1)} %collective-permute-done), calls=%async_computation.1 | async-start | bytes 3276800 | tf_op jit(solution)/shard_map/all_to_all | solution.py:263
  41.9 1.8 %collective-permute-start.2 = (bf16[16,400,128]{2,1,0:T(8,128)(2,1)S(1)}, bf16[16,400,128]{2,1,0:T(8,128)(2,1)}, u32[]{:S(2)}, u32[]{:S(2)}) collective-permute-start(bf16[16,400,128]{2,1,0:T(8,128)(2,1)S(1)} %all_to_all.21.refs_2_), channel_id=1, source_target_pairs={{0,1},{32,33},{64,65},{96,97},{8,9},{40,41},{72,73},{104,105},{16,... | collective-permute-start | bytes 4915208 | tf_op jit(solution)/shard_map/ppermute | solution.py:299
  43.7 1.7 %collective-permute-start.1 = (bf16[16,400,128]{2,1,0:T(8,128)(2,1)S(1)}, bf16[16,400,128]{2,1,0:T(8,128)(2,1)}, u32[]{:S(2)}, u32[]{:S(2)}) collective-permute-start(bf16[16,400,128]{2,1,0:T(8,128)(2,1)S(1)} %all_to_all.21.refs_2_), channel_id=1, source_target_pairs={{0,3},{32,35},{64,67},{96,99},{8,11},{40,43},{72,75},{104,107},{16... | collective-permute-start | bytes 4915208 | tf_op jit(solution)/shard_map/ppermute | solution.py:298
  45.4 1.5 %scores_own_first.1 = (f32[8,1024]{1,0:T(8,128)S(1)}, f32[8,1024]{1,0:T(8,128)S(1)}) custom-call(s32[2,1024]{1,0:T(2,128)S(1)} %get-tuple-element.21.refs_0_.refs_1_.pos_ref, s32[2,1024]{1,0:T(2,128)S(1)} %get-tuple-element.21.refs_0_.refs_1_.pos_ref, bf16[16,400,128]{2,1,0:T(8,128)(2,1)S(1)} %all_to_all.21.refs_2_), custom_call_target="tpu_custom_call" | custom-call | tf_op jit(solution)/shard_map/scores_own_first/pallas_call | solution.py:276
  46.9 15.4 %all-to-all-done.1.refs_3_ = bf16[16,400,128]{2,1,0:T(8,128)(2,1)S(1)} async-done(((bf16[16,400,128]{2,1,0:T(8,128)(2,1)}), bf16[16,400,128]{2,1,0:T(8,128)(2,1)S(1)}, u32[]{:S(2)}, u32[]{:S(2)}) %all-to-all-start.1) | async-done | bytes 1638432 | tf_op jit(solution)/shard_map/all_to_all | solution.py:263
  62.4 2.1 %collective-permute-start.6 = (bf16[16,400,128]{2,1,0:T(8,128)(2,1)S(1)}, bf16[16,400,128]{2,1,0:T(8,128)(2,1)S(1)}, u32[]{:S(2)}, u32[]{:S(2)}) collective-permute-start(bf16[16,400,128]{2,1,0:T(8,128)(2,1)S(1)} %all-to-all-done.1.refs_3_), channel_id=1, source_target_pairs={{0,1},{32,33},{64,65},{96,97},{8,9},{40,41},{72,73},{104,105},{16,... | collective-permute-start | bytes 4915208 | tf_op jit(solution)/shard_map/ppermute | solution.py:309
  64.5 0.1 slice.9
  64.5 2.5 %collective-permute-start.3 = (bf16[8,400,128]{2,1,0:T(8,128)(2,1)S(1)}, bf16[8,400,128]{2,1,0:T(8,128)(2,1)S(1)}, u32[]{:S(2)}, u32[]{:S(2)}) collective-permute-start(bf16[8,400,128]{2,1,0:T(8,128)(2,1)S(1)} %slice.9), channel_id=1, source_target_pairs={{0,3},{32,35},{64,67},{96,99},{8,11},{40,43},{72,75},{104,107},{16... | collective-permute-start | bytes 2457608 | tf_op jit(solution)/shard_map/ppermute | solution.py:307
  67.0 0.1 fusion
  67.1 1.5 %collective-permute-start.4 = (bf16[4,400,128]{2,1,0:T(8,128)(2,1)S(1)}, bf16[4,400,128]{2,1,0:T(8,128)(2,1)S(1)}, u32[]{:S(2)}, u32[]{:S(2)}) collective-permute-start(bf16[4,400,128]{2,1,0:T(8,128)(2,1)S(1)} %get-tuple-element.38), channel_id=1, source_target_pairs={{0,3},{32,35},{64,67},{96,99},{8,11},{40,43},{72,75},{104,107},{16... | collective-permute-start | bytes 1228808 | tf_op jit(solution)/shard_map/ppermute | solution.py:307
  68.6 4.1 %collective-permute-done.2.refs_5_ = bf16[16,400,128]{2,1,0:T(8,128)(2,1)} collective-permute-done((bf16[16,400,128]{2,1,0:T(8,128)(2,1)S(1)}, bf16[16,400,128]{2,1,0:T(8,128)(2,1)}, u32[]{:S(2)}, u32[]{:S(2)}) %collective-permute-start.2) | collective-permute-done | bytes 1638432 | tf_op jit(solution)/shard_map/ppermute | solution.py:299
  72.7 2.5 %collective-permute-start.5 = (bf16[4,400,128]{2,1,0:T(8,128)(2,1)S(1)}, bf16[4,400,128]{2,1,0:T(8,128)(2,1)S(1)}, u32[]{:S(2)}, u32[]{:S(2)}) collective-permute-start(bf16[4,400,128]{2,1,0:T(8,128)(2,1)S(1)} %get-tuple-element.37), channel_id=1, source_target_pairs={{0,3},{32,35},{64,67},{96,99},{8,11},{40,43},{72,75},{104,107},{16... | collective-permute-start | bytes 1228808 | tf_op jit(solution)/shard_map/ppermute | solution.py:307
  75.2 3.1 %scores_own.1 = (f32[8,1024]{1,0:T(8,128)S(1)}, f32[8,1024]{1,0:T(8,128)S(1)}) custom-call(f32[8,1024]{1,0:T(8,128)S(1)} %get-tuple-element.23.refs_0_, f32[8,1024]{1,0:T(8,128)S(1)} %get-tuple-element.24.refs_1_, bf16[16,400,128]{2,1,0:T(8,128)(2,1)S(1)} %all_to_all.21.refs_2_, bf16[16,400,128]{2,1,0:T(8,128)(2,1)S(1)} %all-to-all-done.1.refs_3_), custom_call_target="tpu_custom_call" | custom-call | tf_op jit(solution)/shard_map/scores_own/pallas_call | solution.py:276
  78.4 6.6 %scores_near_first.1 = (f32[8,1024]{1,0:T(8,128)S(1)}, f32[8,1024]{1,0:T(8,128)S(1)}, bf16[16,400,128]{2,1,0:T(8,128)(2,1)S(1)}) custom-call(f32[8,1024]{1,0:T(8,128)S(1)} %get-tuple-element.26.refs_0_, f32[8,1024]{1,0:T(8,128)S(1)} %get-tuple-element.27.refs_1_, bf16[16,400,128]{2,1,0:T(8,128)(2,1)S(1)} %all_to_all.21.refs_2_, ...), custom_call_target="tpu_custom_call" | custom-call | tf_op jit(solution)/shard_map/scores_near_first/pallas_call | solution.py:276
  85.0 2.8 %scores_near_0.1 = (f32[8,1024]{1,0:T(8,128)S(1)}, f32[8,1024]{1,0:T(8,128)S(1)}) custom-call(f32[8,1024]{1,0:T(8,128)S(1)} %get-tuple-element.28.refs_0_, f32[8,1024]{1,0:T(8,128)S(1)} %get-tuple-element.29.refs_1_, bf16[16,400,128]{2,1,0:T(8,128)(2,1)S(1)} %all_to_all.21.refs_2_, bf16[16,400,128]{2,1,0:T(8,128)(2,1)S(1)} %all-to-all-done.1.refs_3_, ...), custom_call_target="tpu_custom_call" | custom-call | tf_op jit(solution)/shard_map/scores_near_0/pallas_call | solution.py:276
  87.8 1.5 %scores_near_8.1 = (f32[8,1024]{1,0:T(8,128)S(1)}, f32[8,1024]{1,0:T(8,128)S(1)}) custom-call(f32[8,1024]{1,0:T(8,128)S(1)} %get-tuple-element.32.refs_0_, f32[8,1024]{1,0:T(8,128)S(1)} %get-tuple-element.33.refs_1_, bf16[16,400,128]{2,1,0:T(8,128)(2,1)S(1)} %all_to_all.21.refs_2_, bf16[16,400,128]{2,1,0:T(8,128)(2,1)S(1)} %all-to-all-done.1.refs_3_, ...), custom_call_target="tpu_custom_call" | custom-call | tf_op jit(solution)/shard_map/scores_near_8/pallas_call | solution.py:276
  89.3 1.4 %collective-permute-done.5.refs_6_ = bf16[4,400,128]{2,1,0:T(8,128)(2,1)S(1)} collective-permute-done((bf16[4,400,128]{2,1,0:T(8,128)(2,1)S(1)}, bf16[4,400,128]{2,1,0:T(8,128)(2,1)S(1)}, u32[]{:S(2)}, u32[]{:S(2)}) %collective-permute-start.5) | collective-permute-done | bytes 409632 | tf_op jit(solution)/shard_map/ppermute | solution.py:307
  90.6 3.4 %scores_near_12.1 = (f32[8,1024]{1,0:T(8,128)}, f32[8,1024]{1,0:T(8,128)}, f32[128,64]{1,0:T(8,128)S(1)}) custom-call(f32[8,1024]{1,0:T(8,128)S(1)} %get-tuple-element.34.refs_0_, f32[8,1024]{1,0:T(8,128)S(1)} %get-tuple-element.35.refs_1_, bf16[16,400,128]{2,1,0:T(8,128)(2,1)S(1)} %all_to_all.21.refs_2_, bf16[16,400,128]{2,1,0:T(8,128)(2,1)S(1)} %all-to-all-done.1.refs_3_, ...), custom_call_target="tpu_custom_call" | custom-call | tf_op jit(solution)/shard_map/scores_near_12/pallas_call | solution.py:276
  94.1 18.0 %all_to_all.22 = f32[128,1,64]{2,1,0:T(1,128)S(1)} all-to-all(f32[128,1,64]{2,1,0:T(1,128)S(1)} %bitcast.7), channel_id=1, replica_groups=mesh['docs'=32,'split'=4] {'docs','split'}, dimensions={0} | all-to-all | bytes 65536 | tf_op jit(solution)/shard_map/all_to_all | solution.py:329
  112.0 1.0 finish.1
  (6 shorter events, 0.0 us)
Async XLA Ops:
  0.0 0.7 copy-start
  6.3 30.1 %collective-permute-start = (bf16[16,400,128]{2,1,0:T(8,128)(2,1)S(1)}, bf16[16,400,128]{2,1,0:T(8,128)(2,1)}, u32[]{:S(2)}, u32[]{:S(2)}) collective-permute-start(bf16[16,400,128]{2,1,0:T(8,128)(2,1)S(1)} %get-tuple-element.25), channel_id=1, source_target_pairs={{0,4},{4,0},{32,36},{36,32},{64,68},{68,64},{96,100},{100,96},{8,1... | collective-permute-start | bytes 4915208 | tf_op jit(solution)/shard_map/ppermute | solution.py:301
  36.4 26.0 %all-to-all-start.1 = ((bf16[16,400,128]{2,1,0:T(8,128)(2,1)}), bf16[16,400,128]{2,1,0:T(8,128)(2,1)S(1)}, u32[]{:S(2)}, u32[]{:S(2)}) async-start(bf16[16,400,128]{2,1,0:T(8,128)(2,1)} %collective-permute-done), calls=%async_computation.1 | async-start | bytes 3276800 | tf_op jit(solution)/shard_map/all_to_all | solution.py:263
  41.9 30.8 %collective-permute-start.2 = (bf16[16,400,128]{2,1,0:T(8,128)(2,1)S(1)}, bf16[16,400,128]{2,1,0:T(8,128)(2,1)}, u32[]{:S(2)}, u32[]{:S(2)}) collective-permute-start(bf16[16,400,128]{2,1,0:T(8,128)(2,1)S(1)} %all_to_all.21.refs_2_), channel_id=1, source_target_pairs={{0,1},{32,33},{64,65},{96,97},{8,9},{40,41},{72,73},{104,105},{16,... | collective-permute-start | bytes 4915208 | tf_op jit(solution)/shard_map/ppermute | solution.py:299
  43.7 34.7 %collective-permute-start.1 = (bf16[16,400,128]{2,1,0:T(8,128)(2,1)S(1)}, bf16[16,400,128]{2,1,0:T(8,128)(2,1)}, u32[]{:S(2)}, u32[]{:S(2)}) collective-permute-start(bf16[16,400,128]{2,1,0:T(8,128)(2,1)S(1)} %all_to_all.21.refs_2_), channel_id=1, source_target_pairs={{0,3},{32,35},{64,67},{96,99},{8,11},{40,43},{72,75},{104,107},{16... | collective-permute-start | bytes 4915208 | tf_op jit(solution)/shard_map/ppermute | solution.py:298
  62.4 28.3 %collective-permute-start.6 = (bf16[16,400,128]{2,1,0:T(8,128)(2,1)S(1)}, bf16[16,400,128]{2,1,0:T(8,128)(2,1)S(1)}, u32[]{:S(2)}, u32[]{:S(2)}) collective-permute-start(bf16[16,400,128]{2,1,0:T(8,128)(2,1)S(1)} %all-to-all-done.1.refs_3_), channel_id=1, source_target_pairs={{0,1},{32,33},{64,65},{96,97},{8,9},{40,41},{72,73},{104,105},{16,... | collective-permute-start | bytes 4915208 | tf_op jit(solution)/shard_map/ppermute | solution.py:309
  64.5 20.4 %collective-permute-start.3 = (bf16[8,400,128]{2,1,0:T(8,128)(2,1)S(1)}, bf16[8,400,128]{2,1,0:T(8,128)(2,1)S(1)}, u32[]{:S(2)}, u32[]{:S(2)}) collective-permute-start(bf16[8,400,128]{2,1,0:T(8,128)(2,1)S(1)} %slice.9), channel_id=1, source_target_pairs={{0,3},{32,35},{64,67},{96,99},{8,11},{40,43},{72,75},{104,107},{16... | collective-permute-start | bytes 2457608 | tf_op jit(solution)/shard_map/ppermute | solution.py:307
  67.1 20.7 %collective-permute-start.4 = (bf16[4,400,128]{2,1,0:T(8,128)(2,1)S(1)}, bf16[4,400,128]{2,1,0:T(8,128)(2,1)S(1)}, u32[]{:S(2)}, u32[]{:S(2)}) collective-permute-start(bf16[4,400,128]{2,1,0:T(8,128)(2,1)S(1)} %get-tuple-element.38), channel_id=1, source_target_pairs={{0,3},{32,35},{64,67},{96,99},{8,11},{40,43},{72,75},{104,107},{16... | collective-permute-start | bytes 1228808 | tf_op jit(solution)/shard_map/ppermute | solution.py:307
  72.7 17.9 %collective-permute-start.5 = (bf16[4,400,128]{2,1,0:T(8,128)(2,1)S(1)}, bf16[4,400,128]{2,1,0:T(8,128)(2,1)S(1)}, u32[]{:S(2)}, u32[]{:S(2)}) collective-permute-start(bf16[4,400,128]{2,1,0:T(8,128)(2,1)S(1)} %get-tuple-element.37), channel_id=1, source_target_pairs={{0,3},{32,35},{64,67},{96,99},{8,11},{40,43},{72,75},{104,107},{16... | collective-permute-start | bytes 1228808 | tf_op jit(solution)/shard_map/ppermute | solution.py:307

commit v5 on v4

--- a/solution.py
+++ b/solution.py
@@ -64,24 +64,25 @@
     return jnp.where(own_core() == 0, lax.axis_index("split"), (lax.axis_index("docs") >> 1) & (SIDE - 1))
 
 
-def place(unit, kind_rng, rank, ids, kind, out):
+def place(unit, kind_rng, rank, ids, kind, out, peers):
     docs, columns = unit.shape
-    owner = kind_rng - kind * PEERS
-    inside = (owner >= 0) & (owner < PEERS) & (rank < CAP)
+    count = peers.stop - peers.start
+    owner = kind_rng - (kind * PEERS + peers.start)
+    inside = (owner >= 0) & (owner < count) & (rank < CAP)
     row = jnp.where(inside, owner * CAP + rank, -1)
-    pick = jnp.where(iota((PEERS * CAP, docs), 0) == row, 1.0, 0.0).astype(BF16)
+    pick = jnp.where(iota((count * CAP, docs), 0) == row, 1.0, 0.0).astype(BF16)
     rows = lax.dot_general(pick, unit, NN, preferred_element_type=F32).astype(BF16)
     for tile in range(columns // LANES):
         part = rows[:, tile * LANES : (tile + 1) * LANES]
-        out[:, tile * CAP : (tile + 1) * CAP, :] = part.reshape(PEERS, CAP, LANES)
-    code_peer = iota((PEERS * CODE_ROWS, docs), 0) // CODE_ROWS
+        out[peers, tile * CAP : (tile + 1) * CAP, :] = part.reshape(count, CAP, LANES)
+    code_peer = iota((count * CODE_ROWS, docs), 0) // CODE_ROWS
     owned = jnp.where(owner == code_peer, 1.0, 0.0).astype(BF16)
     code = jnp.where(iota((LANES, docs), 0) == rank, (ids & (CLU_DEV - 1)) + 1, 0).astype(F32).astype(BF16)
     codes = lax.dot_general(owned, code, NT, preferred_element_type=F32).astype(BF16)
-    out[:, CAP * columns // LANES :, :] = codes.reshape(PEERS, CODE_ROWS, LANES)
-
-
-def prepare(ids_ref, emb_ref, pos_ref, first_ref, other_ref, emb, unit, sems):
+    out[peers, CAP * columns // LANES :, :] = codes.reshape(count, CODE_ROWS, LANES)
+
+
+def prepare(ids_hbm, emb_ref, pos_ref, first_hbm, unit_hbm, emb, unit, first_ref, sems, ids_ref):
     docs, columns = emb.shape
     parts = 4
     size = docs // parts
@@ -89,8 +90,11 @@
         pltpu.make_async_copy(emb_ref.at[pl.ds(p * size, size)], emb.at[pl.ds(p * size, size)], sems.at[p])
         for p in range(parts)
     ]
+    ids_copy = pltpu.make_async_copy(ids_hbm, ids_ref, sems.at[parts])
+    ids_copy.start()
     for copy in copies:
         copy.start()
+    ids_copy.wait()
     ids = ids_ref[...]
     rng = ids >> 2
     key = (ids * docs + iota(ids.shape, 1)).astype(F32)
@@ -108,16 +112,35 @@
         rows = emb[p * size : (p + 1) * size, :]
         scaling = lax.rsqrt(jnp.mean(rows * rows, axis=1, keepdims=True) + EPSILON) * columns ** (-0.5)
         unit[p * size : (p + 1) * size, :] = (rows * scaling).astype(BF16)
+    unit_copy = pltpu.make_async_copy(unit, unit_hbm, sems.at[parts + 1])
+    unit_copy.start()
     kind_rng = rng ^ (own_core() * PEERS)
-    for kind, out in enumerate((first_ref, other_ref)):
-        place(unit[...], kind_rng, rank, ids, kind, out)
+    pos_ref[2:3, :] = kind_rng
+    pos_ref[3:4, :] = ids
+    out_copies = []
+    for part in range(2):
+        peers = slice(part * HALF, (part + 1) * HALF)
+        place(unit[...], kind_rng, rank, ids, 0, first_ref, peers)
+        out_copies.append(
+            pltpu.make_async_copy(
+                first_ref.at[pl.ds(part * HALF, HALF)], first_hbm.at[pl.ds(part * HALF, HALF)], sems.at[parts + 2 + part]
+            )
+        )
+        out_copies[-1].start()
+    unit_copy.wait()
+    for copy in out_copies:
+        copy.wait()
+
+
+def place_other(pos_ref, unit_ref, out_ref):
+    place(unit_ref[...], pos_ref[2:3, :], pos_ref[1:2, :], pos_ref[3:4, :], 1, out_ref, slice(0, PEERS))
 
 
 def slot_codes(ref):
     codes = ref[:, ref.shape[1] - CODE_ROWS :, :].astype(F32)[:, 0, :].astype(BF16)
     lane = iota((1, ref.shape[0] * CAP), 1)
-    spread = jnp.where(iota((LANES, lane.shape[1]), 0) == lane % CAP, 1.0, 0.0).astype(BF16)
-    wide = lax.dot_general(codes, spread, NN, preferred_element_type=F32)
+    spread = jnp.where(iota((CAP, lane.shape[1]), 0) == lane % CAP, 1.0, 0.0).astype(BF16)
+    wide = lax.dot_general(codes[:, :CAP], spread, NN, preferred_element_type=F32)
     return jnp.sum(jnp.where(iota(wide.shape, 0) == lane // CAP, wide, 0.0), axis=0, keepdims=True)
 
 
@@ -241,19 +264,34 @@
     devices = lax.axis_size("docs") * lax.axis_size("split")
     slots = jax.ShapeDtypeStruct((PEERS, CAP * columns // LANES + CODE_ROWS, LANES), BF16)
 
-    pos, first, other = pl.pallas_call(
+    pos, first, unit = pl.pallas_call(
         prepare,
-        in_specs=[VMEM, HBM],
-        out_specs=[VMEM] * 3,
-        out_shape=[jax.ShapeDtypeStruct((2, docs), jnp.int32), slots, slots],
+        in_specs=[HBM, HBM],
+        out_specs=[VMEM, HBM, HBM],
+        out_shape=[
+            jax.ShapeDtypeStruct((4, docs), jnp.int32),
+            slots,
+            jax.ShapeDtypeStruct((docs, columns), BF16),
+        ],
         scratch_shapes=[
             pltpu.VMEM((docs, columns), F32),
             pltpu.VMEM((docs, columns), BF16),
-            pltpu.SemaphoreType.DMA((4,)),
+            pltpu.VMEM(slots.shape, BF16),
+            pltpu.SemaphoreType.DMA((8,)),
+            pltpu.VMEM((1, docs), jnp.int32),
         ],
         compiler_params=PARAMS,
         name="prepare",
-    )(cluster_id.reshape(1, docs), pltpu.with_memory_space_constraint(embeddings, pltpu.HBM))
+    )(pltpu.with_memory_space_constraint(cluster_id.reshape(1, docs), pltpu.HBM), pltpu.with_memory_space_constraint(embeddings, pltpu.HBM))
+
+    other = pl.pallas_call(
+        place_other,
+        in_specs=[VMEM, VMEM],
+        out_specs=VMEM,
+        out_shape=slots,
+        compiler_params=PARAMS,
+        name="place_other",
+    )(lax.ppermute(pos, AXES, core_moves()), lax.ppermute(unit, AXES, core_moves()))
 
     groups = plane_groups()
     moves_near = line_moves([(a, a - 1) for a in range(SIDE)])
@@ -298,7 +336,7 @@
     held[whole_0[1]] = lax.ppermute(own, AXES, moves_near)
     held[whole_0[2]] = lax.ppermute(own, AXES, moves_far)
     state = score_call((pos, pos), whole_0[:1], [every(own_0, own_0)], "scores_own_first")
-    own = to_owner(lax.ppermute(other, AXES, core_moves()))
+    own = to_owner(other)
     whole_1 = (OWN, 1, 0, PEERS)
     held[whole_1] = own
     own = after(own, state[0])
@@ -307,7 +345,8 @@
         held[NEAR, 1, start, end - start] = lax.ppermute(own[start:end], AXES, moves_near)
         if not start:
             held[FAR, 1, 0, PEERS] = lax.ppermute(own, AXES, moves_far)
-    state = score_call(state, (whole_1,), [every(own_0, own_1) + every(own_1, own_1)], "scores_own")
+            state = score_call(state, (whole_1,), [every(own_0, own_1) + every(own_1, own_1)], "scores_own")
+            own = after(own, state[0])
     state = score_call(
         state,
         whole_0[1:],

time: 113 us -> 111 us (0.982)
  blocking collectives: 46.6 us -> 15.9 us
  waiting for transfers between devices: 20.9 us -> 43.5 us
  starting transfers between devices: 19.2 us -> 23.6 us
    all_to_all x1 -> x0, blocking collectives: 28.6 us -> none  [to_owner(): return lax.all_to_all(x, AXES, 0, 0, axis_index_groups=groups, tiled=True)]
    all_to_all x1 -> x2, waiting for transfers between devices: 15.4 us -> 34.6 us  [to_owner(): return lax.all_to_all(x, AXES, 0, 0, axis_index_groups=groups, tiled=True)]
    all_to_all x1 -> x2, starting transfers between devices: 5.53 us -> 12.5 us  [to_owner(): return lax.all_to_all(x, AXES, 0, 0, axis_index_groups=groups, tiled=True)]
    ppermute x1, waiting for transfers between devices: 4.12 us -> 0.01 us  [per_device(): held[whole_0[2]] = lax.ppermute(own, AXES, moves_far)]
    ppermute x1, waiting for transfers between devices: 0.01 us -> 3.02 us  [per_device(): held[FAR, 1, 0, PEERS] = lax.ppermute(own, AXES, moves_far)]
    ppermute x3, waiting for transfers between devices: 1.36 us -> 3.63 us  [per_device(): lax.ppermute(own[start:end], AXES, moves_near)]
    all_to_all x1, blocking collectives: 18 us -> 15.9 us  [per_device(): got = lax.all_to_all(state[2], AXES, 0, 0, tiled=True)]
    ppermute x1, starting transfers between devices: 1.77 us -> 0.01 us  [per_device(): held[whole_0[2]] = lax.ppermute(own, AXES, moves_far)]
  transfers between devices with their start and end apart: 8 -> 10, of which waited for: 3 -> 7; matrix products, arithmetic and copies ran while one was open for 0% -> 0% of each run, Pallas kernels for 14% -> 16%
where the time goes in v5:
time: 111 us
  waiting for transfers between devices  43.5 us (39%)
  Pallas kernels  26.5 us (24%)
  starting transfers between devices  23.6 us (21%)
  blocking collectives  15.9 us (14%)
  local copies, waits for them, and re-layouts  1.28 us (1%)
    all_to_all x2, waiting for transfers between devices, to_owner(): return lax.all_to_all(x, AXES, 0, 0, axis_index_groups=groups, tiled=True)  34.6 us
    pallas_call x6, Pallas kernels, score_call(): pl.pallas_call(lambda *refs: scores(names, new, loaded, pairs, state[0] i...  18.7 us
    all_to_all x1, blocking collectives, per_device(): got = lax.all_to_all(state[2], AXES, 0, 0, tiled=True)  15.9 us
    all_to_all x2, starting transfers between devices, to_owner(): return lax.all_to_all(x, AXES, 0, 0, axis_index_groups=groups, tiled=True)  12.5 us
    ppermute x3, starting transfers between devices, per_device(): lax.ppermute(own[start:end], AXES, moves_near)  6.34 us
    pallas_call x1, Pallas kernels, per_device(): pl.pallas_call(prepare, in_specs=[HBM, HBM], out_specs=[VMEM, HBM, HBM],...  4.84 us
    ppermute x3, waiting for transfers between devices, per_device(): lax.ppermute(own[start:end], AXES, moves_near)  3.63 us
    ppermute x1, waiting for transfers between devices, per_device(): held[FAR, 1, 0, PEERS] = lax.ppermute(own, AXES, moves_far)  3.02 us
  transfers between devices with their start and end apart: 10, of which 7 were waited for; matrix products, arithmetic and copies ran while one was open for 0% of the time, Pallas kernels for 16%

profile of v5, /device:TPU:1, one launch (start us, length us, event | category | flops | bytes accessed | tf_op | source)
XLA Modules:
  0.0 110.9 jit_solution(6406029369026211387)
XLA Ops:
  0.0 4.8 %prepare.1 = (s32[4,1024]{1,0:T(4,128)S(1)}, bf16[16,400,128]{2,1,0:T(8,128)(2,1)}, bf16[1024,768]{1,0:T(8,128)(2,1)}) custom-call(s32[1,1024]{1,0:T(1,128)} %bitcast.8, f32[1024,768]{1,0:T(8,128)} %emb_ref.1), custom_call_target="tpu_custom_call" | custom-call | tf_op jit(solution)/shard_map/prepare/pallas_call | solution.py:267
  4.8 1.5 %collective-permute-start.1 = (bf16[1024,768]{1,0:T(8,128)(2,1)}, bf16[1024,768]{1,0:T(8,128)(2,1)S(1)}, u32[]{:S(2)}, u32[]{:S(2)}) collective-permute-start(bf16[1024,768]{1,0:T(8,128)(2,1)} %get-tuple-element.26), channel_id=1, source_target_pairs={{0,4},{4,0},{32,36},{36,32},{64,68},{68,64},{96,100},{100,96},{8,1... | collective-permute-start | bytes 4718600 | tf_op jit(solution)/shard_map/ppermute | solution.py:294
  6.4 7.7 %all-to-all-start = ((bf16[16,400,128]{2,1,0:T(8,128)(2,1)}), bf16[16,400,128]{2,1,0:T(8,128)(2,1)S(1)}, u32[]{:S(2)}, u32[]{:S(2)}) async-start(bf16[16,400,128]{2,1,0:T(8,128)(2,1)} %get-tuple-element.23), calls=%async_computation | async-start | bytes 3276800 | tf_op jit(solution)/shard_map/all_to_all | solution.py:301
  14.6 0.8 collective-permute-done.pos_ref
  15.4 1.9 %place_other.1 = bf16[16,400,128]{2,1,0:T(8,128)(2,1)S(1)} custom-call(s32[4,1024]{1,0:T(4,128)S(1)} %collective-permute-done.pos_ref, bf16[1024,768]{1,0:T(8,128)(2,1)S(1)} %collective-permute-done.1.unit_ref), custom_call_target="tpu_custom_call" | custom-call | tf_op jit(solution)/shard_map/place_other/pallas_call | solution.py:287
  17.4 1.2 %copy-done = bf16[16,400,128]{2,1,0:T(8,128)(2,1)} copy-done((bf16[16,400,128]{2,1,0:T(8,128)(2,1)}, bf16[16,400,128]{2,1,0:T(8,128)(2,1)S(1)}, u32[]{:S(2)}) %copy-start) | copy-done | bytes 1638424
  18.6 17.4 %all-to-all-done.refs_2_ = bf16[16,400,128]{2,1,0:T(8,128)(2,1)S(1)} async-done(((bf16[16,400,128]{2,1,0:T(8,128)(2,1)}), bf16[16,400,128]{2,1,0:T(8,128)(2,1)S(1)}, u32[]{:S(2)}, u32[]{:S(2)}) %all-to-all-start) | async-done | bytes 1638432 | tf_op jit(solution)/shard_map/all_to_all | solution.py:301
  36.0 4.8 %all-to-all-start.1 = ((bf16[16,400,128]{2,1,0:T(8,128)(2,1)}), bf16[16,400,128]{2,1,0:T(8,128)(2,1)S(1)}, u32[]{:S(2)}, u32[]{:S(2)}) async-start(bf16[16,400,128]{2,1,0:T(8,128)(2,1)} %copy-done), calls=%async_computation.1 | async-start | bytes 3276800 | tf_op jit(solution)/shard_map/all_to_all | solution.py:301
  40.8 2.0 %collective-permute-start.2 = (bf16[16,400,128]{2,1,0:T(8,128)(2,1)S(1)}, bf16[16,400,128]{2,1,0:T(8,128)(2,1)}, u32[]{:S(2)}, u32[]{:S(2)}) collective-permute-start(bf16[16,400,128]{2,1,0:T(8,128)(2,1)S(1)} %all-to-all-done.refs_2_), channel_id=1, source_target_pairs={{0,3},{32,35},{64,67},{96,99},{8,11},{40,43},{72,75},{104,107},{16... | collective-permute-start | bytes 4915208 | tf_op jit(solution)/shard_map/ppermute | solution.py:336
  42.9 1.5 %scores_own_first.1 = (f32[8,1024]{1,0:T(8,128)S(1)}, f32[8,1024]{1,0:T(8,128)S(1)}) custom-call(s32[4,1024]{1,0:T(4,128)S(1)} %get-tuple-element.22.refs_0_.refs_1_.pos_ref, s32[4,1024]{1,0:T(4,128)S(1)} %get-tuple-element.22.refs_0_.refs_1_.pos_ref, bf16[16,400,128]{2,1,0:T(8,128)(2,1)S(1)} %all-to-all-done.refs_2_), custom_call_target="tpu_custom_call" | custom-call | tf_op jit(solution)/shard_map/scores_own_first/pallas_call | solution.py:314
  44.4 17.2 %all-to-all-done.1.refs_3_ = bf16[16,400,128]{2,1,0:T(8,128)(2,1)S(1)} async-done(((bf16[16,400,128]{2,1,0:T(8,128)(2,1)}), bf16[16,400,128]{2,1,0:T(8,128)(2,1)S(1)}, u32[]{:S(2)}, u32[]{:S(2)}) %all-to-all-start.1) | async-done | bytes 1638432 | tf_op jit(solution)/shard_map/all_to_all | solution.py:301
  62.3 2.1 %collective-permute-start.4 = (bf16[8,400,128]{2,1,0:T(8,128)(2,1)S(1)}, bf16[8,400,128]{2,1,0:T(8,128)(2,1)S(1)}, u32[]{:S(2)}, u32[]{:S(2)}) collective-permute-start(bf16[8,400,128]{2,1,0:T(8,128)(2,1)S(1)} %slice.9), channel_id=1, source_target_pairs={{0,3},{32,35},{64,67},{96,99},{8,11},{40,43},{72,75},{104,107},{16... | collective-permute-start | bytes 2457608 | tf_op jit(solution)/shard_map/ppermute | solution.py:345
  64.3 3.1 %scores_own.1 = (f32[8,1024]{1,0:T(8,128)S(1)}, f32[8,1024]{1,0:T(8,128)S(1)}) custom-call(f32[8,1024]{1,0:T(8,128)S(1)} %get-tuple-element.24.refs_0_, f32[8,1024]{1,0:T(8,128)S(1)} %get-tuple-element.25.refs_1_, bf16[16,400,128]{2,1,0:T(8,128)(2,1)S(1)} %all-to-all-done.refs_2_, bf16[16,400,128]{2,1,0:T(8,128)(2,1)S(1)} %all-to-all-done.1.refs_3_), custom_call_target="tpu_custom_call" | custom-call | tf_op jit(solution)/shard_map/scores_own/pallas_call | solution.py:314
  67.6 1.1 %collective-permute-start.5 = (bf16[4,400,128]{2,1,0:T(8,128)(2,1)S(1)}, bf16[4,400,128]{2,1,0:T(8,128)(2,1)S(1)}, u32[]{:S(2)}, u32[]{:S(2)}) collective-permute-start(bf16[4,400,128]{2,1,0:T(8,128)(2,1)S(1)} %get-tuple-element.40), channel_id=1, source_target_pairs={{0,3},{32,35},{64,67},{96,99},{8,11},{40,43},{72,75},{104,107},{16... | collective-permute-start | bytes 1228808 | tf_op jit(solution)/shard_map/ppermute | solution.py:345
  68.7 1.4 %collective-permute-done.2.refs_4_ = bf16[16,400,128]{2,1,0:T(8,128)(2,1)} collective-permute-done((bf16[16,400,128]{2,1,0:T(8,128)(2,1)S(1)}, bf16[16,400,128]{2,1,0:T(8,128)(2,1)}, u32[]{:S(2)}, u32[]{:S(2)}) %collective-permute-start.2) | collective-permute-done | bytes 1638432 | tf_op jit(solution)/shard_map/ppermute | solution.py:336
  70.0 3.2 %collective-permute-start.6 = (bf16[4,400,128]{2,1,0:T(8,128)(2,1)S(1)}, bf16[4,400,128]{2,1,0:T(8,128)(2,1)S(1)}, u32[]{:S(2)}, u32[]{:S(2)}) collective-permute-start(bf16[4,400,128]{2,1,0:T(8,128)(2,1)S(1)} %get-tuple-element.39), channel_id=1, source_target_pairs={{0,3},{32,35},{64,67},{96,99},{8,11},{40,43},{72,75},{104,107},{16... | collective-permute-start | bytes 1228808 | tf_op jit(solution)/shard_map/ppermute | solution.py:345
  73.2 6.3 %scores_near_first.1 = (f32[8,1024]{1,0:T(8,128)S(1)}, f32[8,1024]{1,0:T(8,128)S(1)}, bf16[16,400,128]{2,1,0:T(8,128)(2,1)S(1)}) custom-call(f32[8,1024]{1,0:T(8,128)S(1)} %get-tuple-element.27.refs_0_, f32[8,1024]{1,0:T(8,128)S(1)} %get-tuple-element.28.refs_1_, bf16[16,400,128]{2,1,0:T(8,128)(2,1)S(1)} %all-to-all-done.refs_2_, ...), custom_call_target="tpu_custom_call" | custom-call | tf_op jit(solution)/shard_map/scores_near_first/pallas_call | solution.py:314
  79.6 2.8 %scores_near_0.1 = (f32[8,1024]{1,0:T(8,128)S(1)}, f32[8,1024]{1,0:T(8,128)S(1)}) custom-call(f32[8,1024]{1,0:T(8,128)S(1)} %get-tuple-element.29.refs_0_, f32[8,1024]{1,0:T(8,128)S(1)} %get-tuple-element.30.refs_1_, bf16[16,400,128]{2,1,0:T(8,128)(2,1)S(1)} %all-to-all-done.refs_2_, bf16[16,400,128]{2,1,0:T(8,128)(2,1)S(1)} %all-to-all-done.1.refs_3_, ...), custom_call_target="tpu_custom_call" | custom-call | tf_op jit(solution)/shard_map/scores_near_0/pallas_call | solution.py:314
  83.1 1.5 %scores_near_8.1 = (f32[8,1024]{1,0:T(8,128)S(1)}, f32[8,1024]{1,0:T(8,128)S(1)}) custom-call(f32[8,1024]{1,0:T(8,128)S(1)} %get-tuple-element.33.refs_0_, f32[8,1024]{1,0:T(8,128)S(1)} %get-tuple-element.34.refs_1_, bf16[16,400,128]{2,1,0:T(8,128)(2,1)S(1)} %all-to-all-done.refs_2_, bf16[16,400,128]{2,1,0:T(8,128)(2,1)S(1)} %all-to-all-done.1.refs_3_, ...), custom_call_target="tpu_custom_call" | custom-call | tf_op jit(solution)/shard_map/scores_near_8/pallas_call | solution.py:314
  84.6 2.9 %collective-permute-done.6.refs_6_ = bf16[4,400,128]{2,1,0:T(8,128)(2,1)S(1)} collective-permute-done((bf16[4,400,128]{2,1,0:T(8,128)(2,1)S(1)}, bf16[4,400,128]{2,1,0:T(8,128)(2,1)S(1)}, u32[]{:S(2)}, u32[]{:S(2)}) %collective-permute-start.6) | collective-permute-done | bytes 409632 | tf_op jit(solution)/shard_map/ppermute | solution.py:345
  87.5 3.0 %collective-permute-done.7.refs_8_ = bf16[16,400,128]{2,1,0:T(8,128)(2,1)S(1)} collective-permute-done((bf16[16,400,128]{2,1,0:T(8,128)(2,1)S(1)}, bf16[16,400,128]{2,1,0:T(8,128)(2,1)S(1)}, u32[]{:S(2)}, u32[]{:S(2)}) %collective-permute-start.7) | collective-permute-done | bytes 1638432 | tf_op jit(solution)/shard_map/ppermute | solution.py:347
  90.5 3.4 %scores_near_12.1 = (f32[8,1024]{1,0:T(8,128)}, f32[8,1024]{1,0:T(8,128)}, f32[128,64]{1,0:T(8,128)S(1)}) custom-call(f32[8,1024]{1,0:T(8,128)S(1)} %get-tuple-element.36.refs_0_, f32[8,1024]{1,0:T(8,128)S(1)} %get-tuple-element.37.refs_1_, bf16[16,400,128]{2,1,0:T(8,128)(2,1)S(1)} %all-to-all-done.refs_2_, ...), custom_call_target="tpu_custom_call" | custom-call | tf_op jit(solution)/shard_map/scores_near_12/pallas_call | solution.py:314
  93.9 15.9 %all_to_all.21 = f32[128,1,64]{2,1,0:T(1,128)S(1)} all-to-all(f32[128,1,64]{2,1,0:T(1,128)S(1)} %bitcast.7), channel_id=1, replica_groups=mesh['docs'=32,'split'=4] {'docs','split'}, dimensions={0} | all-to-all | bytes 65536 | tf_op jit(solution)/shard_map/all_to_all | solution.py:368
  109.8 1.0 finish.1
  (10 shorter events, 2.1 us)
Async XLA Ops:
  4.8 10.6 %collective-permute-start.1 = (bf16[1024,768]{1,0:T(8,128)(2,1)}, bf16[1024,768]{1,0:T(8,128)(2,1)S(1)}, u32[]{:S(2)}, u32[]{:S(2)}) collective-permute-start(bf16[1024,768]{1,0:T(8,128)(2,1)} %get-tuple-element.26), channel_id=1, source_target_pairs={{0,4},{4,0},{32,36},{36,32},{64,68},{68,64},{96,100},{100,96},{8,1... | collective-permute-start | bytes 4718600 | tf_op jit(solution)/shard_map/ppermute | solution.py:294
  6.4 29.6 %all-to-all-start = ((bf16[16,400,128]{2,1,0:T(8,128)(2,1)}), bf16[16,400,128]{2,1,0:T(8,128)(2,1)S(1)}, u32[]{:S(2)}, u32[]{:S(2)}) async-start(bf16[16,400,128]{2,1,0:T(8,128)(2,1)} %get-tuple-element.23), calls=%async_computation | async-start | bytes 3276800 | tf_op jit(solution)/shard_map/all_to_all | solution.py:301
  14.0 1.4 %collective-permute-start = (s32[4,1024]{1,0:T(4,128)S(1)}, s32[4,1024]{1,0:T(4,128)S(1)}, u32[]{:S(2)}, u32[]{:S(2)}) collective-permute-start(s32[4,1024]{1,0:T(4,128)S(1)} %get-tuple-element.22.refs_0_.refs_1_.pos_ref), channel_id=1, source_target_pairs={{0,4},{4,0},{32,36},{36,32},{64,68},{68,64},{96,100},{100,96},{8,1... | collective-permute-start | bytes 49160 | tf_op jit(solution)/shard_map/ppermute | solution.py:294
  17.4 1.2 %copy-start = (bf16[16,400,128]{2,1,0:T(8,128)(2,1)}, bf16[16,400,128]{2,1,0:T(8,128)(2,1)S(1)}, u32[]{:S(2)}) copy-start(bf16[16,400,128]{2,1,0:T(8,128)(2,1)S(1)} %place_other.1) | copy-start | bytes 4915204
  36.0 25.6 %all-to-all-start.1 = ((bf16[16,400,128]{2,1,0:T(8,128)(2,1)}), bf16[16,400,128]{2,1,0:T(8,128)(2,1)S(1)}, u32[]{:S(2)}, u32[]{:S(2)}) async-start(bf16[16,400,128]{2,1,0:T(8,128)(2,1)} %copy-done), calls=%async_computation.1 | async-start | bytes 3276800 | tf_op jit(solution)/shard_map/all_to_all | solution.py:301
  40.8 29.2 %collective-permute-start.2 = (bf16[16,400,128]{2,1,0:T(8,128)(2,1)S(1)}, bf16[16,400,128]{2,1,0:T(8,128)(2,1)}, u32[]{:S(2)}, u32[]{:S(2)}) collective-permute-start(bf16[16,400,128]{2,1,0:T(8,128)(2,1)S(1)} %all-to-all-done.refs_2_), channel_id=1, source_target_pairs={{0,3},{32,35},{64,67},{96,99},{8,11},{40,43},{72,75},{104,107},{16... | collective-permute-start | bytes 4915208 | tf_op jit(solution)/shard_map/ppermute | solution.py:336
  42.8 30.4 %collective-permute-start.3 = (bf16[16,400,128]{2,1,0:T(8,128)(2,1)S(1)}, bf16[16,400,128]{2,1,0:T(8,128)(2,1)}, u32[]{:S(2)}, u32[]{:S(2)}) collective-permute-start(bf16[16,400,128]{2,1,0:T(8,128)(2,1)S(1)} %all-to-all-done.refs_2_), channel_id=1, source_target_pairs={{0,1},{32,33},{64,65},{96,97},{8,9},{40,41},{72,73},{104,105},{16,... | collective-permute-start | bytes 4915208 | tf_op jit(solution)/shard_map/ppermute | solution.py:337
  61.5 29.0 %collective-permute-start.7 = (bf16[16,400,128]{2,1,0:T(8,128)(2,1)S(1)}, bf16[16,400,128]{2,1,0:T(8,128)(2,1)S(1)}, u32[]{:S(2)}, u32[]{:S(2)}) collective-permute-start(bf16[16,400,128]{2,1,0:T(8,128)(2,1)S(1)} %all-to-all-done.1.refs_3_), channel_id=1, source_target_pairs={{0,1},{32,33},{64,65},{96,97},{8,9},{40,41},{72,73},{104,105},{16,... | collective-permute-start | bytes 4915208 | tf_op jit(solution)/shard_map/ppermute | solution.py:347
  62.3 17.3 %collective-permute-start.4 = (bf16[8,400,128]{2,1,0:T(8,128)(2,1)S(1)}, bf16[8,400,128]{2,1,0:T(8,128)(2,1)S(1)}, u32[]{:S(2)}, u32[]{:S(2)}) collective-permute-start(bf16[8,400,128]{2,1,0:T(8,128)(2,1)S(1)} %slice.9), channel_id=1, source_target_pairs={{0,3},{32,35},{64,67},{96,99},{8,11},{40,43},{72,75},{104,107},{16... | collective-permute-start | bytes 2457608 | tf_op jit(solution)/shard_map/ppermute | solution.py:345
  67.6 15.5 %collective-permute-start.5 = (bf16[4,400,128]{2,1,0:T(8,128)(2,1)S(1)}, bf16[4,400,128]{2,1,0:T(8,128)(2,1)S(1)}, u32[]{:S(2)}, u32[]{:S(2)}) collective-permute-start(bf16[4,400,128]{2,1,0:T(8,128)(2,1)S(1)} %get-tuple-element.40), channel_id=1, source_target_pairs={{0,3},{32,35},{64,67},{96,99},{8,11},{40,43},{72,75},{104,107},{16... | collective-permute-start | bytes 1228808 | tf_op jit(solution)/shard_map/ppermute | solution.py:345
  70.0 17.4 %collective-permute-start.6 = (bf16[4,400,128]{2,1,0:T(8,128)(2,1)S(1)}, bf16[4,400,128]{2,1,0:T(8,128)(2,1)S(1)}, u32[]{:S(2)}, u32[]{:S(2)}) collective-permute-start(bf16[4,400,128]{2,1,0:T(8,128)(2,1)S(1)} %get-tuple-element.39), channel_id=1, source_target_pairs={{0,3},{32,35},{64,67},{96,99},{8,11},{40,43},{72,75},{104,107},{16... | collective-permute-start | bytes 1228808 | tf_op jit(solution)/shard_map/ppermute | solution.py:345

commit v6 on v5

--- a/solution.py
+++ b/solution.py
@@ -15,7 +15,7 @@
 PEERS = SIDE * SIDE
 CAP = 64
 LANES = 128
-CODE_ROWS = 16
+CODE_ROWS = 8
 HALF = PEERS // 2
 ROWS = 8
 CHUNKS = ((0, 0, 64), (1, 0, 48), (1, 48, 16))

time: 111 us -> 110 us (level)
  no operation moved by 1% of the time
where the time goes in v6:
time: 110 us
  waiting for transfers between devices  42.8 us (39%)
  Pallas kernels  26.5 us (24%)
  starting transfers between devices  23.2 us (21%)
  blocking collectives  15.8 us (14%)
  local copies, waits for them, and re-layouts  1.28 us (1%)
    all_to_all x2, waiting for transfers between devices, to_owner(): return lax.all_to_all(x, AXES, 0, 0, axis_index_groups=groups, tiled=True)  34.3 us
    pallas_call x6, Pallas kernels, score_call(): pl.pallas_call(lambda *refs: scores(names, new, loaded, pairs, state[0] i...  18.7 us
    all_to_all x1, blocking collectives, per_device(): got = lax.all_to_all(state[2], AXES, 0, 0, tiled=True)  15.8 us
    all_to_all x2, starting transfers between devices, to_owner(): return lax.all_to_all(x, AXES, 0, 0, axis_index_groups=groups, tiled=True)  12.4 us
    ppermute x3, starting transfers between devices, per_device(): lax.ppermute(own[start:end], AXES, moves_near)  6.34 us
    pallas_call x1, Pallas kernels, per_device(): pl.pallas_call(prepare, in_specs=[HBM, HBM], out_specs=[VMEM, HBM, HBM],...  4.88 us
    ppermute x3, waiting for transfers between devices, per_device(): lax.ppermute(own[start:end], AXES, moves_near)  3.36 us
    ppermute x1, waiting for transfers between devices, per_device(): held[FAR, 1, 0, PEERS] = lax.ppermute(own, AXES, moves_far)  2.99 us
  transfers between devices with their start and end apart: 10, of which 7 were waited for; matrix products, arithmetic and copies ran while one was open for 0% of the time, Pallas kernels for 16%

profile of v6, /device:TPU:1, one launch (start us, length us, event | category | flops | bytes accessed | tf_op | source)
XLA Modules:
  0.0 109.7 jit_solution(12951583337411819400)
XLA Ops:
  0.0 4.9 %prepare.1 = (s32[4,1024]{1,0:T(4,128)S(1)}, bf16[16,392,128]{2,1,0:T(8,128)(2,1)}, bf16[1024,768]{1,0:T(8,128)(2,1)}) custom-call(s32[1,1024]{1,0:T(1,128)} %bitcast.8, f32[1024,768]{1,0:T(8,128)} %emb_ref.1), custom_call_target="tpu_custom_call" | custom-call | tf_op jit(solution)/shard_map/prepare/pallas_call | solution.py:267
  4.9 1.5 %collective-permute-start.1 = (bf16[1024,768]{1,0:T(8,128)(2,1)}, bf16[1024,768]{1,0:T(8,128)(2,1)S(1)}, u32[]{:S(2)}, u32[]{:S(2)}) collective-permute-start(bf16[1024,768]{1,0:T(8,128)(2,1)} %get-tuple-element.26), channel_id=1, source_target_pairs={{0,4},{4,0},{32,36},{36,32},{64,68},{68,64},{96,100},{100,96},{8,1... | collective-permute-start | bytes 4718600 | tf_op jit(solution)/shard_map/ppermute | solution.py:294
  6.4 7.7 %all-to-all-start = ((bf16[16,392,128]{2,1,0:T(8,128)(2,1)}), bf16[16,392,128]{2,1,0:T(8,128)(2,1)S(1)}, u32[]{:S(2)}, u32[]{:S(2)}) async-start(bf16[16,392,128]{2,1,0:T(8,128)(2,1)} %get-tuple-element.23), calls=%async_computation | async-start | bytes 3211264 | tf_op jit(solution)/shard_map/all_to_all | solution.py:301
  14.6 0.8 collective-permute-done.pos_ref
  15.5 1.9 %place_other.1 = bf16[16,392,128]{2,1,0:T(8,128)(2,1)S(1)} custom-call(s32[4,1024]{1,0:T(4,128)S(1)} %collective-permute-done.pos_ref, bf16[1024,768]{1,0:T(8,128)(2,1)S(1)} %collective-permute-done.1.unit_ref), custom_call_target="tpu_custom_call" | custom-call | tf_op jit(solution)/shard_map/place_other/pallas_call | solution.py:287
  17.4 1.2 %copy-done = bf16[16,392,128]{2,1,0:T(8,128)(2,1)} copy-done((bf16[16,392,128]{2,1,0:T(8,128)(2,1)}, bf16[16,392,128]{2,1,0:T(8,128)(2,1)S(1)}, u32[]{:S(2)}) %copy-start) | copy-done | bytes 1605656
  18.5 17.3 %all-to-all-done.refs_2_ = bf16[16,392,128]{2,1,0:T(8,128)(2,1)S(1)} async-done(((bf16[16,392,128]{2,1,0:T(8,128)(2,1)}), bf16[16,392,128]{2,1,0:T(8,128)(2,1)S(1)}, u32[]{:S(2)}, u32[]{:S(2)}) %all-to-all-start) | async-done | bytes 1605664 | tf_op jit(solution)/shard_map/all_to_all | solution.py:301
  35.9 4.7 %all-to-all-start.1 = ((bf16[16,392,128]{2,1,0:T(8,128)(2,1)}), bf16[16,392,128]{2,1,0:T(8,128)(2,1)S(1)}, u32[]{:S(2)}, u32[]{:S(2)}) async-start(bf16[16,392,128]{2,1,0:T(8,128)(2,1)} %copy-done), calls=%async_computation.1 | async-start | bytes 3211264 | tf_op jit(solution)/shard_map/all_to_all | solution.py:301
  40.6 2.0 %collective-permute-start.2 = (bf16[16,392,128]{2,1,0:T(8,128)(2,1)S(1)}, bf16[16,392,128]{2,1,0:T(8,128)(2,1)}, u32[]{:S(2)}, u32[]{:S(2)}) collective-permute-start(bf16[16,392,128]{2,1,0:T(8,128)(2,1)S(1)} %all-to-all-done.refs_2_), channel_id=1, source_target_pairs={{0,3},{32,35},{64,67},{96,99},{8,11},{40,43},{72,75},{104,107},{16... | collective-permute-start | bytes 4816904 | tf_op jit(solution)/shard_map/ppermute | solution.py:336
  42.5 1.5 %scores_own_first.1 = (f32[8,1024]{1,0:T(8,128)S(1)}, f32[8,1024]{1,0:T(8,128)S(1)}) custom-call(s32[4,1024]{1,0:T(4,128)S(1)} %get-tuple-element.22.refs_0_.refs_1_.pos_ref, s32[4,1024]{1,0:T(4,128)S(1)} %get-tuple-element.22.refs_0_.refs_1_.pos_ref, bf16[16,392,128]{2,1,0:T(8,128)(2,1)S(1)} %all-to-all-done.refs_2_), custom_call_target="tpu_custom_call" | custom-call | tf_op jit(solution)/shard_map/scores_own_first/pallas_call | solution.py:314
  44.1 16.9 %all-to-all-done.1.refs_3_ = bf16[16,392,128]{2,1,0:T(8,128)(2,1)S(1)} async-done(((bf16[16,392,128]{2,1,0:T(8,128)(2,1)}), bf16[16,392,128]{2,1,0:T(8,128)(2,1)S(1)}, u32[]{:S(2)}, u32[]{:S(2)}) %all-to-all-start.1) | async-done | bytes 1605664 | tf_op jit(solution)/shard_map/all_to_all | solution.py:301
  61.5 2.3 %collective-permute-start.4 = (bf16[8,392,128]{2,1,0:T(8,128)(2,1)S(1)}, bf16[8,392,128]{2,1,0:T(8,128)(2,1)S(1)}, u32[]{:S(2)}, u32[]{:S(2)}) collective-permute-start(bf16[8,392,128]{2,1,0:T(8,128)(2,1)S(1)} %slice.9), channel_id=1, source_target_pairs={{0,3},{32,35},{64,67},{96,99},{8,11},{40,43},{72,75},{104,107},{16... | collective-permute-start | bytes 2408456 | tf_op jit(solution)/shard_map/ppermute | solution.py:345
  63.8 3.2 %scores_own.1 = (f32[8,1024]{1,0:T(8,128)S(1)}, f32[8,1024]{1,0:T(8,128)S(1)}) custom-call(f32[8,1024]{1,0:T(8,128)S(1)} %get-tuple-element.24.refs_0_, f32[8,1024]{1,0:T(8,128)S(1)} %get-tuple-element.25.refs_1_, bf16[16,392,128]{2,1,0:T(8,128)(2,1)S(1)} %all-to-all-done.refs_2_, bf16[16,392,128]{2,1,0:T(8,128)(2,1)S(1)} %all-to-all-done.1.refs_3_), custom_call_target="tpu_custom_call" | custom-call | tf_op jit(solution)/shard_map/scores_own/pallas_call | solution.py:314
  67.0 1.0 collective-permute-start.5
  68.0 1.3 %collective-permute-done.2.refs_4_ = bf16[16,392,128]{2,1,0:T(8,128)(2,1)} collective-permute-done((bf16[16,392,128]{2,1,0:T(8,128)(2,1)S(1)}, bf16[16,392,128]{2,1,0:T(8,128)(2,1)}, u32[]{:S(2)}, u32[]{:S(2)}) %collective-permute-start.2) | collective-permute-done | bytes 1605664 | tf_op jit(solution)/shard_map/ppermute | solution.py:336
  69.3 3.1 %collective-permute-start.6 = (bf16[4,392,128]{2,1,0:T(8,128)(2,1)S(1)}, bf16[4,392,128]{2,1,0:T(8,128)(2,1)S(1)}, u32[]{:S(2)}, u32[]{:S(2)}) collective-permute-start(bf16[4,392,128]{2,1,0:T(8,128)(2,1)S(1)} %get-tuple-element.39), channel_id=1, source_target_pairs={{0,3},{32,35},{64,67},{96,99},{8,11},{40,43},{72,75},{104,107},{16... | collective-permute-start | bytes 1204232 | tf_op jit(solution)/shard_map/ppermute | solution.py:345
  72.4 6.3 %scores_near_first.1 = (f32[8,1024]{1,0:T(8,128)S(1)}, f32[8,1024]{1,0:T(8,128)S(1)}, bf16[16,392,128]{2,1,0:T(8,128)(2,1)S(1)}) custom-call(f32[8,1024]{1,0:T(8,128)S(1)} %get-tuple-element.27.refs_0_, f32[8,1024]{1,0:T(8,128)S(1)} %get-tuple-element.28.refs_1_, bf16[16,392,128]{2,1,0:T(8,128)(2,1)S(1)} %all-to-all-done.refs_2_, ...), custom_call_target="tpu_custom_call" | custom-call | tf_op jit(solution)/shard_map/scores_near_first/pallas_call | solution.py:314
  78.7 2.8 %scores_near_0.1 = (f32[8,1024]{1,0:T(8,128)S(1)}, f32[8,1024]{1,0:T(8,128)S(1)}) custom-call(f32[8,1024]{1,0:T(8,128)S(1)} %get-tuple-element.29.refs_0_, f32[8,1024]{1,0:T(8,128)S(1)} %get-tuple-element.30.refs_1_, bf16[16,392,128]{2,1,0:T(8,128)(2,1)S(1)} %all-to-all-done.refs_2_, bf16[16,392,128]{2,1,0:T(8,128)(2,1)S(1)} %all-to-all-done.1.refs_3_, ...), custom_call_target="tpu_custom_call" | custom-call | tf_op jit(solution)/shard_map/scores_near_0/pallas_call | solution.py:314
  82.1 1.5 %scores_near_8.1 = (f32[8,1024]{1,0:T(8,128)S(1)}, f32[8,1024]{1,0:T(8,128)S(1)}) custom-call(f32[8,1024]{1,0:T(8,128)S(1)} %get-tuple-element.33.refs_0_, f32[8,1024]{1,0:T(8,128)S(1)} %get-tuple-element.34.refs_1_, bf16[16,392,128]{2,1,0:T(8,128)(2,1)S(1)} %all-to-all-done.refs_2_, bf16[16,392,128]{2,1,0:T(8,128)(2,1)S(1)} %all-to-all-done.1.refs_3_, ...), custom_call_target="tpu_custom_call" | custom-call | tf_op jit(solution)/shard_map/scores_near_8/pallas_call | solution.py:314
  83.6 2.8 %collective-permute-done.6.refs_6_ = bf16[4,392,128]{2,1,0:T(8,128)(2,1)S(1)} collective-permute-done((bf16[4,392,128]{2,1,0:T(8,128)(2,1)S(1)}, bf16[4,392,128]{2,1,0:T(8,128)(2,1)S(1)}, u32[]{:S(2)}, u32[]{:S(2)}) %collective-permute-start.6) | collective-permute-done | bytes 401440 | tf_op jit(solution)/shard_map/ppermute | solution.py:345
  86.4 3.0 %collective-permute-done.7.refs_8_ = bf16[16,392,128]{2,1,0:T(8,128)(2,1)S(1)} collective-permute-done((bf16[16,392,128]{2,1,0:T(8,128)(2,1)S(1)}, bf16[16,392,128]{2,1,0:T(8,128)(2,1)S(1)}, u32[]{:S(2)}, u32[]{:S(2)}) %collective-permute-start.7) | collective-permute-done | bytes 1605664 | tf_op jit(solution)/shard_map/ppermute | solution.py:347
  89.4 3.4 %scores_near_12.1 = (f32[8,1024]{1,0:T(8,128)}, f32[8,1024]{1,0:T(8,128)}, f32[128,64]{1,0:T(8,128)S(1)}) custom-call(f32[8,1024]{1,0:T(8,128)S(1)} %get-tuple-element.36.refs_0_, f32[8,1024]{1,0:T(8,128)S(1)} %get-tuple-element.37.refs_1_, bf16[16,392,128]{2,1,0:T(8,128)(2,1)S(1)} %all-to-all-done.refs_2_, ...), custom_call_target="tpu_custom_call" | custom-call | tf_op jit(solution)/shard_map/scores_near_12/pallas_call | solution.py:314
  92.8 15.8 %all_to_all.21 = f32[128,1,64]{2,1,0:T(1,128)S(1)} all-to-all(f32[128,1,64]{2,1,0:T(1,128)S(1)} %bitcast.7), channel_id=1, replica_groups=mesh['docs'=32,'split'=4] {'docs','split'}, dimensions={0} | all-to-all | bytes 65536 | tf_op jit(solution)/shard_map/all_to_all | solution.py:368
  108.6 1.0 finish.1
  (10 shorter events, 1.7 us)
Async XLA Ops:
  4.9 10.6 %collective-permute-start.1 = (bf16[1024,768]{1,0:T(8,128)(2,1)}, bf16[1024,768]{1,0:T(8,128)(2,1)S(1)}, u32[]{:S(2)}, u32[]{:S(2)}) collective-permute-start(bf16[1024,768]{1,0:T(8,128)(2,1)} %get-tuple-element.26), channel_id=1, source_target_pairs={{0,4},{4,0},{32,36},{36,32},{64,68},{68,64},{96,100},{100,96},{8,1... | collective-permute-start | bytes 4718600 | tf_op jit(solution)/shard_map/ppermute | solution.py:294
  6.4 29.5 %all-to-all-start = ((bf16[16,392,128]{2,1,0:T(8,128)(2,1)}), bf16[16,392,128]{2,1,0:T(8,128)(2,1)S(1)}, u32[]{:S(2)}, u32[]{:S(2)}) async-start(bf16[16,392,128]{2,1,0:T(8,128)(2,1)} %get-tuple-element.23), calls=%async_computation | async-start | bytes 3211264 | tf_op jit(solution)/shard_map/all_to_all | solution.py:301
  14.1 1.4 %collective-permute-start = (s32[4,1024]{1,0:T(4,128)S(1)}, s32[4,1024]{1,0:T(4,128)S(1)}, u32[]{:S(2)}, u32[]{:S(2)}) collective-permute-start(s32[4,1024]{1,0:T(4,128)S(1)} %get-tuple-element.22.refs_0_.refs_1_.pos_ref), channel_id=1, source_target_pairs={{0,4},{4,0},{32,36},{36,32},{64,68},{68,64},{96,100},{100,96},{8,1... | collective-permute-start | bytes 49160 | tf_op jit(solution)/shard_map/ppermute | solution.py:294
  17.4 1.2 %copy-start = (bf16[16,392,128]{2,1,0:T(8,128)(2,1)}, bf16[16,392,128]{2,1,0:T(8,128)(2,1)S(1)}, u32[]{:S(2)}) copy-start(bf16[16,392,128]{2,1,0:T(8,128)(2,1)S(1)} %place_other.1) | copy-start | bytes 4816900
  35.9 25.1 %all-to-all-start.1 = ((bf16[16,392,128]{2,1,0:T(8,128)(2,1)}), bf16[16,392,128]{2,1,0:T(8,128)(2,1)S(1)}, u32[]{:S(2)}, u32[]{:S(2)}) async-start(bf16[16,392,128]{2,1,0:T(8,128)(2,1)} %copy-done), calls=%async_computation.1 | async-start | bytes 3211264 | tf_op jit(solution)/shard_map/all_to_all | solution.py:301
  40.6 28.7 %collective-permute-start.2 = (bf16[16,392,128]{2,1,0:T(8,128)(2,1)S(1)}, bf16[16,392,128]{2,1,0:T(8,128)(2,1)}, u32[]{:S(2)}, u32[]{:S(2)}) collective-permute-start(bf16[16,392,128]{2,1,0:T(8,128)(2,1)S(1)} %all-to-all-done.refs_2_), channel_id=1, source_target_pairs={{0,3},{32,35},{64,67},{96,99},{8,11},{40,43},{72,75},{104,107},{16... | collective-permute-start | bytes 4816904 | tf_op jit(solution)/shard_map/ppermute | solution.py:336
  42.5 29.8 %collective-permute-start.3 = (bf16[16,392,128]{2,1,0:T(8,128)(2,1)S(1)}, bf16[16,392,128]{2,1,0:T(8,128)(2,1)}, u32[]{:S(2)}, u32[]{:S(2)}) collective-permute-start(bf16[16,392,128]{2,1,0:T(8,128)(2,1)S(1)} %all-to-all-done.refs_2_), channel_id=1, source_target_pairs={{0,1},{32,33},{64,65},{96,97},{8,9},{40,41},{72,73},{104,105},{16,... | collective-permute-start | bytes 4816904 | tf_op jit(solution)/shard_map/ppermute | solution.py:337
  61.0 28.4 %collective-permute-start.7 = (bf16[16,392,128]{2,1,0:T(8,128)(2,1)S(1)}, bf16[16,392,128]{2,1,0:T(8,128)(2,1)S(1)}, u32[]{:S(2)}, u32[]{:S(2)}) collective-permute-start(bf16[16,392,128]{2,1,0:T(8,128)(2,1)S(1)} %all-to-all-done.1.refs_3_), channel_id=1, source_target_pairs={{0,1},{32,33},{64,65},{96,97},{8,9},{40,41},{72,73},{104,105},{16,... | collective-permute-start | bytes 4816904 | tf_op jit(solution)/shard_map/ppermute | solution.py:347
  61.5 17.2 %collective-permute-start.4 = (bf16[8,392,128]{2,1,0:T(8,128)(2,1)S(1)}, bf16[8,392,128]{2,1,0:T(8,128)(2,1)S(1)}, u32[]{:S(2)}, u32[]{:S(2)}) collective-permute-start(bf16[8,392,128]{2,1,0:T(8,128)(2,1)S(1)} %slice.9), channel_id=1, source_target_pairs={{0,3},{32,35},{64,67},{96,99},{8,11},{40,43},{72,75},{104,107},{16... | collective-permute-start | bytes 2408456 | tf_op jit(solution)/shard_map/ppermute | solution.py:345
  67.0 15.1 %collective-permute-start.5 = (bf16[4,392,128]{2,1,0:T(8,128)(2,1)S(1)}, bf16[4,392,128]{2,1,0:T(8,128)(2,1)S(1)}, u32[]{:S(2)}, u32[]{:S(2)}) collective-permute-start(bf16[4,392,128]{2,1,0:T(8,128)(2,1)S(1)} %get-tuple-element.40), channel_id=1, source_target_pairs={{0,3},{32,35},{64,67},{96,99},{8,11},{40,43},{72,75},{104,107},{16... | collective-permute-start | bytes 1204232 | tf_op jit(solution)/shard_map/ppermute | solution.py:345
  69.3 17.1 %collective-permute-start.6 = (bf16[4,392,128]{2,1,0:T(8,128)(2,1)S(1)}, bf16[4,392,128]{2,1,0:T(8,128)(2,1)S(1)}, u32[]{:S(2)}, u32[]{:S(2)}) collective-permute-start(bf16[4,392,128]{2,1,0:T(8,128)(2,1)S(1)} %get-tuple-element.39), channel_id=1, source_target_pairs={{0,3},{32,35},{64,67},{96,99},{8,11},{40,43},{72,75},{104,107},{16... | collective-permute-start | bytes 1204232 | tf_op jit(solution)/shard_map/ppermute | solution.py:345

commit v7 on v6

--- a/solution.py
+++ b/solution.py
@@ -340,31 +340,37 @@
     whole_1 = (OWN, 1, 0, PEERS)
     held[whole_1] = own
     own = after(own, state[0])
-    parts = ((0, 8), (8, 12), (12, 16))
-    for start, end in parts:
+    parts = ((0, 12), (12, 16))
+    for number, (start, end) in enumerate(parts):
         held[NEAR, 1, start, end - start] = lax.ppermute(own[start:end], AXES, moves_near)
+        half = (1 - number) * HALF
+        held[FAR, 1, half, HALF] = lax.ppermute(own[half : half + HALF], AXES, moves_far)
         if not start:
-            held[FAR, 1, 0, PEERS] = lax.ppermute(own, AXES, moves_far)
             state = score_call(state, (whole_1,), [every(own_0, own_1) + every(own_1, own_1)], "scores_own")
             own = after(own, state[0])
     state = score_call(
         state,
         whole_0[1:],
-        [every(own_0 + own_1, near_0), every(near_0[:1], far_0, HEAVY) + every(near_0, far_0[1:], LIGHT)],
+        [
+            every(own_0 + own_1, near_0),
+            every(own_1, far_0) + every(near_0[:1], far_0, HEAVY) + every(near_0, far_0[1:], LIGHT),
+        ],
         "scores_near_first",
         whole_0[1:],
     )
-    for start, end in parts:
+    older, (far_a, far_b) = [], blocks(FAR, 1)
+    for number, (start, end) in enumerate(parts):
         near = blocks(NEAR, 1, start, end)
+        older += near
         new = ((NEAR, 1, start, end - start),)
-        pairs = [every(own_0 + own_1, near) + every(near, far_0)]
-        if end == PEERS:
-            new += ((FAR, 1, 0, PEERS),)
-            older = [block for part in parts for block in blocks(NEAR, 1, *part)]
-            far_1 = blocks(FAR, 1)
-            first_half = [block for block in older if block[2] < HALF]
-            pairs.append(every(first_half, far_1, HEAVY) + every(older, far_1[1:], LIGHT))
-        state = score_call(state, new, pairs, f"scores_near_{start}", (), end == PEERS)
+        pairs = every(own_1, near) + every(near, far_0)
+        if not start:
+            new += (far_b,)
+            pairs += every([b for b in older if b[2] < HALF], [far_b], HEAVY) + every(older, [far_b], LIGHT)
+        else:
+            new += (far_a,)
+            pairs += every([b for b in older if b[2] < HALF], [far_a], HEAVY) + every(near, [far_b], LIGHT)
+        state = score_call(state, new, [pairs], f"scores_near_{start}", last=end == PEERS)
     got = lax.all_to_all(state[2], AXES, 0, 0, tiled=True)
     out = pl.pallas_call(
         finish,

time: 110 us -> 109 us (level)
  starting transfers between devices: 23.2 us -> 21.8 us
    ppermute x3 -> x2, waiting for transfers between devices: 3.36 us -> 2.01 us  [per_device(): lax.ppermute(own[start:end], AXES, moves_near)]
    ppermute x1, waiting for transfers between devices: 1.3 us -> 2.54 us  [per_device(): held[whole_0[1]] = lax.ppermute(own, AXES, moves_near)]
    ppermute x3 -> x2, starting transfers between devices: 6.34 us -> 5.26 us  [per_device(): lax.ppermute(own[start:end], AXES, moves_near)]
    ppermute x1 -> x2, waiting for transfers between devices: 2.99 us -> 3.41 us  [per_device(): lax.ppermute(own[half:half + HALF], AXES, moves_far)]
    pallas_call x6 -> x5, Pallas kernels: 18.7 us -> 18.9 us  [score_call(): pl.pallas_call(lambda *refs: scores(names, new, loaded, pairs, state[0] i...]
  transfers between devices with their start and end apart: 10 -> 10, of which waited for: 7 -> 8; matrix products, arithmetic and copies ran while one was open for 0% -> 0% of each run, Pallas kernels for 16% -> 17%
where the time goes in v7:
time: 109 us
  waiting for transfers between devices  43.1 us (40%)
  Pallas kernels  26.7 us (24%)
  starting transfers between devices  21.8 us (20%)
  blocking collectives  15.6 us (14%)
  local copies, waits for them, and re-layouts  1.4 us (1%)
    all_to_all x2, waiting for transfers between devices, to_owner(): return lax.all_to_all(x, AXES, 0, 0, axis_index_groups=groups, tiled=True)  34.3 us
    pallas_call x5, Pallas kernels, score_call(): pl.pallas_call(lambda *refs: scores(names, new, loaded, pairs, state[0] i...  18.9 us
    all_to_all x1, blocking collectives, per_device(): got = lax.all_to_all(state[2], AXES, 0, 0, tiled=True)  15.6 us
    all_to_all x2, starting transfers between devices, to_owner(): return lax.all_to_all(x, AXES, 0, 0, axis_index_groups=groups, tiled=True)  12.4 us
    ppermute x2, starting transfers between devices, per_device(): lax.ppermute(own[start:end], AXES, moves_near)  5.26 us
    pallas_call x1, Pallas kernels, per_device(): pl.pallas_call(prepare, in_specs=[HBM, HBM], out_specs=[VMEM, HBM, HBM],...  4.88 us
    ppermute x2, waiting for transfers between devices, per_device(): lax.ppermute(own[half:half + HALF], AXES, moves_far)  3.41 us
    ppermute x1, waiting for transfers between devices, per_device(): held[whole_0[1]] = lax.ppermute(own, AXES, moves_near)  2.54 us
  transfers between devices with their start and end apart: 10, of which 8 were waited for; matrix products, arithmetic and copies ran while one was open for 0% of the time, Pallas kernels for 17%

profile of v7, /device:TPU:1, one launch (start us, length us, event | category | flops | bytes accessed | tf_op | source)
XLA Modules:
  0.0 108.7 jit_solution(17871960303998610447)
XLA Ops:
  0.0 4.9 %prepare.1 = (s32[4,1024]{1,0:T(4,128)S(1)}, bf16[16,392,128]{2,1,0:T(8,128)(2,1)}, bf16[1024,768]{1,0:T(8,128)(2,1)}) custom-call(s32[1,1024]{1,0:T(1,128)} %bitcast.8, f32[1024,768]{1,0:T(8,128)} %emb_ref.1), custom_call_target="tpu_custom_call" | custom-call | tf_op jit(solution)/shard_map/prepare/pallas_call | solution.py:267
  4.9 1.5 %collective-permute-start.1 = (bf16[1024,768]{1,0:T(8,128)(2,1)}, bf16[1024,768]{1,0:T(8,128)(2,1)S(1)}, u32[]{:S(2)}, u32[]{:S(2)}) collective-permute-start(bf16[1024,768]{1,0:T(8,128)(2,1)} %get-tuple-element.24), channel_id=1, source_target_pairs={{0,4},{4,0},{32,36},{36,32},{64,68},{68,64},{96,100},{100,96},{8,1... | collective-permute-start | bytes 4718600 | tf_op jit(solution)/shard_map/ppermute | solution.py:294
  6.4 7.7 %all-to-all-start = ((bf16[16,392,128]{2,1,0:T(8,128)(2,1)}), bf16[16,392,128]{2,1,0:T(8,128)(2,1)S(1)}, u32[]{:S(2)}, u32[]{:S(2)}) async-start(bf16[16,392,128]{2,1,0:T(8,128)(2,1)} %get-tuple-element.21), calls=%async_computation | async-start | bytes 3211264 | tf_op jit(solution)/shard_map/all_to_all | solution.py:301
  14.1 0.6 collective-permute-start
  14.6 0.8 collective-permute-done.pos_ref
  15.5 1.9 %place_other.1 = bf16[16,392,128]{2,1,0:T(8,128)(2,1)S(1)} custom-call(s32[4,1024]{1,0:T(4,128)S(1)} %collective-permute-done.pos_ref, bf16[1024,768]{1,0:T(8,128)(2,1)S(1)} %collective-permute-done.1.unit_ref), custom_call_target="tpu_custom_call" | custom-call | tf_op jit(solution)/shard_map/place_other/pallas_call | solution.py:287
  17.4 1.2 %copy-done = bf16[16,392,128]{2,1,0:T(8,128)(2,1)} copy-done((bf16[16,392,128]{2,1,0:T(8,128)(2,1)}, bf16[16,392,128]{2,1,0:T(8,128)(2,1)S(1)}, u32[]{:S(2)}) %copy-start) | copy-done | bytes 1605656
  18.5 17.3 %all-to-all-done.refs_2_ = bf16[16,392,128]{2,1,0:T(8,128)(2,1)S(1)} async-done(((bf16[16,392,128]{2,1,0:T(8,128)(2,1)}), bf16[16,392,128]{2,1,0:T(8,128)(2,1)S(1)}, u32[]{:S(2)}, u32[]{:S(2)}) %all-to-all-start) | async-done | bytes 1605664 | tf_op jit(solution)/shard_map/all_to_all | solution.py:301
  35.9 4.7 %all-to-all-start.1 = ((bf16[16,392,128]{2,1,0:T(8,128)(2,1)}), bf16[16,392,128]{2,1,0:T(8,128)(2,1)S(1)}, u32[]{:S(2)}, u32[]{:S(2)}) async-start(bf16[16,392,128]{2,1,0:T(8,128)(2,1)} %copy-done), calls=%async_computation.1 | async-start | bytes 3211264 | tf_op jit(solution)/shard_map/all_to_all | solution.py:301
  40.6 2.0 %collective-permute-start.2 = (bf16[16,392,128]{2,1,0:T(8,128)(2,1)S(1)}, bf16[16,392,128]{2,1,0:T(8,128)(2,1)}, u32[]{:S(2)}, u32[]{:S(2)}) collective-permute-start(bf16[16,392,128]{2,1,0:T(8,128)(2,1)S(1)} %all-to-all-done.refs_2_), channel_id=1, source_target_pairs={{0,3},{32,35},{64,67},{96,99},{8,11},{40,43},{72,75},{104,107},{16... | collective-permute-start | bytes 4816904 | tf_op jit(solution)/shard_map/ppermute | solution.py:336
  42.5 1.5 %scores_own_first.1 = (f32[8,1024]{1,0:T(8,128)S(1)}, f32[8,1024]{1,0:T(8,128)S(1)}) custom-call(s32[4,1024]{1,0:T(4,128)S(1)} %get-tuple-element.20.refs_0_.refs_1_.pos_ref, s32[4,1024]{1,0:T(4,128)S(1)} %get-tuple-element.20.refs_0_.refs_1_.pos_ref, bf16[16,392,128]{2,1,0:T(8,128)(2,1)S(1)} %all-to-all-done.refs_2_), custom_call_target="tpu_custom_call" | custom-call | tf_op jit(solution)/shard_map/scores_own_first/pallas_call | solution.py:314
  44.0 17.0 %all-to-all-done.1.refs_3_.refs_2_ = bf16[16,392,128]{2,1,0:T(8,128)(2,1)S(1)} async-done(((bf16[16,392,128]{2,1,0:T(8,128)(2,1)}), bf16[16,392,128]{2,1,0:T(8,128)(2,1)S(1)}, u32[]{:S(2)}, u32[]{:S(2)}) %all-to-all-start.1) | async-done | bytes 1605664 | tf_op jit(solution)/shard_map/all_to_all | solution.py:301
  61.1 2.2 %collective-permute-start.4 = (bf16[12,392,128]{2,1,0:T(8,128)(2,1)S(1)}, bf16[12,392,128]{2,1,0:T(8,128)(2,1)S(1)}, u32[]{:S(2)}, u32[]{:S(2)}) collective-permute-start(bf16[12,392,128]{2,1,0:T(8,128)(2,1)S(1)} %slice.12), channel_id=1, source_target_pairs={{0,3},{32,35},{64,67},{96,99},{8,11},{40,43},{72,75},{104,107},{16... | collective-permute-start | bytes 3612680 | tf_op jit(solution)/shard_map/ppermute | solution.py:345
  63.4 3.2 %scores_own.1 = (f32[8,1024]{1,0:T(8,128)S(1)}, f32[8,1024]{1,0:T(8,128)S(1)}) custom-call(f32[8,1024]{1,0:T(8,128)S(1)} %get-tuple-element.22.refs_0_, f32[8,1024]{1,0:T(8,128)S(1)} %get-tuple-element.23.refs_1_, bf16[16,392,128]{2,1,0:T(8,128)(2,1)S(1)} %all-to-all-done.refs_2_, bf16[16,392,128]{2,1,0:T(8,128)(2,1)S(1)} %all-to-all-done.1.refs_3_.refs_2_), custom_call_target="tpu_custom_call" | custom-call | tf_op jit(solution)/shard_map/scores_own/pallas_call | solution.py:314
  66.7 2.5 %collective-permute-done.2.refs_4_ = bf16[16,392,128]{2,1,0:T(8,128)(2,1)} collective-permute-done((bf16[16,392,128]{2,1,0:T(8,128)(2,1)S(1)}, bf16[16,392,128]{2,1,0:T(8,128)(2,1)}, u32[]{:S(2)}, u32[]{:S(2)}) %collective-permute-start.2) | collective-permute-done | bytes 1605664 | tf_op jit(solution)/shard_map/ppermute | solution.py:336
  69.3 3.1 %collective-permute-start.6 = (bf16[4,392,128]{2,1,0:T(8,128)(2,1)S(1)}, bf16[4,392,128]{2,1,0:T(8,128)(2,1)S(1)}, u32[]{:S(2)}, u32[]{:S(2)}) collective-permute-start(bf16[4,392,128]{2,1,0:T(8,128)(2,1)S(1)} %slice.14), channel_id=1, source_target_pairs={{0,3},{32,35},{64,67},{96,99},{8,11},{40,43},{72,75},{104,107},{16... | collective-permute-start | bytes 1204232 | tf_op jit(solution)/shard_map/ppermute | solution.py:345
  72.4 8.2 %scores_near_first.1 = (f32[8,1024]{1,0:T(8,128)S(1)}, f32[8,1024]{1,0:T(8,128)S(1)}, bf16[16,392,128]{2,1,0:T(8,128)(2,1)S(1)}) custom-call(f32[8,1024]{1,0:T(8,128)S(1)} %get-tuple-element.25.refs_0_, f32[8,1024]{1,0:T(8,128)S(1)} %get-tuple-element.26.refs_1_, bf16[16,392,128]{2,1,0:T(8,128)(2,1)S(1)} %all-to-all-done.refs_2_, ...), custom_call_target="tpu_custom_call" | custom-call | tf_op jit(solution)/shard_map/scores_near_first/pallas_call | solution.py:314
  80.9 1.2 %collective-permute-done.4.refs_3_ = bf16[12,392,128]{2,1,0:T(8,128)(2,1)S(1)} collective-permute-done((bf16[12,392,128]{2,1,0:T(8,128)(2,1)S(1)}, bf16[12,392,128]{2,1,0:T(8,128)(2,1)S(1)}, u32[]{:S(2)}, u32[]{:S(2)}) %collective-permute-start.4) | collective-permute-done | bytes 1204256 | tf_op jit(solution)/shard_map/ppermute | solution.py:345
  82.1 3.5 %scores_near_0.1 = (f32[8,1024]{1,0:T(8,128)S(1)}, f32[8,1024]{1,0:T(8,128)S(1)}) custom-call(f32[8,1024]{1,0:T(8,128)S(1)} %get-tuple-element.27.refs_0_, f32[8,1024]{1,0:T(8,128)S(1)} %get-tuple-element.28.refs_1_, bf16[16,392,128]{2,1,0:T(8,128)(2,1)S(1)} %all-to-all-done.1.refs_3_.refs_2_, bf16[12,392,128]{2,1,0:T(8,128)(2,1)S(1)} %collective-permute-done.4.refs_3_, ...), custom_call_target="tpu_custom_call" | custom-call | tf_op jit(solution)/shard_map/scores_near_0/pallas_call | solution.py:314
  85.6 0.8 collective-permute-done.6.refs_4_
  86.4 3.1 %collective-permute-done.7.refs_6_ = bf16[8,392,128]{2,1,0:T(8,128)(2,1)S(1)} collective-permute-done((bf16[8,392,128]{2,1,0:T(8,128)(2,1)S(1)}, bf16[8,392,128]{2,1,0:T(8,128)(2,1)S(1)}, u32[]{:S(2)}, u32[]{:S(2)}) %collective-permute-start.7) | collective-permute-done | bytes 802848 | tf_op jit(solution)/shard_map/ppermute | solution.py:347
  89.5 2.6 %scores_near_12.1 = (f32[8,1024]{1,0:T(8,128)}, f32[8,1024]{1,0:T(8,128)}, f32[128,64]{1,0:T(8,128)S(1)}) custom-call(f32[8,1024]{1,0:T(8,128)S(1)} %get-tuple-element.31.refs_0_, f32[8,1024]{1,0:T(8,128)S(1)} %get-tuple-element.32.refs_1_, bf16[16,392,128]{2,1,0:T(8,128)(2,1)S(1)} %all-to-all-done.1.refs_3_.refs_2_, ...), custom_call_target="tpu_custom_call" | custom-call | tf_op jit(solution)/shard_map/scores_near_12/pallas_call | solution.py:314
  92.1 15.6 %all_to_all.21 = f32[128,1,64]{2,1,0:T(1,128)S(1)} all-to-all(f32[128,1,64]{2,1,0:T(1,128)S(1)} %bitcast.7), channel_id=1, replica_groups=mesh['docs'=32,'split'=4] {'docs','split'}, dimensions={0} | all-to-all | bytes 65536 | tf_op jit(solution)/shard_map/all_to_all | solution.py:374
  107.6 1.0 finish.1
  (11 shorter events, 0.7 us)
Async XLA Ops:
  4.9 10.6 %collective-permute-start.1 = (bf16[1024,768]{1,0:T(8,128)(2,1)}, bf16[1024,768]{1,0:T(8,128)(2,1)S(1)}, u32[]{:S(2)}, u32[]{:S(2)}) collective-permute-start(bf16[1024,768]{1,0:T(8,128)(2,1)} %get-tuple-element.24), channel_id=1, source_target_pairs={{0,4},{4,0},{32,36},{36,32},{64,68},{68,64},{96,100},{100,96},{8,1... | collective-permute-start | bytes 4718600 | tf_op jit(solution)/shard_map/ppermute | solution.py:294
  6.4 29.5 %all-to-all-start = ((bf16[16,392,128]{2,1,0:T(8,128)(2,1)}), bf16[16,392,128]{2,1,0:T(8,128)(2,1)S(1)}, u32[]{:S(2)}, u32[]{:S(2)}) async-start(bf16[16,392,128]{2,1,0:T(8,128)(2,1)} %get-tuple-element.21), calls=%async_computation | async-start | bytes 3211264 | tf_op jit(solution)/shard_map/all_to_all | solution.py:301
  14.1 1.4 %collective-permute-start = (s32[4,1024]{1,0:T(4,128)S(1)}, s32[4,1024]{1,0:T(4,128)S(1)}, u32[]{:S(2)}, u32[]{:S(2)}) collective-permute-start(s32[4,1024]{1,0:T(4,128)S(1)} %get-tuple-element.20.refs_0_.refs_1_.pos_ref), channel_id=1, source_target_pairs={{0,4},{4,0},{32,36},{36,32},{64,68},{68,64},{96,100},{100,96},{8,1... | collective-permute-start | bytes 49160 | tf_op jit(solution)/shard_map/ppermute | solution.py:294
  17.4 1.2 %copy-start = (bf16[16,392,128]{2,1,0:T(8,128)(2,1)}, bf16[16,392,128]{2,1,0:T(8,128)(2,1)S(1)}, u32[]{:S(2)}) copy-start(bf16[16,392,128]{2,1,0:T(8,128)(2,1)S(1)} %place_other.1) | copy-start | bytes 4816900
  35.9 25.1 %all-to-all-start.1 = ((bf16[16,392,128]{2,1,0:T(8,128)(2,1)}), bf16[16,392,128]{2,1,0:T(8,128)(2,1)S(1)}, u32[]{:S(2)}, u32[]{:S(2)}) async-start(bf16[16,392,128]{2,1,0:T(8,128)(2,1)} %copy-done), calls=%async_computation.1 | async-start | bytes 3211264 | tf_op jit(solution)/shard_map/all_to_all | solution.py:301
  40.6 28.7 %collective-permute-start.2 = (bf16[16,392,128]{2,1,0:T(8,128)(2,1)S(1)}, bf16[16,392,128]{2,1,0:T(8,128)(2,1)}, u32[]{:S(2)}, u32[]{:S(2)}) collective-permute-start(bf16[16,392,128]{2,1,0:T(8,128)(2,1)S(1)} %all-to-all-done.refs_2_), channel_id=1, source_target_pairs={{0,3},{32,35},{64,67},{96,99},{8,11},{40,43},{72,75},{104,107},{16... | collective-permute-start | bytes 4816904 | tf_op jit(solution)/shard_map/ppermute | solution.py:336
  42.5 29.8 %collective-permute-start.3 = (bf16[16,392,128]{2,1,0:T(8,128)(2,1)S(1)}, bf16[16,392,128]{2,1,0:T(8,128)(2,1)}, u32[]{:S(2)}, u32[]{:S(2)}) collective-permute-start(bf16[16,392,128]{2,1,0:T(8,128)(2,1)S(1)} %all-to-all-done.refs_2_), channel_id=1, source_target_pairs={{0,1},{32,33},{64,65},{96,97},{8,9},{40,41},{72,73},{104,105},{16,... | collective-permute-start | bytes 4816904 | tf_op jit(solution)/shard_map/ppermute | solution.py:337
  61.1 21.0 %collective-permute-start.4 = (bf16[12,392,128]{2,1,0:T(8,128)(2,1)S(1)}, bf16[12,392,128]{2,1,0:T(8,128)(2,1)S(1)}, u32[]{:S(2)}, u32[]{:S(2)}) collective-permute-start(bf16[12,392,128]{2,1,0:T(8,128)(2,1)S(1)} %slice.12), channel_id=1, source_target_pairs={{0,3},{32,35},{64,67},{96,99},{8,11},{40,43},{72,75},{104,107},{16... | collective-permute-start | bytes 3612680 | tf_op jit(solution)/shard_map/ppermute | solution.py:345
  63.3 17.5 %collective-permute-start.5 = (bf16[8,392,128]{2,1,0:T(8,128)(2,1)S(1)}, bf16[8,392,128]{2,1,0:T(8,128)(2,1)S(1)}, u32[]{:S(2)}, u32[]{:S(2)}) collective-permute-start(bf16[8,392,128]{2,1,0:T(8,128)(2,1)S(1)} %slice.13), channel_id=1, source_target_pairs={{0,1},{32,33},{64,65},{96,97},{8,9},{40,41},{72,73},{104,105},{16,... | collective-permute-start | bytes 2408456 | tf_op jit(solution)/shard_map/ppermute | solution.py:347
  66.6 22.8 %collective-permute-start.7 = (bf16[8,392,128]{2,1,0:T(8,128)(2,1)S(1)}, bf16[8,392,128]{2,1,0:T(8,128)(2,1)S(1)}, u32[]{:S(2)}, u32[]{:S(2)}) collective-permute-start(bf16[8,392,128]{2,1,0:T(8,128)(2,1)S(1)} %slice.15), channel_id=1, source_target_pairs={{0,1},{32,33},{64,65},{96,97},{8,9},{40,41},{72,73},{104,105},{16,... | collective-permute-start | bytes 2408456 | tf_op jit(solution)/shard_map/ppermute | solution.py:347
  69.3 17.1 %collective-permute-start.6 = (bf16[4,392,128]{2,1,0:T(8,128)(2,1)S(1)}, bf16[4,392,128]{2,1,0:T(8,128)(2,1)S(1)}, u32[]{:S(2)}, u32[]{:S(2)}) collective-permute-start(bf16[4,392,128]{2,1,0:T(8,128)(2,1)S(1)} %slice.14), channel_id=1, source_target_pairs={{0,3},{32,35},{64,67},{96,99},{8,11},{40,43},{72,75},{104,107},{16... | collective-permute-start | bytes 1204232 | tf_op jit(solution)/shard_map/ppermute | solution.py:345

commit v8 on v7

--- a/solution.py
+++ b/solution.py
@@ -157,6 +157,8 @@
 def scores(names, new, loaded, pairs, fresh, last, best_in_ref, codes_in_ref, *refs):
     arrays = dict(zip(names, refs[: len(names)]))
     refs = list(refs[len(names) :])
+    if last:
+        refs = [*refs[1:3], refs[0]]
     best_ref, codes_ref = refs[:2]
     copies = {}
     for number, name in enumerate(loaded):
@@ -306,17 +308,15 @@
         names = sorted({holder(held, n) for some in pairs for p in some for n in p[:2]})
         table = jax.ShapeDtypeStruct((ROWS, PEERS * CAP), F32)
         extra = [jax.ShapeDtypeStruct(held[n].shape, BF16) for n in loaded[-1:]]
-        if last:
-            extra.append(jax.ShapeDtypeStruct((devices, CAP), F32))
         scratch = [pltpu.VMEM(held[n].shape, BF16) for n in loaded[:-1]]
         if loaded:
             scratch.append(pltpu.SemaphoreType.DMA((len(loaded),)))
         out = pl.pallas_call(
             lambda *refs: scores(names, new, loaded, pairs, state[0] is pos, last, *refs),
             in_specs=[VMEM, VMEM] + [HBM if n in loaded else VMEM for n in names],
-            out_specs=[VMEM] * (2 + len(extra)),
-            out_shape=[table, table, *extra],
-            scratch_shapes=scratch,
+            out_specs=[VMEM] * (1 if last else 2 + len(extra)),
+            out_shape=[jax.ShapeDtypeStruct((devices, CAP), F32)] if last else [table, table, *extra],
+            scratch_shapes=[pltpu.VMEM(table.shape, F32)] * 2 if last else scratch,
             compiler_params=SCORE_PARAMS,
             name=name,
         )(*state[:2], *[held[n] for n in names])
@@ -371,7 +371,7 @@
             new += (far_a,)
             pairs += every([b for b in older if b[2] < HALF], [far_a], HEAVY) + every(near, [far_b], LIGHT)
         state = score_call(state, new, [pairs], f"scores_near_{start}", last=end == PEERS)
-    got = lax.all_to_all(state[2], AXES, 0, 0, tiled=True)
+    got = lax.all_to_all(state[0], AXES, 0, 0, tiled=True)
     out = pl.pallas_call(
         finish,
         in_specs=[VMEM, VMEM],

time: 109 us -> 108 us (level)
  local copies, waits for them, and re-layouts: 1.4 us -> 3.9 us
  waiting for transfers between devices: 43.1 us -> 40.6 us
    all_to_all x2, waiting for transfers between devices: 34.3 us -> 31.8 us  [to_owner(): return lax.all_to_all(x, AXES, 0, 0, axis_index_groups=groups, tiled=True)]
    unnamed x2 -> x6, local copies, waits for them, and re-layouts: 1.18 us -> 3.68 us
where the time goes in v8:
time: 108 us
  waiting for transfers between devices  40.6 us (38%)
  Pallas kernels  26.1 us (24%)
  starting transfers between devices  21.8 us (20%)
  blocking collectives  15.6 us (14%)
  local copies, waits for them, and re-layouts  3.9 us (4%)
    all_to_all x2, waiting for transfers between devices, to_owner(): return lax.all_to_all(x, AXES, 0, 0, axis_index_groups=groups, tiled=True)  31.8 us
    pallas_call x5, Pallas kernels, score_call(): pl.pallas_call(lambda *refs: scores(names, new, loaded, pairs, state[0] i...  18.3 us
    all_to_all x1, blocking collectives, per_device(): got = lax.all_to_all(state[0], AXES, 0, 0, tiled=True)  15.6 us
    all_to_all x2, starting transfers between devices, to_owner(): return lax.all_to_all(x, AXES, 0, 0, axis_index_groups=groups, tiled=True)  12.4 us
    ppermute x2, starting transfers between devices, per_device(): lax.ppermute(own[start:end], AXES, moves_near)  5.26 us
    pallas_call x1, Pallas kernels, per_device(): pl.pallas_call(prepare, in_specs=[HBM, HBM], out_specs=[VMEM, HBM, HBM],...  4.89 us
    unnamed x6, local copies, waits for them, and re-layouts  3.68 us
    ppermute x2, waiting for transfers between devices, per_device(): lax.ppermute(own[half:half + HALF], AXES, moves_far)  3.42 us
  transfers between devices with their start and end apart: 10, of which 8 were waited for; matrix products, arithmetic and copies ran while one was open for 0% of the time, Pallas kernels for 17%

profile of v8, /device:TPU:1, one launch (start us, length us, event | category | flops | bytes accessed | tf_op | source)
XLA Modules:
  0.0 108.1 jit_solution(5826196479798695383)
XLA Ops:
  0.0 4.9 %prepare.1 = (s32[4,1024]{1,0:T(4,128)S(1)}, bf16[16,392,128]{2,1,0:T(8,128)(2,1)}, bf16[1024,768]{1,0:T(8,128)(2,1)}) custom-call(s32[1,1024]{1,0:T(1,128)} %bitcast.8, f32[1024,768]{1,0:T(8,128)} %emb_ref.1), custom_call_target="tpu_custom_call" | custom-call | tf_op jit(solution)/shard_map/prepare/pallas_call | solution.py:269
  4.9 1.5 %collective-permute-start.1 = (bf16[1024,768]{1,0:T(8,128)(2,1)}, bf16[1024,768]{1,0:T(8,128)(2,1)S(1)}, u32[]{:S(2)}, u32[]{:S(2)}) collective-permute-start(bf16[1024,768]{1,0:T(8,128)(2,1)} %get-tuple-element.23), channel_id=1, source_target_pairs={{0,4},{4,0},{32,36},{36,32},{64,68},{68,64},{96,100},{100,96},{8,1... | collective-permute-start | bytes 4718600 | tf_op jit(solution)/shard_map/ppermute | solution.py:296
  6.4 7.7 %all-to-all-start = ((bf16[16,392,128]{2,1,0:T(8,128)(2,1)}), bf16[16,392,128]{2,1,0:T(8,128)(2,1)S(1)}, u32[]{:S(2)}, u32[]{:S(2)}) async-start(bf16[16,392,128]{2,1,0:T(8,128)(2,1)} %get-tuple-element.20), calls=%async_computation | async-start | bytes 3211264 | tf_op jit(solution)/shard_map/all_to_all | solution.py:303
  14.6 0.8 collective-permute-done.pos_ref
  15.5 1.1 %copy-done.1 = bf16[1024,768]{1,0:T(8,128)(2,1)} copy-done((bf16[1024,768]{1,0:T(8,128)(2,1)}, bf16[1024,768]{1,0:T(8,128)(2,1)S(1)}, u32[]{:S(2)}) %copy-start.1) | copy-done | bytes 1572888
  16.6 1.4 %copy-done.2 = bf16[1024,768]{1,0:T(8,128)(2,1)S(1)} copy-done((bf16[1024,768]{1,0:T(8,128)(2,1)S(1)}, bf16[1024,768]{1,0:T(8,128)(2,1)}, u32[]{:S(2)}) %copy-start.2) | copy-done | bytes 1572888
  18.0 1.9 %place_other.1 = bf16[16,392,128]{2,1,0:T(8,128)(2,1)S(1)} custom-call(s32[4,1024]{1,0:T(4,128)S(1)} %collective-permute-done.pos_ref, bf16[1024,768]{1,0:T(8,128)(2,1)S(1)} %copy-done.2), custom_call_target="tpu_custom_call" | custom-call | tf_op jit(solution)/shard_map/place_other/pallas_call | solution.py:289
  19.9 1.1 %copy-done = bf16[16,392,128]{2,1,0:T(8,128)(2,1)} copy-done((bf16[16,392,128]{2,1,0:T(8,128)(2,1)}, bf16[16,392,128]{2,1,0:T(8,128)(2,1)S(1)}, u32[]{:S(2)}) %copy-start) | copy-done | bytes 1605656
  21.1 14.8 %all-to-all-done.refs_2_ = bf16[16,392,128]{2,1,0:T(8,128)(2,1)S(1)} async-done(((bf16[16,392,128]{2,1,0:T(8,128)(2,1)}), bf16[16,392,128]{2,1,0:T(8,128)(2,1)S(1)}, u32[]{:S(2)}, u32[]{:S(2)}) %all-to-all-start) | async-done | bytes 1605664 | tf_op jit(solution)/shard_map/all_to_all | solution.py:303
  35.9 4.7 %all-to-all-start.1 = ((bf16[16,392,128]{2,1,0:T(8,128)(2,1)}), bf16[16,392,128]{2,1,0:T(8,128)(2,1)S(1)}, u32[]{:S(2)}, u32[]{:S(2)}) async-start(bf16[16,392,128]{2,1,0:T(8,128)(2,1)} %copy-done), calls=%async_computation.1 | async-start | bytes 3211264 | tf_op jit(solution)/shard_map/all_to_all | solution.py:303
  40.6 2.0 %collective-permute-start.2 = (bf16[16,392,128]{2,1,0:T(8,128)(2,1)S(1)}, bf16[16,392,128]{2,1,0:T(8,128)(2,1)}, u32[]{:S(2)}, u32[]{:S(2)}) collective-permute-start(bf16[16,392,128]{2,1,0:T(8,128)(2,1)S(1)} %all-to-all-done.refs_2_), channel_id=1, source_target_pairs={{0,3},{32,35},{64,67},{96,99},{8,11},{40,43},{72,75},{104,107},{16... | collective-permute-start | bytes 4816904 | tf_op jit(solution)/shard_map/ppermute | solution.py:336
  42.6 1.5 %scores_own_first.1 = (f32[8,1024]{1,0:T(8,128)S(1)}, f32[8,1024]{1,0:T(8,128)S(1)}) custom-call(s32[4,1024]{1,0:T(4,128)S(1)} %get-tuple-element.19.refs_0_.refs_1_.pos_ref, s32[4,1024]{1,0:T(4,128)S(1)} %get-tuple-element.19.refs_0_.refs_1_.pos_ref, bf16[16,392,128]{2,1,0:T(8,128)(2,1)S(1)} %all-to-all-done.refs_2_), custom_call_target="tpu_custom_call" | custom-call | tf_op jit(solution)/shard_map/scores_own_first/pallas_call | solution.py:314
  44.1 16.9 %all-to-all-done.1.refs_3_.refs_2_ = bf16[16,392,128]{2,1,0:T(8,128)(2,1)S(1)} async-done(((bf16[16,392,128]{2,1,0:T(8,128)(2,1)}), bf16[16,392,128]{2,1,0:T(8,128)(2,1)S(1)}, u32[]{:S(2)}, u32[]{:S(2)}) %all-to-all-start.1) | async-done | bytes 1605664 | tf_op jit(solution)/shard_map/all_to_all | solution.py:303
  61.1 2.2 %collective-permute-start.4 = (bf16[12,392,128]{2,1,0:T(8,128)(2,1)S(1)}, bf16[12,392,128]{2,1,0:T(8,128)(2,1)S(1)}, u32[]{:S(2)}, u32[]{:S(2)}) collective-permute-start(bf16[12,392,128]{2,1,0:T(8,128)(2,1)S(1)} %slice.12), channel_id=1, source_target_pairs={{0,3},{32,35},{64,67},{96,99},{8,11},{40,43},{72,75},{104,107},{16... | collective-permute-start | bytes 3612680 | tf_op jit(solution)/shard_map/ppermute | solution.py:345
  63.4 3.2 %scores_own.1 = (f32[8,1024]{1,0:T(8,128)S(1)}, f32[8,1024]{1,0:T(8,128)S(1)}) custom-call(f32[8,1024]{1,0:T(8,128)S(1)} %get-tuple-element.21.refs_0_, f32[8,1024]{1,0:T(8,128)S(1)} %get-tuple-element.22.refs_1_, bf16[16,392,128]{2,1,0:T(8,128)(2,1)S(1)} %all-to-all-done.refs_2_, bf16[16,392,128]{2,1,0:T(8,128)(2,1)S(1)} %all-to-all-done.1.refs_3_.refs_2_), custom_call_target="tpu_custom_call" | custom-call | tf_op jit(solution)/shard_map/scores_own/pallas_call | solution.py:314
  66.8 2.5 %collective-permute-done.2.refs_4_ = bf16[16,392,128]{2,1,0:T(8,128)(2,1)} collective-permute-done((bf16[16,392,128]{2,1,0:T(8,128)(2,1)S(1)}, bf16[16,392,128]{2,1,0:T(8,128)(2,1)}, u32[]{:S(2)}, u32[]{:S(2)}) %collective-permute-start.2) | collective-permute-done | bytes 1605664 | tf_op jit(solution)/shard_map/ppermute | solution.py:336
  69.3 3.1 %collective-permute-start.6 = (bf16[4,392,128]{2,1,0:T(8,128)(2,1)S(1)}, bf16[4,392,128]{2,1,0:T(8,128)(2,1)S(1)}, u32[]{:S(2)}, u32[]{:S(2)}) collective-permute-start(bf16[4,392,128]{2,1,0:T(8,128)(2,1)S(1)} %slice.14), channel_id=1, source_target_pairs={{0,3},{32,35},{64,67},{96,99},{8,11},{40,43},{72,75},{104,107},{16... | collective-permute-start | bytes 1204232 | tf_op jit(solution)/shard_map/ppermute | solution.py:345
  72.4 8.2 %scores_near_first.1 = (f32[8,1024]{1,0:T(8,128)S(1)}, f32[8,1024]{1,0:T(8,128)S(1)}, bf16[16,392,128]{2,1,0:T(8,128)(2,1)S(1)}) custom-call(f32[8,1024]{1,0:T(8,128)S(1)} %get-tuple-element.24.refs_0_, f32[8,1024]{1,0:T(8,128)S(1)} %get-tuple-element.25.refs_1_, bf16[16,392,128]{2,1,0:T(8,128)(2,1)S(1)} %all-to-all-done.refs_2_, ...), custom_call_target="tpu_custom_call" | custom-call | tf_op jit(solution)/shard_map/scores_near_first/pallas_call | solution.py:314
  80.9 1.2 %collective-permute-done.4.refs_3_ = bf16[12,392,128]{2,1,0:T(8,128)(2,1)S(1)} collective-permute-done((bf16[12,392,128]{2,1,0:T(8,128)(2,1)S(1)}, bf16[12,392,128]{2,1,0:T(8,128)(2,1)S(1)}, u32[]{:S(2)}, u32[]{:S(2)}) %collective-permute-start.4) | collective-permute-done | bytes 1204256 | tf_op jit(solution)/shard_map/ppermute | solution.py:345
  82.1 3.5 %scores_near_0.1 = (f32[8,1024]{1,0:T(8,128)S(1)}, f32[8,1024]{1,0:T(8,128)S(1)}) custom-call(f32[8,1024]{1,0:T(8,128)S(1)} %get-tuple-element.26.refs_0_, f32[8,1024]{1,0:T(8,128)S(1)} %get-tuple-element.27.refs_1_, bf16[16,392,128]{2,1,0:T(8,128)(2,1)S(1)} %all-to-all-done.1.refs_3_.refs_2_, bf16[12,392,128]{2,1,0:T(8,128)(2,1)S(1)} %collective-permute-done.4.refs_3_, ...), custom_call_target="tpu_custom_call" | custom-call | tf_op jit(solution)/shard_map/scores_near_0/pallas_call | solution.py:314
  86.4 3.1 %collective-permute-done.7.refs_6_ = bf16[8,392,128]{2,1,0:T(8,128)(2,1)S(1)} collective-permute-done((bf16[8,392,128]{2,1,0:T(8,128)(2,1)S(1)}, bf16[8,392,128]{2,1,0:T(8,128)(2,1)S(1)}, u32[]{:S(2)}, u32[]{:S(2)}) %collective-permute-start.7) | collective-permute-done | bytes 802848 | tf_op jit(solution)/shard_map/ppermute | solution.py:347
  89.5 2.0 %scores_near_12.1 = f32[128,64]{1,0:T(8,128)S(1)} custom-call(f32[8,1024]{1,0:T(8,128)S(1)} %get-tuple-element.30.refs_0_, f32[8,1024]{1,0:T(8,128)S(1)} %get-tuple-element.31.refs_1_, bf16[16,392,128]{2,1,0:T(8,128)(2,1)S(1)} %all-to-all-done.1.refs_3_.refs_2_, bf16[12,392,128]{2,1,0:T(8,128)(2,1)S(1)} %collective-permute-done.4.refs_3_, ...), custom_call_target="tpu_custom_call" | custom-call | tf_op jit(solution)/shard_map/scores_near_12/pallas_call | solution.py:314
  91.5 15.6 %all_to_all.21 = f32[128,1,64]{2,1,0:T(1,128)S(1)} all-to-all(f32[128,1,64]{2,1,0:T(1,128)S(1)} %bitcast.6), channel_id=1, replica_groups=mesh['docs'=32,'split'=4] {'docs','split'}, dimensions={0} | all-to-all | bytes 65536 | tf_op jit(solution)/shard_map/all_to_all | solution.py:374
  107.1 1.0 finish.1
  (15 shorter events, 2.1 us)
Async XLA Ops:
  4.9 10.6 %collective-permute-start.1 = (bf16[1024,768]{1,0:T(8,128)(2,1)}, bf16[1024,768]{1,0:T(8,128)(2,1)S(1)}, u32[]{:S(2)}, u32[]{:S(2)}) collective-permute-start(bf16[1024,768]{1,0:T(8,128)(2,1)} %get-tuple-element.23), channel_id=1, source_target_pairs={{0,4},{4,0},{32,36},{36,32},{64,68},{68,64},{96,100},{100,96},{8,1... | collective-permute-start | bytes 4718600 | tf_op jit(solution)/shard_map/ppermute | solution.py:296
  6.4 29.5 %all-to-all-start = ((bf16[16,392,128]{2,1,0:T(8,128)(2,1)}), bf16[16,392,128]{2,1,0:T(8,128)(2,1)S(1)}, u32[]{:S(2)}, u32[]{:S(2)}) async-start(bf16[16,392,128]{2,1,0:T(8,128)(2,1)} %get-tuple-element.20), calls=%async_computation | async-start | bytes 3211264 | tf_op jit(solution)/shard_map/all_to_all | solution.py:303
  14.1 1.4 %collective-permute-start = (s32[4,1024]{1,0:T(4,128)S(1)}, s32[4,1024]{1,0:T(4,128)S(1)}, u32[]{:S(2)}, u32[]{:S(2)}) collective-permute-start(s32[4,1024]{1,0:T(4,128)S(1)} %get-tuple-element.19.refs_0_.refs_1_.pos_ref), channel_id=1, source_target_pairs={{0,4},{4,0},{32,36},{36,32},{64,68},{68,64},{96,100},{100,96},{8,1... | collective-permute-start | bytes 49160 | tf_op jit(solution)/shard_map/ppermute | solution.py:296
  15.5 1.1 %copy-start.1 = (bf16[1024,768]{1,0:T(8,128)(2,1)}, bf16[1024,768]{1,0:T(8,128)(2,1)S(1)}, u32[]{:S(2)}) copy-start(bf16[1024,768]{1,0:T(8,128)(2,1)S(1)} %collective-permute-done.1.unit_ref) | copy-start | bytes 4718596
  16.6 1.4 %copy-start.2 = (bf16[1024,768]{1,0:T(8,128)(2,1)S(1)}, bf16[1024,768]{1,0:T(8,128)(2,1)}, u32[]{:S(2)}) copy-start(bf16[1024,768]{1,0:T(8,128)(2,1)} %copy-done.1) | copy-start | bytes 4718596
  19.9 1.1 %copy-start = (bf16[16,392,128]{2,1,0:T(8,128)(2,1)}, bf16[16,392,128]{2,1,0:T(8,128)(2,1)S(1)}, u32[]{:S(2)}) copy-start(bf16[16,392,128]{2,1,0:T(8,128)(2,1)S(1)} %place_other.1) | copy-start | bytes 4816900
  35.9 25.1 %all-to-all-start.1 = ((bf16[16,392,128]{2,1,0:T(8,128)(2,1)}), bf16[16,392,128]{2,1,0:T(8,128)(2,1)S(1)}, u32[]{:S(2)}, u32[]{:S(2)}) async-start(bf16[16,392,128]{2,1,0:T(8,128)(2,1)} %copy-done), calls=%async_computation.1 | async-start | bytes 3211264 | tf_op jit(solution)/shard_map/all_to_all | solution.py:303
  40.6 28.7 %collective-permute-start.2 = (bf16[16,392,128]{2,1,0:T(8,128)(2,1)S(1)}, bf16[16,392,128]{2,1,0:T(8,128)(2,1)}, u32[]{:S(2)}, u32[]{:S(2)}) collective-permute-start(bf16[16,392,128]{2,1,0:T(8,128)(2,1)S(1)} %all-to-all-done.refs_2_), channel_id=1, source_target_pairs={{0,3},{32,35},{64,67},{96,99},{8,11},{40,43},{72,75},{104,107},{16... | collective-permute-start | bytes 4816904 | tf_op jit(solution)/shard_map/ppermute | solution.py:336
  42.6 29.8 %collective-permute-start.3 = (bf16[16,392,128]{2,1,0:T(8,128)(2,1)S(1)}, bf16[16,392,128]{2,1,0:T(8,128)(2,1)}, u32[]{:S(2)}, u32[]{:S(2)}) collective-permute-start(bf16[16,392,128]{2,1,0:T(8,128)(2,1)S(1)} %all-to-all-done.refs_2_), channel_id=1, source_target_pairs={{0,1},{32,33},{64,65},{96,97},{8,9},{40,41},{72,73},{104,105},{16,... | collective-permute-start | bytes 4816904 | tf_op jit(solution)/shard_map/ppermute | solution.py:337
  61.1 21.0 %collective-permute-start.4 = (bf16[12,392,128]{2,1,0:T(8,128)(2,1)S(1)}, bf16[12,392,128]{2,1,0:T(8,128)(2,1)S(1)}, u32[]{:S(2)}, u32[]{:S(2)}) collective-permute-start(bf16[12,392,128]{2,1,0:T(8,128)(2,1)S(1)} %slice.12), channel_id=1, source_target_pairs={{0,3},{32,35},{64,67},{96,99},{8,11},{40,43},{72,75},{104,107},{16... | collective-permute-start | bytes 3612680 | tf_op jit(solution)/shard_map/ppermute | solution.py:345
  63.3 17.5 %collective-permute-start.5 = (bf16[8,392,128]{2,1,0:T(8,128)(2,1)S(1)}, bf16[8,392,128]{2,1,0:T(8,128)(2,1)S(1)}, u32[]{:S(2)}, u32[]{:S(2)}) collective-permute-start(bf16[8,392,128]{2,1,0:T(8,128)(2,1)S(1)} %slice.13), channel_id=1, source_target_pairs={{0,1},{32,33},{64,65},{96,97},{8,9},{40,41},{72,73},{104,105},{16,... | collective-permute-start | bytes 2408456 | tf_op jit(solution)/shard_map/ppermute | solution.py:347
  66.6 22.8 %collective-permute-start.7 = (bf16[8,392,128]{2,1,0:T(8,128)(2,1)S(1)}, bf16[8,392,128]{2,1,0:T(8,128)(2,1)S(1)}, u32[]{:S(2)}, u32[]{:S(2)}) collective-permute-start(bf16[8,392,128]{2,1,0:T(8,128)(2,1)S(1)} %slice.15), channel_id=1, source_target_pairs={{0,1},{32,33},{64,65},{96,97},{8,9},{40,41},{72,73},{104,105},{16,... | collective-permute-start | bytes 2408456 | tf_op jit(solution)/shard_map/ppermute | solution.py:347
  69.3 17.1 %collective-permute-start.6 = (bf16[4,392,128]{2,1,0:T(8,128)(2,1)S(1)}, bf16[4,392,128]{2,1,0:T(8,128)(2,1)S(1)}, u32[]{:S(2)}, u32[]{:S(2)}) collective-permute-start(bf16[4,392,128]{2,1,0:T(8,128)(2,1)S(1)} %slice.14), channel_id=1, source_target_pairs={{0,3},{32,35},{64,67},{96,99},{8,11},{40,43},{72,75},{104,107},{16... | collective-permute-start | bytes 1204232 | tf_op jit(solution)/shard_map/ppermute | solution.py:345

commit v9 on v8

--- a/solution.py
+++ b/solution.py
@@ -250,10 +250,12 @@
         rows = [got_ref[pl.ds(z * 2 * PEERS + line * 2 * SIDE + SIDE, SIDE), :] for line in range(SIDE)]
         second.append(functools.reduce(jnp.maximum, rows))
     best = jnp.concatenate([first] + second, axis=0)
-    pick = jnp.where(iota((best.shape[0], docs), 0) == rng, 1.0, 0.0)
-    found = lax.dot_general(
-        best, pick, (((0,), (0,)), ((), ())), precision=lax.Precision.HIGHEST, preferred_element_type=F32
-    )
+    pick = jnp.where(iota((best.shape[0], docs), 0) == rng, 1.0, 0.0).astype(BF16)
+    found, rest = 0.0, best
+    for _ in range(3):
+        part = rest.astype(BF16)
+        rest = rest - part.astype(F32)
+        found = found + lax.dot_general(part, pick, (((0,), (0,)), ((), ())), preferred_element_type=F32)
     out_ref[...] = jnp.sum(jnp.where(iota((CAP, docs), 0) == rank, found, 0.0), axis=0, keepdims=True)
 
 
@@ -347,7 +349,6 @@
         held[FAR, 1, half, HALF] = lax.ppermute(own[half : half + HALF], AXES, moves_far)
         if not start:
             state = score_call(state, (whole_1,), [every(own_0, own_1) + every(own_1, own_1)], "scores_own")
-            own = after(own, state[0])
     state = score_call(
         state,
         whole_0[1:],

time: 108 us -> 108 us (level)
    ppermute x1, waiting for transfers between devices: 2.54 us -> 5.71 us  [per_device(): held[whole_0[1]] = lax.ppermute(own, AXES, moves_near)]
    ppermute x2, waiting for transfers between devices: 2.01 us -> 0.01 us  [per_device(): lax.ppermute(own[start:end], AXES, moves_near)]
    ppermute x2, waiting for transfers between devices: 3.42 us -> 2.01 us  [per_device(): lax.ppermute(own[half:half + HALF], AXES, moves_far)]
  transfers between devices with their start and end apart: 10 -> 10, of which waited for: 8 -> 5; matrix products, arithmetic and copies ran while one was open for 0% -> 0% of each run, Pallas kernels for 17% -> 17%
where the time goes in v9:
time: 108 us
  waiting for transfers between devices  40.3 us (37%)
  Pallas kernels  26.2 us (24%)
  starting transfers between devices  21.8 us (20%)
  blocking collectives  15.6 us (14%)
  local copies, waits for them, and re-layouts  3.91 us (4%)
    all_to_all x2, waiting for transfers between devices, to_owner(): return lax.all_to_all(x, AXES, 0, 0, axis_index_groups=groups, tiled=True)  31.8 us
    pallas_call x5, Pallas kernels, score_call(): pl.pallas_call(lambda *refs: scores(names, new, loaded, pairs, state[0] i...  18.6 us
    all_to_all x1, blocking collectives, per_device(): got = lax.all_to_all(state[0], AXES, 0, 0, tiled=True)  15.6 us
    all_to_all x2, starting transfers between devices, to_owner(): return lax.all_to_all(x, AXES, 0, 0, axis_index_groups=groups, tiled=True)  12.4 us
    ppermute x1, waiting for transfers between devices, per_device(): held[whole_0[1]] = lax.ppermute(own, AXES, moves_near)  5.71 us
    ppermute x2, starting transfers between devices, per_device(): lax.ppermute(own[start:end], AXES, moves_near)  5.26 us
    pallas_call x1, Pallas kernels, per_device(): pl.pallas_call(prepare, in_specs=[HBM, HBM], out_specs=[VMEM, HBM, HBM],...  4.89 us
    unnamed x6, local copies, waits for them, and re-layouts  3.7 us
  transfers between devices with their start and end apart: 10, of which 5 were waited for; matrix products, arithmetic and copies ran while one was open for 0% of the time, Pallas kernels for 17%

profile of v9, /device:TPU:1, one launch (start us, length us, event | category | flops | bytes accessed | tf_op | source)
XLA Modules:
  0.0 108.0 jit_solution(14899565792369328103)
XLA Ops:
  0.0 4.9 %prepare.1 = (s32[4,1024]{1,0:T(4,128)S(1)}, bf16[16,392,128]{2,1,0:T(8,128)(2,1)}, bf16[1024,768]{1,0:T(8,128)(2,1)}) custom-call(s32[1,1024]{1,0:T(1,128)} %bitcast.8, f32[1024,768]{1,0:T(8,128)} %emb_ref.1), custom_call_target="tpu_custom_call" | custom-call | tf_op jit(solution)/shard_map/prepare/pallas_call | solution.py:271
  4.9 1.5 %collective-permute-start.1 = (bf16[1024,768]{1,0:T(8,128)(2,1)}, bf16[1024,768]{1,0:T(8,128)(2,1)S(1)}, u32[]{:S(2)}, u32[]{:S(2)}) collective-permute-start(bf16[1024,768]{1,0:T(8,128)(2,1)} %get-tuple-element.22), channel_id=1, source_target_pairs={{0,4},{4,0},{32,36},{36,32},{64,68},{68,64},{96,100},{100,96},{8,1... | collective-permute-start | bytes 4718600 | tf_op jit(solution)/shard_map/ppermute | solution.py:298
  6.4 7.7 %all-to-all-start = ((bf16[16,392,128]{2,1,0:T(8,128)(2,1)}), bf16[16,392,128]{2,1,0:T(8,128)(2,1)S(1)}, u32[]{:S(2)}, u32[]{:S(2)}) async-start(bf16[16,392,128]{2,1,0:T(8,128)(2,1)} %get-tuple-element.19), calls=%async_computation | async-start | bytes 3211264 | tf_op jit(solution)/shard_map/all_to_all | solution.py:305
  14.1 0.6 collective-permute-start
  14.6 0.8 collective-permute-done.pos_ref
  15.5 1.1 %copy-done.1 = bf16[1024,768]{1,0:T(8,128)(2,1)} copy-done((bf16[1024,768]{1,0:T(8,128)(2,1)}, bf16[1024,768]{1,0:T(8,128)(2,1)S(1)}, u32[]{:S(2)}) %copy-start.1) | copy-done | bytes 1572888
  16.6 1.4 %copy-done.2 = bf16[1024,768]{1,0:T(8,128)(2,1)S(1)} copy-done((bf16[1024,768]{1,0:T(8,128)(2,1)S(1)}, bf16[1024,768]{1,0:T(8,128)(2,1)}, u32[]{:S(2)}) %copy-start.2) | copy-done | bytes 1572888
  18.0 1.9 %place_other.1 = bf16[16,392,128]{2,1,0:T(8,128)(2,1)S(1)} custom-call(s32[4,1024]{1,0:T(4,128)S(1)} %collective-permute-done.pos_ref, bf16[1024,768]{1,0:T(8,128)(2,1)S(1)} %copy-done.2), custom_call_target="tpu_custom_call" | custom-call | tf_op jit(solution)/shard_map/place_other/pallas_call | solution.py:291
  19.9 1.1 %copy-done = bf16[16,392,128]{2,1,0:T(8,128)(2,1)} copy-done((bf16[16,392,128]{2,1,0:T(8,128)(2,1)}, bf16[16,392,128]{2,1,0:T(8,128)(2,1)S(1)}, u32[]{:S(2)}) %copy-start) | copy-done | bytes 1605656
  21.1 14.8 %all-to-all-done.refs_2_ = bf16[16,392,128]{2,1,0:T(8,128)(2,1)S(1)} async-done(((bf16[16,392,128]{2,1,0:T(8,128)(2,1)}), bf16[16,392,128]{2,1,0:T(8,128)(2,1)S(1)}, u32[]{:S(2)}, u32[]{:S(2)}) %all-to-all-start) | async-done | bytes 1605664 | tf_op jit(solution)/shard_map/all_to_all | solution.py:305
  35.9 4.7 %all-to-all-start.1 = ((bf16[16,392,128]{2,1,0:T(8,128)(2,1)}), bf16[16,392,128]{2,1,0:T(8,128)(2,1)S(1)}, u32[]{:S(2)}, u32[]{:S(2)}) async-start(bf16[16,392,128]{2,1,0:T(8,128)(2,1)} %copy-done), calls=%async_computation.1 | async-start | bytes 3211264 | tf_op jit(solution)/shard_map/all_to_all | solution.py:305
  40.6 2.0 %collective-permute-start.2 = (bf16[16,392,128]{2,1,0:T(8,128)(2,1)S(1)}, bf16[16,392,128]{2,1,0:T(8,128)(2,1)}, u32[]{:S(2)}, u32[]{:S(2)}) collective-permute-start(bf16[16,392,128]{2,1,0:T(8,128)(2,1)S(1)} %all-to-all-done.refs_2_), channel_id=1, source_target_pairs={{0,3},{32,35},{64,67},{96,99},{8,11},{40,43},{72,75},{104,107},{16... | collective-permute-start | bytes 4816904 | tf_op jit(solution)/shard_map/ppermute | solution.py:338
  42.6 1.5 %scores_own_first.1 = (f32[8,1024]{1,0:T(8,128)S(1)}, f32[8,1024]{1,0:T(8,128)S(1)}) custom-call(s32[4,1024]{1,0:T(4,128)S(1)} %get-tuple-element.18.refs_0_.refs_1_.pos_ref, s32[4,1024]{1,0:T(4,128)S(1)} %get-tuple-element.18.refs_0_.refs_1_.pos_ref, bf16[16,392,128]{2,1,0:T(8,128)(2,1)S(1)} %all-to-all-done.refs_2_), custom_call_target="tpu_custom_call" | custom-call | tf_op jit(solution)/shard_map/scores_own_first/pallas_call | solution.py:316
  44.1 16.9 %all-to-all-done.1.refs_3_.refs_2_ = bf16[16,392,128]{2,1,0:T(8,128)(2,1)S(1)} async-done(((bf16[16,392,128]{2,1,0:T(8,128)(2,1)}), bf16[16,392,128]{2,1,0:T(8,128)(2,1)S(1)}, u32[]{:S(2)}, u32[]{:S(2)}) %all-to-all-start.1) | async-done | bytes 1605664 | tf_op jit(solution)/shard_map/all_to_all | solution.py:305
  61.1 2.2 %collective-permute-start.4 = (bf16[12,392,128]{2,1,0:T(8,128)(2,1)S(1)}, bf16[12,392,128]{2,1,0:T(8,128)(2,1)S(1)}, u32[]{:S(2)}, u32[]{:S(2)}) collective-permute-start(bf16[12,392,128]{2,1,0:T(8,128)(2,1)S(1)} %slice.12), channel_id=1, source_target_pairs={{0,3},{32,35},{64,67},{96,99},{8,11},{40,43},{72,75},{104,107},{16... | collective-permute-start | bytes 3612680 | tf_op jit(solution)/shard_map/ppermute | solution.py:347
  63.6 5.7 %collective-permute-done.2.refs_4_ = bf16[16,392,128]{2,1,0:T(8,128)(2,1)} collective-permute-done((bf16[16,392,128]{2,1,0:T(8,128)(2,1)S(1)}, bf16[16,392,128]{2,1,0:T(8,128)(2,1)}, u32[]{:S(2)}, u32[]{:S(2)}) %collective-permute-start.2) | collective-permute-done | bytes 1605664 | tf_op jit(solution)/shard_map/ppermute | solution.py:338
  69.3 3.1 %collective-permute-start.6 = (bf16[4,392,128]{2,1,0:T(8,128)(2,1)S(1)}, bf16[4,392,128]{2,1,0:T(8,128)(2,1)S(1)}, u32[]{:S(2)}, u32[]{:S(2)}) collective-permute-start(bf16[4,392,128]{2,1,0:T(8,128)(2,1)S(1)} %slice.14), channel_id=1, source_target_pairs={{0,3},{32,35},{64,67},{96,99},{8,11},{40,43},{72,75},{104,107},{16... | collective-permute-start | bytes 1204232 | tf_op jit(solution)/shard_map/ppermute | solution.py:347
  72.4 3.1 %scores_own.1 = (f32[8,1024]{1,0:T(8,128)S(1)}, f32[8,1024]{1,0:T(8,128)S(1)}) custom-call(f32[8,1024]{1,0:T(8,128)S(1)} %get-tuple-element.20.refs_0_, f32[8,1024]{1,0:T(8,128)S(1)} %get-tuple-element.21.refs_1_, bf16[16,392,128]{2,1,0:T(8,128)(2,1)S(1)} %all-to-all-done.refs_2_, bf16[16,392,128]{2,1,0:T(8,128)(2,1)S(1)} %all-to-all-done.1.refs_3_.refs_2_), custom_call_target="tpu_custom_call" | custom-call | tf_op jit(solution)/shard_map/scores_own/pallas_call | solution.py:316
  75.5 8.2 %scores_near_first.1 = (f32[8,1024]{1,0:T(8,128)S(1)}, f32[8,1024]{1,0:T(8,128)S(1)}, bf16[16,392,128]{2,1,0:T(8,128)(2,1)S(1)}) custom-call(f32[8,1024]{1,0:T(8,128)S(1)} %get-tuple-element.23.refs_0_, f32[8,1024]{1,0:T(8,128)S(1)} %get-tuple-element.24.refs_1_, bf16[16,392,128]{2,1,0:T(8,128)(2,1)S(1)} %all-to-all-done.refs_2_, ...), custom_call_target="tpu_custom_call" | custom-call | tf_op jit(solution)/shard_map/scores_near_first/pallas_call | solution.py:316
  83.7 3.7 %scores_near_0.1 = (f32[8,1024]{1,0:T(8,128)S(1)}, f32[8,1024]{1,0:T(8,128)S(1)}) custom-call(f32[8,1024]{1,0:T(8,128)S(1)} %get-tuple-element.25.refs_0_, f32[8,1024]{1,0:T(8,128)S(1)} %get-tuple-element.26.refs_1_, bf16[16,392,128]{2,1,0:T(8,128)(2,1)S(1)} %all-to-all-done.1.refs_3_.refs_2_, bf16[12,392,128]{2,1,0:T(8,128)(2,1)S(1)} %collective-permute-done.4.refs_3_, ...), custom_call_target="tpu_custom_call" | custom-call | tf_op jit(solution)/shard_map/scores_near_0/pallas_call | solution.py:316
  87.5 2.0 %collective-permute-done.7.refs_6_ = bf16[8,392,128]{2,1,0:T(8,128)(2,1)S(1)} collective-permute-done((bf16[8,392,128]{2,1,0:T(8,128)(2,1)S(1)}, bf16[8,392,128]{2,1,0:T(8,128)(2,1)S(1)}, u32[]{:S(2)}, u32[]{:S(2)}) %collective-permute-start.7) | collective-permute-done | bytes 802848 | tf_op jit(solution)/shard_map/ppermute | solution.py:349
  89.5 2.0 %scores_near_12.1 = f32[128,64]{1,0:T(8,128)S(1)} custom-call(f32[8,1024]{1,0:T(8,128)S(1)} %get-tuple-element.29.refs_0_, f32[8,1024]{1,0:T(8,128)S(1)} %get-tuple-element.30.refs_1_, bf16[16,392,128]{2,1,0:T(8,128)(2,1)S(1)} %all-to-all-done.1.refs_3_.refs_2_, bf16[12,392,128]{2,1,0:T(8,128)(2,1)S(1)} %collective-permute-done.4.refs_3_, ...), custom_call_target="tpu_custom_call" | custom-call | tf_op jit(solution)/shard_map/scores_near_12/pallas_call | solution.py:316
  91.5 15.6 %all_to_all.21 = f32[128,1,64]{2,1,0:T(1,128)S(1)} all-to-all(f32[128,1,64]{2,1,0:T(1,128)S(1)} %bitcast.6), channel_id=1, replica_groups=mesh['docs'=32,'split'=4] {'docs','split'}, dimensions={0} | all-to-all | bytes 65536 | tf_op jit(solution)/shard_map/all_to_all | solution.py:375
  107.1 0.9 finish.1
  (14 shorter events, 0.4 us)
Async XLA Ops:
  4.9 10.6 %collective-permute-start.1 = (bf16[1024,768]{1,0:T(8,128)(2,1)}, bf16[1024,768]{1,0:T(8,128)(2,1)S(1)}, u32[]{:S(2)}, u32[]{:S(2)}) collective-permute-start(bf16[1024,768]{1,0:T(8,128)(2,1)} %get-tuple-element.22), channel_id=1, source_target_pairs={{0,4},{4,0},{32,36},{36,32},{64,68},{68,64},{96,100},{100,96},{8,1... | collective-permute-start | bytes 4718600 | tf_op jit(solution)/shard_map/ppermute | solution.py:298
  6.4 29.5 %all-to-all-start = ((bf16[16,392,128]{2,1,0:T(8,128)(2,1)}), bf16[16,392,128]{2,1,0:T(8,128)(2,1)S(1)}, u32[]{:S(2)}, u32[]{:S(2)}) async-start(bf16[16,392,128]{2,1,0:T(8,128)(2,1)} %get-tuple-element.19), calls=%async_computation | async-start | bytes 3211264 | tf_op jit(solution)/shard_map/all_to_all | solution.py:305
  14.1 1.4 %collective-permute-start = (s32[4,1024]{1,0:T(4,128)S(1)}, s32[4,1024]{1,0:T(4,128)S(1)}, u32[]{:S(2)}, u32[]{:S(2)}) collective-permute-start(s32[4,1024]{1,0:T(4,128)S(1)} %get-tuple-element.18.refs_0_.refs_1_.pos_ref), channel_id=1, source_target_pairs={{0,4},{4,0},{32,36},{36,32},{64,68},{68,64},{96,100},{100,96},{8,1... | collective-permute-start | bytes 49160 | tf_op jit(solution)/shard_map/ppermute | solution.py:298
  15.5 1.1 %copy-start.1 = (bf16[1024,768]{1,0:T(8,128)(2,1)}, bf16[1024,768]{1,0:T(8,128)(2,1)S(1)}, u32[]{:S(2)}) copy-start(bf16[1024,768]{1,0:T(8,128)(2,1)S(1)} %collective-permute-done.1.unit_ref) | copy-start | bytes 4718596
  16.6 1.4 %copy-start.2 = (bf16[1024,768]{1,0:T(8,128)(2,1)S(1)}, bf16[1024,768]{1,0:T(8,128)(2,1)}, u32[]{:S(2)}) copy-start(bf16[1024,768]{1,0:T(8,128)(2,1)} %copy-done.1) | copy-start | bytes 4718596
  19.9 1.2 %copy-start = (bf16[16,392,128]{2,1,0:T(8,128)(2,1)}, bf16[16,392,128]{2,1,0:T(8,128)(2,1)S(1)}, u32[]{:S(2)}) copy-start(bf16[16,392,128]{2,1,0:T(8,128)(2,1)S(1)} %place_other.1) | copy-start | bytes 4816900
  35.9 25.1 %all-to-all-start.1 = ((bf16[16,392,128]{2,1,0:T(8,128)(2,1)}), bf16[16,392,128]{2,1,0:T(8,128)(2,1)S(1)}, u32[]{:S(2)}, u32[]{:S(2)}) async-start(bf16[16,392,128]{2,1,0:T(8,128)(2,1)} %copy-done), calls=%async_computation.1 | async-start | bytes 3211264 | tf_op jit(solution)/shard_map/all_to_all | solution.py:305
  40.6 28.7 %collective-permute-start.2 = (bf16[16,392,128]{2,1,0:T(8,128)(2,1)S(1)}, bf16[16,392,128]{2,1,0:T(8,128)(2,1)}, u32[]{:S(2)}, u32[]{:S(2)}) collective-permute-start(bf16[16,392,128]{2,1,0:T(8,128)(2,1)S(1)} %all-to-all-done.refs_2_), channel_id=1, source_target_pairs={{0,3},{32,35},{64,67},{96,99},{8,11},{40,43},{72,75},{104,107},{16... | collective-permute-start | bytes 4816904 | tf_op jit(solution)/shard_map/ppermute | solution.py:338
  42.5 33.0 %collective-permute-start.3 = (bf16[16,392,128]{2,1,0:T(8,128)(2,1)S(1)}, bf16[16,392,128]{2,1,0:T(8,128)(2,1)}, u32[]{:S(2)}, u32[]{:S(2)}) collective-permute-start(bf16[16,392,128]{2,1,0:T(8,128)(2,1)S(1)} %all-to-all-done.refs_2_), channel_id=1, source_target_pairs={{0,1},{32,33},{64,65},{96,97},{8,9},{40,41},{72,73},{104,105},{16,... | collective-permute-start | bytes 4816904 | tf_op jit(solution)/shard_map/ppermute | solution.py:339
  61.1 22.6 %collective-permute-start.4 = (bf16[12,392,128]{2,1,0:T(8,128)(2,1)S(1)}, bf16[12,392,128]{2,1,0:T(8,128)(2,1)S(1)}, u32[]{:S(2)}, u32[]{:S(2)}) collective-permute-start(bf16[12,392,128]{2,1,0:T(8,128)(2,1)S(1)} %slice.12), channel_id=1, source_target_pairs={{0,3},{32,35},{64,67},{96,99},{8,11},{40,43},{72,75},{104,107},{16... | collective-permute-start | bytes 3612680 | tf_op jit(solution)/shard_map/ppermute | solution.py:347
  63.4 20.3 %collective-permute-start.5 = (bf16[8,392,128]{2,1,0:T(8,128)(2,1)S(1)}, bf16[8,392,128]{2,1,0:T(8,128)(2,1)S(1)}, u32[]{:S(2)}, u32[]{:S(2)}) collective-permute-start(bf16[8,392,128]{2,1,0:T(8,128)(2,1)S(1)} %get-tuple-element.32), channel_id=1, source_target_pairs={{0,1},{32,33},{64,65},{96,97},{8,9},{40,41},{72,73},{104,105},{16,... | collective-permute-start | bytes 2408456 | tf_op jit(solution)/shard_map/ppermute | solution.py:349
  63.5 26.0 %collective-permute-start.7 = (bf16[8,392,128]{2,1,0:T(8,128)(2,1)S(1)}, bf16[8,392,128]{2,1,0:T(8,128)(2,1)S(1)}, u32[]{:S(2)}, u32[]{:S(2)}) collective-permute-start(bf16[8,392,128]{2,1,0:T(8,128)(2,1)S(1)} %get-tuple-element.31), channel_id=1, source_target_pairs={{0,1},{32,33},{64,65},{96,97},{8,9},{40,41},{72,73},{104,105},{16,... | collective-permute-start | bytes 2408456 | tf_op jit(solution)/shard_map/ppermute | solution.py:349
  69.3 18.2 %collective-permute-start.6 = (bf16[4,392,128]{2,1,0:T(8,128)(2,1)S(1)}, bf16[4,392,128]{2,1,0:T(8,128)(2,1)S(1)}, u32[]{:S(2)}, u32[]{:S(2)}) collective-permute-start(bf16[4,392,128]{2,1,0:T(8,128)(2,1)S(1)} %slice.14), channel_id=1, source_target_pairs={{0,3},{32,35},{64,67},{96,99},{8,11},{40,43},{72,75},{104,107},{16... | collective-permute-start | bytes 1204232 | tf_op jit(solution)/shard_map/ppermute | solution.py:347

commit v10 on v9

--- a/solution.py
+++ b/solution.py
@@ -28,7 +28,7 @@
 VMEM = pl.BlockSpec(memory_space=pltpu.VMEM)
 HBM = pl.BlockSpec(memory_space=pltpu.HBM)
 PARAMS = pltpu.CompilerParams(vmem_limit_bytes=24 * 2**20)
-SCORE_PARAMS = pltpu.CompilerParams(vmem_limit_bytes=28 * 2**20)
+SCORE_PARAMS = pltpu.CompilerParams(vmem_limit_bytes=20 * 2**20)
 
 
 def iota(shape, axis):

time: 108 us -> 108 us (level)
  no operation moved by 1% of the time
where the time goes in v10:
time: 108 us
  waiting for transfers between devices  40.3 us (37%)
  Pallas kernels  26.2 us (24%)
  starting transfers between devices  21.8 us (20%)
  blocking collectives  15.6 us (14%)
  local copies, waits for them, and re-layouts  3.91 us (4%)
    all_to_all x2, waiting for transfers between devices, to_owner(): return lax.all_to_all(x, AXES, 0, 0, axis_index_groups=groups, tiled=True)  31.8 us
    pallas_call x5, Pallas kernels, score_call(): pl.pallas_call(lambda *refs: scores(names, new, loaded, pairs, state[0] i...  18.6 us
    all_to_all x1, blocking collectives, per_device(): got = lax.all_to_all(state[0], AXES, 0, 0, tiled=True)  15.6 us
    all_to_all x2, starting transfers between devices, to_owner(): return lax.all_to_all(x, AXES, 0, 0, axis_index_groups=groups, tiled=True)  12.4 us
    ppermute x1, waiting for transfers between devices, per_device(): held[whole_0[1]] = lax.ppermute(own, AXES, moves_near)  5.71 us
    ppermute x2, starting transfers between devices, per_device(): lax.ppermute(own[start:end], AXES, moves_near)  5.26 us
    pallas_call x1, Pallas kernels, per_device(): pl.pallas_call(prepare, in_specs=[HBM, HBM], out_specs=[VMEM, HBM, HBM],...  4.89 us
    unnamed x6, local copies, waits for them, and re-layouts  3.7 us
  transfers between devices with their start and end apart: 10, of which 5 were waited for; matrix products, arithmetic and copies ran while one was open for 0% of the time, Pallas kernels for 17%

profile of v10, /device:TPU:1, one launch (start us, length us, event | category | flops | bytes accessed | tf_op | source)
XLA Modules:
  0.0 108.0 jit_solution(1325827934001473305)
XLA Ops:
  0.0 4.9 %prepare.1 = (s32[4,1024]{1,0:T(4,128)S(1)}, bf16[16,392,128]{2,1,0:T(8,128)(2,1)}, bf16[1024,768]{1,0:T(8,128)(2,1)}) custom-call(s32[1,1024]{1,0:T(1,128)} %bitcast.8, f32[1024,768]{1,0:T(8,128)} %emb_ref.1), custom_call_target="tpu_custom_call" | custom-call | tf_op jit(solution)/shard_map/prepare/pallas_call | solution.py:271
  4.9 1.5 %collective-permute-start.1 = (bf16[1024,768]{1,0:T(8,128)(2,1)}, bf16[1024,768]{1,0:T(8,128)(2,1)S(1)}, u32[]{:S(2)}, u32[]{:S(2)}) collective-permute-start(bf16[1024,768]{1,0:T(8,128)(2,1)} %get-tuple-element.22), channel_id=1, source_target_pairs={{0,4},{4,0},{32,36},{36,32},{64,68},{68,64},{96,100},{100,96},{8,1... | collective-permute-start | bytes 4718600 | tf_op jit(solution)/shard_map/ppermute | solution.py:298
  6.4 7.7 %all-to-all-start = ((bf16[16,392,128]{2,1,0:T(8,128)(2,1)}), bf16[16,392,128]{2,1,0:T(8,128)(2,1)S(1)}, u32[]{:S(2)}, u32[]{:S(2)}) async-start(bf16[16,392,128]{2,1,0:T(8,128)(2,1)} %get-tuple-element.19), calls=%async_computation | async-start | bytes 3211264 | tf_op jit(solution)/shard_map/all_to_all | solution.py:305
  14.1 0.6 collective-permute-start
  14.6 0.8 collective-permute-done.pos_ref
  15.5 1.1 %copy-done.1 = bf16[1024,768]{1,0:T(8,128)(2,1)} copy-done((bf16[1024,768]{1,0:T(8,128)(2,1)}, bf16[1024,768]{1,0:T(8,128)(2,1)S(1)}, u32[]{:S(2)}) %copy-start.1) | copy-done | bytes 1572888
  16.6 1.4 %copy-done.2 = bf16[1024,768]{1,0:T(8,128)(2,1)S(1)} copy-done((bf16[1024,768]{1,0:T(8,128)(2,1)S(1)}, bf16[1024,768]{1,0:T(8,128)(2,1)}, u32[]{:S(2)}) %copy-start.2) | copy-done | bytes 1572888
  18.0 1.9 %place_other.1 = bf16[16,392,128]{2,1,0:T(8,128)(2,1)S(1)} custom-call(s32[4,1024]{1,0:T(4,128)S(1)} %collective-permute-done.pos_ref, bf16[1024,768]{1,0:T(8,128)(2,1)S(1)} %copy-done.2), custom_call_target="tpu_custom_call" | custom-call | tf_op jit(solution)/shard_map/place_other/pallas_call | solution.py:291
  19.9 1.1 %copy-done = bf16[16,392,128]{2,1,0:T(8,128)(2,1)} copy-done((bf16[16,392,128]{2,1,0:T(8,128)(2,1)}, bf16[16,392,128]{2,1,0:T(8,128)(2,1)S(1)}, u32[]{:S(2)}) %copy-start) | copy-done | bytes 1605656
  21.1 14.8 %all-to-all-done.refs_2_ = bf16[16,392,128]{2,1,0:T(8,128)(2,1)S(1)} async-done(((bf16[16,392,128]{2,1,0:T(8,128)(2,1)}), bf16[16,392,128]{2,1,0:T(8,128)(2,1)S(1)}, u32[]{:S(2)}, u32[]{:S(2)}) %all-to-all-start) | async-done | bytes 1605664 | tf_op jit(solution)/shard_map/all_to_all | solution.py:305
  35.9 4.7 %all-to-all-start.1 = ((bf16[16,392,128]{2,1,0:T(8,128)(2,1)}), bf16[16,392,128]{2,1,0:T(8,128)(2,1)S(1)}, u32[]{:S(2)}, u32[]{:S(2)}) async-start(bf16[16,392,128]{2,1,0:T(8,128)(2,1)} %copy-done), calls=%async_computation.1 | async-start | bytes 3211264 | tf_op jit(solution)/shard_map/all_to_all | solution.py:305
  40.6 2.0 %collective-permute-start.2 = (bf16[16,392,128]{2,1,0:T(8,128)(2,1)S(1)}, bf16[16,392,128]{2,1,0:T(8,128)(2,1)}, u32[]{:S(2)}, u32[]{:S(2)}) collective-permute-start(bf16[16,392,128]{2,1,0:T(8,128)(2,1)S(1)} %all-to-all-done.refs_2_), channel_id=1, source_target_pairs={{0,3},{32,35},{64,67},{96,99},{8,11},{40,43},{72,75},{104,107},{16... | collective-permute-start | bytes 4816904 | tf_op jit(solution)/shard_map/ppermute | solution.py:338
  42.6 1.5 %scores_own_first.1 = (f32[8,1024]{1,0:T(8,128)S(1)}, f32[8,1024]{1,0:T(8,128)S(1)}) custom-call(s32[4,1024]{1,0:T(4,128)S(1)} %get-tuple-element.18.refs_0_.refs_1_.pos_ref, s32[4,1024]{1,0:T(4,128)S(1)} %get-tuple-element.18.refs_0_.refs_1_.pos_ref, bf16[16,392,128]{2,1,0:T(8,128)(2,1)S(1)} %all-to-all-done.refs_2_), custom_call_target="tpu_custom_call" | custom-call | tf_op jit(solution)/shard_map/scores_own_first/pallas_call | solution.py:316
  44.1 16.9 %all-to-all-done.1.refs_3_.refs_2_ = bf16[16,392,128]{2,1,0:T(8,128)(2,1)S(1)} async-done(((bf16[16,392,128]{2,1,0:T(8,128)(2,1)}), bf16[16,392,128]{2,1,0:T(8,128)(2,1)S(1)}, u32[]{:S(2)}, u32[]{:S(2)}) %all-to-all-start.1) | async-done | bytes 1605664 | tf_op jit(solution)/shard_map/all_to_all | solution.py:305
  61.1 2.2 %collective-permute-start.4 = (bf16[12,392,128]{2,1,0:T(8,128)(2,1)S(1)}, bf16[12,392,128]{2,1,0:T(8,128)(2,1)S(1)}, u32[]{:S(2)}, u32[]{:S(2)}) collective-permute-start(bf16[12,392,128]{2,1,0:T(8,128)(2,1)S(1)} %slice.12), channel_id=1, source_target_pairs={{0,3},{32,35},{64,67},{96,99},{8,11},{40,43},{72,75},{104,107},{16... | collective-permute-start | bytes 3612680 | tf_op jit(solution)/shard_map/ppermute | solution.py:347
  63.6 5.7 %collective-permute-done.2.refs_4_ = bf16[16,392,128]{2,1,0:T(8,128)(2,1)} collective-permute-done((bf16[16,392,128]{2,1,0:T(8,128)(2,1)S(1)}, bf16[16,392,128]{2,1,0:T(8,128)(2,1)}, u32[]{:S(2)}, u32[]{:S(2)}) %collective-permute-start.2) | collective-permute-done | bytes 1605664 | tf_op jit(solution)/shard_map/ppermute | solution.py:338
  69.3 3.1 %collective-permute-start.6 = (bf16[4,392,128]{2,1,0:T(8,128)(2,1)S(1)}, bf16[4,392,128]{2,1,0:T(8,128)(2,1)S(1)}, u32[]{:S(2)}, u32[]{:S(2)}) collective-permute-start(bf16[4,392,128]{2,1,0:T(8,128)(2,1)S(1)} %slice.14), channel_id=1, source_target_pairs={{0,3},{32,35},{64,67},{96,99},{8,11},{40,43},{72,75},{104,107},{16... | collective-permute-start | bytes 1204232 | tf_op jit(solution)/shard_map/ppermute | solution.py:347
  72.4 3.1 %scores_own.1 = (f32[8,1024]{1,0:T(8,128)S(1)}, f32[8,1024]{1,0:T(8,128)S(1)}) custom-call(f32[8,1024]{1,0:T(8,128)S(1)} %get-tuple-element.20.refs_0_, f32[8,1024]{1,0:T(8,128)S(1)} %get-tuple-element.21.refs_1_, bf16[16,392,128]{2,1,0:T(8,128)(2,1)S(1)} %all-to-all-done.refs_2_, bf16[16,392,128]{2,1,0:T(8,128)(2,1)S(1)} %all-to-all-done.1.refs_3_.refs_2_), custom_call_target="tpu_custom_call" | custom-call | tf_op jit(solution)/shard_map/scores_own/pallas_call | solution.py:316
  75.5 8.2 %scores_near_first.1 = (f32[8,1024]{1,0:T(8,128)S(1)}, f32[8,1024]{1,0:T(8,128)S(1)}, bf16[16,392,128]{2,1,0:T(8,128)(2,1)S(1)}) custom-call(f32[8,1024]{1,0:T(8,128)S(1)} %get-tuple-element.23.refs_0_, f32[8,1024]{1,0:T(8,128)S(1)} %get-tuple-element.24.refs_1_, bf16[16,392,128]{2,1,0:T(8,128)(2,1)S(1)} %all-to-all-done.refs_2_, ...), custom_call_target="tpu_custom_call" | custom-call | tf_op jit(solution)/shard_map/scores_near_first/pallas_call | solution.py:316
  83.7 3.7 %scores_near_0.1 = (f32[8,1024]{1,0:T(8,128)S(1)}, f32[8,1024]{1,0:T(8,128)S(1)}) custom-call(f32[8,1024]{1,0:T(8,128)S(1)} %get-tuple-element.25.refs_0_, f32[8,1024]{1,0:T(8,128)S(1)} %get-tuple-element.26.refs_1_, bf16[16,392,128]{2,1,0:T(8,128)(2,1)S(1)} %all-to-all-done.1.refs_3_.refs_2_, bf16[12,392,128]{2,1,0:T(8,128)(2,1)S(1)} %collective-permute-done.4.refs_3_, ...), custom_call_target="tpu_custom_call" | custom-call | tf_op jit(solution)/shard_map/scores_near_0/pallas_call | solution.py:316
  87.5 2.0 %collective-permute-done.7.refs_6_ = bf16[8,392,128]{2,1,0:T(8,128)(2,1)S(1)} collective-permute-done((bf16[8,392,128]{2,1,0:T(8,128)(2,1)S(1)}, bf16[8,392,128]{2,1,0:T(8,128)(2,1)S(1)}, u32[]{:S(2)}, u32[]{:S(2)}) %collective-permute-start.7) | collective-permute-done | bytes 802848 | tf_op jit(solution)/shard_map/ppermute | solution.py:349
  89.5 2.0 %scores_near_12.1 = f32[128,64]{1,0:T(8,128)S(1)} custom-call(f32[8,1024]{1,0:T(8,128)S(1)} %get-tuple-element.29.refs_0_, f32[8,1024]{1,0:T(8,128)S(1)} %get-tuple-element.30.refs_1_, bf16[16,392,128]{2,1,0:T(8,128)(2,1)S(1)} %all-to-all-done.1.refs_3_.refs_2_, bf16[12,392,128]{2,1,0:T(8,128)(2,1)S(1)} %collective-permute-done.4.refs_3_, ...), custom_call_target="tpu_custom_call" | custom-call | tf_op jit(solution)/shard_map/scores_near_12/pallas_call | solution.py:316
  91.5 15.6 %all_to_all.21 = f32[128,1,64]{2,1,0:T(1,128)S(1)} all-to-all(f32[128,1,64]{2,1,0:T(1,128)S(1)} %bitcast.6), channel_id=1, replica_groups=mesh['docs'=32,'split'=4] {'docs','split'}, dimensions={0} | all-to-all | bytes 65536 | tf_op jit(solution)/shard_map/all_to_all | solution.py:375
  107.1 0.9 finish.1
  (14 shorter events, 0.4 us)
Async XLA Ops:
  4.9 10.6 %collective-permute-start.1 = (bf16[1024,768]{1,0:T(8,128)(2,1)}, bf16[1024,768]{1,0:T(8,128)(2,1)S(1)}, u32[]{:S(2)}, u32[]{:S(2)}) collective-permute-start(bf16[1024,768]{1,0:T(8,128)(2,1)} %get-tuple-element.22), channel_id=1, source_target_pairs={{0,4},{4,0},{32,36},{36,32},{64,68},{68,64},{96,100},{100,96},{8,1... | collective-permute-start | bytes 4718600 | tf_op jit(solution)/shard_map/ppermute | solution.py:298
  6.4 29.5 %all-to-all-start = ((bf16[16,392,128]{2,1,0:T(8,128)(2,1)}), bf16[16,392,128]{2,1,0:T(8,128)(2,1)S(1)}, u32[]{:S(2)}, u32[]{:S(2)}) async-start(bf16[16,392,128]{2,1,0:T(8,128)(2,1)} %get-tuple-element.19), calls=%async_computation | async-start | bytes 3211264 | tf_op jit(solution)/shard_map/all_to_all | solution.py:305
  14.1 1.4 %collective-permute-start = (s32[4,1024]{1,0:T(4,128)S(1)}, s32[4,1024]{1,0:T(4,128)S(1)}, u32[]{:S(2)}, u32[]{:S(2)}) collective-permute-start(s32[4,1024]{1,0:T(4,128)S(1)} %get-tuple-element.18.refs_0_.refs_1_.pos_ref), channel_id=1, source_target_pairs={{0,4},{4,0},{32,36},{36,32},{64,68},{68,64},{96,100},{100,96},{8,1... | collective-permute-start | bytes 49160 | tf_op jit(solution)/shard_map/ppermute | solution.py:298
  15.5 1.1 %copy-start.1 = (bf16[1024,768]{1,0:T(8,128)(2,1)}, bf16[1024,768]{1,0:T(8,128)(2,1)S(1)}, u32[]{:S(2)}) copy-start(bf16[1024,768]{1,0:T(8,128)(2,1)S(1)} %collective-permute-done.1.unit_ref) | copy-start | bytes 4718596
  16.6 1.4 %copy-start.2 = (bf16[1024,768]{1,0:T(8,128)(2,1)S(1)}, bf16[1024,768]{1,0:T(8,128)(2,1)}, u32[]{:S(2)}) copy-start(bf16[1024,768]{1,0:T(8,128)(2,1)} %copy-done.1) | copy-start | bytes 4718596
  19.9 1.2 %copy-start = (bf16[16,392,128]{2,1,0:T(8,128)(2,1)}, bf16[16,392,128]{2,1,0:T(8,128)(2,1)S(1)}, u32[]{:S(2)}) copy-start(bf16[16,392,128]{2,1,0:T(8,128)(2,1)S(1)} %place_other.1) | copy-start | bytes 4816900
  35.9 25.1 %all-to-all-start.1 = ((bf16[16,392,128]{2,1,0:T(8,128)(2,1)}), bf16[16,392,128]{2,1,0:T(8,128)(2,1)S(1)}, u32[]{:S(2)}, u32[]{:S(2)}) async-start(bf16[16,392,128]{2,1,0:T(8,128)(2,1)} %copy-done), calls=%async_computation.1 | async-start | bytes 3211264 | tf_op jit(solution)/shard_map/all_to_all | solution.py:305
  40.6 28.7 %collective-permute-start.2 = (bf16[16,392,128]{2,1,0:T(8,128)(2,1)S(1)}, bf16[16,392,128]{2,1,0:T(8,128)(2,1)}, u32[]{:S(2)}, u32[]{:S(2)}) collective-permute-start(bf16[16,392,128]{2,1,0:T(8,128)(2,1)S(1)} %all-to-all-done.refs_2_), channel_id=1, source_target_pairs={{0,3},{32,35},{64,67},{96,99},{8,11},{40,43},{72,75},{104,107},{16... | collective-permute-start | bytes 4816904 | tf_op jit(solution)/shard_map/ppermute | solution.py:338
  42.5 33.0 %collective-permute-start.3 = (bf16[16,392,128]{2,1,0:T(8,128)(2,1)S(1)}, bf16[16,392,128]{2,1,0:T(8,128)(2,1)}, u32[]{:S(2)}, u32[]{:S(2)}) collective-permute-start(bf16[16,392,128]{2,1,0:T(8,128)(2,1)S(1)} %all-to-all-done.refs_2_), channel_id=1, source_target_pairs={{0,1},{32,33},{64,65},{96,97},{8,9},{40,41},{72,73},{104,105},{16,... | collective-permute-start | bytes 4816904 | tf_op jit(solution)/shard_map/ppermute | solution.py:339
  61.1 22.6 %collective-permute-start.4 = (bf16[12,392,128]{2,1,0:T(8,128)(2,1)S(1)}, bf16[12,392,128]{2,1,0:T(8,128)(2,1)S(1)}, u32[]{:S(2)}, u32[]{:S(2)}) collective-permute-start(bf16[12,392,128]{2,1,0:T(8,128)(2,1)S(1)} %slice.12), channel_id=1, source_target_pairs={{0,3},{32,35},{64,67},{96,99},{8,11},{40,43},{72,75},{104,107},{16... | collective-permute-start | bytes 3612680 | tf_op jit(solution)/shard_map/ppermute | solution.py:347
  63.4 20.3 %collective-permute-start.5 = (bf16[8,392,128]{2,1,0:T(8,128)(2,1)S(1)}, bf16[8,392,128]{2,1,0:T(8,128)(2,1)S(1)}, u32[]{:S(2)}, u32[]{:S(2)}) collective-permute-start(bf16[8,392,128]{2,1,0:T(8,128)(2,1)S(1)} %get-tuple-element.32), channel_id=1, source_target_pairs={{0,1},{32,33},{64,65},{96,97},{8,9},{40,41},{72,73},{104,105},{16,... | collective-permute-start | bytes 2408456 | tf_op jit(solution)/shard_map/ppermute | solution.py:349
  63.5 26.0 %collective-permute-start.7 = (bf16[8,392,128]{2,1,0:T(8,128)(2,1)S(1)}, bf16[8,392,128]{2,1,0:T(8,128)(2,1)S(1)}, u32[]{:S(2)}, u32[]{:S(2)}) collective-permute-start(bf16[8,392,128]{2,1,0:T(8,128)(2,1)S(1)} %get-tuple-element.31), channel_id=1, source_target_pairs={{0,1},{32,33},{64,65},{96,97},{8,9},{40,41},{72,73},{104,105},{16,... | collective-permute-start | bytes 2408456 | tf_op jit(solution)/shard_map/ppermute | solution.py:349
  69.3 18.2 %collective-permute-start.6 = (bf16[4,392,128]{2,1,0:T(8,128)(2,1)S(1)}, bf16[4,392,128]{2,1,0:T(8,128)(2,1)S(1)}, u32[]{:S(2)}, u32[]{:S(2)}) collective-permute-start(bf16[4,392,128]{2,1,0:T(8,128)(2,1)S(1)} %slice.14), channel_id=1, source_target_pairs={{0,3},{32,35},{64,67},{96,99},{8,11},{40,43},{72,75},{104,107},{16... | collective-permute-start | bytes 1204232 | tf_op jit(solution)/shard_map/ppermute | solution.py:347
